TPU v7x, 128 devices: a whole 4x4x4 slice. The times are simulated.
128 devices in a mesh: row: 4 (over y), col: 32 (over x, z, core).
Axes of the slice: x: 4, y: 4, z: 4, core: 2. Of those that a mesh axis runs over, the one named last changes fastest.
Arguments:
- basis: bfloat16 [65536, 1024], P(('row', 'col')), may hold values from -6 to 6
- dmat: bfloat16 [8192, 128, 128], P(('row', 'col')), may hold values from -0.0078125 to 0.0078125
- tile_home: int32 [8192], replicated, may hold values from 0 to 8191, as said below
- pair_tiles: int32 [512, 32], P(('row', 'col')), may hold values from 0 to 8191, as said below
- pair_pos: int32 [512, 32], P(('row', 'col')), may hold values from 0 to 63, as said below
- coords: float32 [3, 65536], P(None, ('row', 'col')), may hold values from -5 to 5
- weights: float32 [65536], P(('row', 'col')), may hold values from 0.6 to 6
- grad_sq: float32 [65536], P(('row', 'col')), may hold values from 0.5 to 6
- pair_keep: int32 [512, 512], replicated, may hold values from 0 to 1, as said below
Outputs:
- field_matrix_pieces: float32 [8192, 128, 128], P(('row', 'col'))
- correlation_field: float32 [65536], P(('row', 'col'))
Inputs may be any that keep to these rules, and one draw needn't show every extreme that they name: A permutation: tile t is row tile_home[t] of dmat, and rows g * 64 to (g+1) * 64 - 1 lie on device g of row+col. `pair_tiles`: the blocks of one device name at most 2 tiles (repeats counted) stored on any one device, and one storing device is named exactly 2 times by the blocks of every device. `pair_pos`: pair position q stands for orbital tiles q // 8 and q % 8 of the block; the positions of one block are distinct. pair_keep[b,b] = 1 for every block b.
All inputs are finite; a program needn't handle non-finite values.
Results may differ from a plain program's by a relative error of at most 0.004.
Values may be sent and summed in bfloat16 or wider, within the bound.
A program may use at most 128 MiB of HBM per device.

v0:
```python
import jax
import jax.numpy as jnp
from jax import lax
from jax.sharding import PartitionSpec as P

gradient_coef = 0.0093
kappa_coef = 6.3
density_floor = 0.1


def point_features(raw_density, grad_sq):
    density = jax.nn.softplus(raw_density) + density_floor
    ratio = grad_sq / (density * density)
    omega_zero = jnp.sqrt(gradient_coef * ratio * ratio + 4.0 * jnp.pi / 3.0 * density)
    kappa_point = kappa_coef * 1.5 * jnp.pi * (density / (9.0 * jnp.pi)) ** (1.0 / 6.0)
    return (density, omega_zero, kappa_point)


def pair_block(target_feat, source_feat, keep_rows, block_rows):
    distance = jnp.zeros((target_feat.shape[1], source_feat.shape[1]), jnp.float32)
    for axis_pos in range(3):
        offset = target_feat[2 + axis_pos][:, None] - source_feat[3 + axis_pos][None, :]
        distance = distance + offset * offset
    target_term = target_feat[0][:, None] * distance + target_feat[1][:, None]
    source_term = source_feat[1][None, :] * distance + source_feat[2][None, :]
    kernel = -1.5 / (target_term * source_term * (target_term + source_term))
    target_blocks = target_feat.shape[1] // block_rows
    source_blocks = source_feat.shape[1] // block_rows
    shaped = kernel.reshape(target_blocks, block_rows, source_blocks, block_rows)
    weight = keep_rows[:, None, :, None] * source_feat[0].reshape(1, 1, source_blocks, block_rows)
    return jnp.sum(shaped * weight, axis=(2, 3)).reshape(-1)


def target_sweep(targets, sources, keep_rows, block_rows):
    width_rows = targets.shape[1]
    group_size = width_rows
    while group_size > 1024 and group_size // block_rows % 2 == 0:
        group_size = group_size // 2
    turns_count = width_rows // group_size

    def one_group(turn_index):
        part_feat = lax.dynamic_slice_in_dim(targets, turn_index * group_size, group_size, 1)
        part_keep = lax.dynamic_slice_in_dim(
            keep_rows, turn_index * (group_size // block_rows), group_size // block_rows, 0
        )
        return pair_block(part_feat, sources, part_keep, block_rows)

    return lax.map(one_group, jnp.arange(turns_count, dtype=jnp.int32)).reshape(-1)


def gather_tiles(atomic_basis_evaluations, positions):
    return jax.vmap(lambda values, chosen: values[:, chosen, :])(
        atomic_basis_evaluations, positions
    )


def body(basis, dmat, tile_home, pair_tiles, pair_pos, coords, weights, grad_sq, pair_keep):
    peer_count = lax.axis_size(("row", "col"))
    row_count = lax.axis_size("row")
    col_count = lax.axis_size("col")
    block_count = pair_tiles.shape[0]
    pair_count = pair_tiles.shape[1]
    store_count = dmat.shape[0]
    tile_width = dmat.shape[1]
    local_points = basis.shape[0]
    block_rows = local_points // block_count
    tile_count = basis.shape[1] // tile_width
    request_count = block_count * pair_count
    capacity = max(2, (2 * request_count + peer_count - 1) // peer_count)
    retained_submatrices = tile_home[pair_tiles.reshape(-1)]
    owner_of = retained_submatrices // store_count
    within = retained_submatrices % store_count
    owner_hot = (owner_of[:, None] == jnp.arange(peer_count, dtype=jnp.int32)[None, :]).astype(
        jnp.int32
    )
    earlier = jnp.sum((jnp.cumsum(owner_hot, axis=0) - owner_hot) * owner_hot, axis=1)
    slot_index = owner_of * capacity + earlier
    asking = jnp.full((peer_count * capacity,), -1, jnp.int32).at[slot_index].set(within)
    asked_for = lax.all_to_all(
        asking.reshape(peer_count, capacity),
        ("row", "col"),
        split_axis=0,
        concat_axis=0,
        tiled=True,
    ).reshape(-1)
    present = asked_for >= 0
    picked = jnp.take(dmat, jnp.maximum(asked_for, 0), axis=0)
    outgoing = jnp.where(present[:, None, None], picked, jnp.zeros_like(picked))
    outgoing = outgoing.reshape(peer_count, capacity, tile_width, tile_width)
    arrived = lax.all_to_all(outgoing, ("row", "col"), split_axis=0, concat_axis=0, tiled=True)
    fetched = arrived.reshape(peer_count * capacity, tile_width, tile_width)[slot_index]
    fetched = fetched.reshape(block_count, pair_count, tile_width, tile_width)
    atomic_basis_evaluations = basis.reshape(block_count, block_rows, tile_count, tile_width)
    first_slot_number = pair_pos // tile_count
    second_slot_number = pair_pos % tile_count
    left_orb = gather_tiles(atomic_basis_evaluations, first_slot_number)
    right_orb = gather_tiles(atomic_basis_evaluations, second_slot_number)
    mixed_rows = jnp.einsum(
        "bpna,bnac->bpnc", left_orb, fetched, preferred_element_type=jnp.float32
    )
    raw_density = jnp.sum(mixed_rows * right_orb.astype(jnp.float32), axis=(2, 3)).reshape(-1)
    density, omega_zero, kappa_point = point_features(raw_density, grad_sq)
    strength = weights * density
    source_feat = jnp.concatenate([jnp.stack([strength, omega_zero, kappa_point]), coords], axis=0)
    target_feat = jnp.concatenate([jnp.stack([omega_zero, kappa_point]), coords], axis=0)
    keep_mask = pair_keep.astype(jnp.float32)
    row_index = lax.axis_index("row")
    col_index = lax.axis_index("col")
    sources = lax.all_gather(source_feat, "row", axis=1, tiled=True)
    targets = lax.all_gather(target_feat, "col", axis=1, tiled=True)
    source_list = (
        (jnp.arange(row_count, dtype=jnp.int32)[:, None] * col_count + col_index) * block_count
        + jnp.arange(block_count, dtype=jnp.int32)[None, :]
    ).reshape(-1)
    keep_rows = lax.dynamic_slice_in_dim(
        keep_mask, row_index * col_count * block_count, col_count * block_count, 0
    )
    keep_grid = jnp.take(keep_rows, source_list, axis=1)
    correlation_field = lax.psum_scatter(
        target_sweep(targets, sources, keep_grid, block_rows),
        "col",
        scatter_dimension=0,
        tiled=True,
    )
    scaled = (basis.astype(jnp.float32) * (weights * correlation_field)[:, None]).astype(
        jnp.bfloat16
    )
    scaled_left = gather_tiles(
        scaled.reshape(block_count, block_rows, tile_count, tile_width), first_slot_number
    )
    new_tiles = jnp.einsum(
        "bpna,bpnc->bnac", scaled_left, right_orb, preferred_element_type=jnp.float32
    ).astype(jnp.bfloat16)
    returning = (
        jnp.zeros((peer_count * capacity, tile_width, tile_width), jnp.bfloat16)
        .at[slot_index]
        .set(new_tiles.reshape(-1, tile_width, tile_width))
    )
    returning = returning.reshape(peer_count, capacity, tile_width, tile_width)
    landed = lax.all_to_all(returning, ("row", "col"), split_axis=0, concat_axis=0, tiled=True)
    received_submatrices = landed.reshape(peer_count * capacity, tile_width * tile_width)
    submatrix_picker = (
        asked_for[None, :] == jnp.arange(store_count, dtype=jnp.int32)[:, None]
    ).astype(jnp.bfloat16)
    field_matrix_pieces = jnp.dot(
        submatrix_picker, received_submatrices, preferred_element_type=jnp.float32
    ).reshape(store_count, tile_width, tile_width)
    return (field_matrix_pieces, correlation_field)


def solution(mesh):
    in_specs = (
        P(("row", "col"), None),
        P(("row", "col"), None, None),
        P(),
        P(("row", "col"), None),
        P(("row", "col"), None),
        P(None, ("row", "col")),
        P(("row", "col")),
        P(("row", "col")),
        P(),
    )
    out_specs = (P(("row", "col"), None, None), P(("row", "col")))
    return jax.shard_map(body, mesh=mesh, in_specs=in_specs, out_specs=out_specs, check_vma=False)
```

profile of v0, /device:TPU:1, one launch (start us, length us, event | category | flops | bytes accessed | tf_op | source)
XLA Modules:
  0.0 864.0 jit_solution(14366918582789362261)
XLA Ops:
  11.4 20.7 %all_to_all.19 = s32[128,1,2]{2,1,0:T(1,128)S(1)} all-to-all(s32[128,1,2]{2,1,0:T(1,128)S(1)} %bitcast.167), channel_id=1, replica_groups=mesh['row'=4,'col'=32] {'row','col'}, dimensions={0} | all-to-all | bytes 2048 | tf_op jit(solution)/shard_map/all_to_all | solution.py:79
  70.1 85.3 %all-to-all-done.1 = bf16[128,2,128,128]{3,2,1,0:T(8,128)(2,1)} async-done(((bf16[128,2,128,128]{3,2,1,0:T(8,128)(2,1)}), bf16[128,2,128,128]{3,2,1,0:T(8,128)(2,1)}, u32[]{:S(2)}, u32[]{:S(2)}) %all-to-all-start.1) | async-done | bytes 8388640 | tf_op jit(solution)/shard_map/all_to_all | solution.py:90
  178.7 28.7 %all_gather.6 = f32[5,16384]{1,0:T(8,128)S(1)} all-gather(f32[5,512]{1,0:T(8,128)S(1)} %pad_maximum_fusion), channel_id=1, replica_groups=mesh['row'=4,'col'=32] {'col'}, dimensions={1}, use_global_device_ids=true | all-gather | bytes 337920 | tf_op jit(solution)/shard_map/all_gather | solution.py:110
  207.4 356.7 %while.10 = (s32[]{:T(128)}, f32[16,1024]{1,0:T(8,128)S(1)}, s32[16]{0:T(128)S(1)}, f32[5,16384]{1,0:T(8,128)S(1)}, f32[6,2048]{1,0:T(8,128)S(1)}, /*index=5*/f3...) while((s32[]{:T(128)}, f32[16,1024]{1,0:T(8,128)S(1)}, ...), condition=%wide.region_6.7_spmd, body=%wide.region_4.6_spmd.sunk | while | flops 37764108 | bytes 354121 | solution.py:48
  209.5 20.0 %multiply_reduce_fusion.2 = f32[8,128]{1,0:T(8,128)S(1)} fusion(f32[8,16,128]{2,1,0:T(8,128)S(1)} %broadcast_multiply_fusion.2, f32[16,128]{1,0:T(8,128)S(1)} %bitcast.169, f32[16,128]{1,0:T(8,128)S(1)} %bitcast.170, f32[8,128]{1,0:T(8,128)S(1)} %bitcast.178, f32[16,128]{1,0:T(8,128)S(1)} %bitcast.171, f32[8,128]{1,0:T(8,128)S(1)} %bitcast.175, ...), kind=kLoop, calls=%fused_computation.9.clone.1 | loop fusion | flops 37747712 | bytes 131072 | tf_op jit(solution)/shard_map/while/body/eval_jaxpr/reduce_sum | solution.py:31
  231.8 20.0 %multiply_reduce_fusion.2 = f32[8,128]{1,0:T(8,128)S(1)} fusion(f32[8,16,128]{2,1,0:T(8,128)S(1)} %broadcast_multiply_fusion.2, f32[16,128]{1,0:T(8,128)S(1)} %bitcast.169, f32[16,128]{1,0:T(8,128)S(1)} %bitcast.170, f32[8,128]{1,0:T(8,128)S(1)} %bitcast.178, f32[16,128]{1,0:T(8,128)S(1)} %bitcast.171, f32[8,128]{1,0:T(8,128)S(1)} %bitcast.175, ...), kind=kLoop, calls=%fused_computation.9.clone.1 | loop fusion | flops 37747712 | bytes 131072 | tf_op jit(solution)/shard_map/while/body/eval_jaxpr/reduce_sum | solution.py:31
  254.1 20.0 %multiply_reduce_fusion.2 = f32[8,128]{1,0:T(8,128)S(1)} fusion(f32[8,16,128]{2,1,0:T(8,128)S(1)} %broadcast_multiply_fusion.2, f32[16,128]{1,0:T(8,128)S(1)} %bitcast.169, f32[16,128]{1,0:T(8,128)S(1)} %bitcast.170, f32[8,128]{1,0:T(8,128)S(1)} %bitcast.178, f32[16,128]{1,0:T(8,128)S(1)} %bitcast.171, f32[8,128]{1,0:T(8,128)S(1)} %bitcast.175, ...), kind=kLoop, calls=%fused_computation.9.clone.1 | loop fusion | flops 37747712 | bytes 131072 | tf_op jit(solution)/shard_map/while/body/eval_jaxpr/reduce_sum | solution.py:31
  276.4 20.0 %multiply_reduce_fusion.2 = f32[8,128]{1,0:T(8,128)S(1)} fusion(f32[8,16,128]{2,1,0:T(8,128)S(1)} %broadcast_multiply_fusion.2, f32[16,128]{1,0:T(8,128)S(1)} %bitcast.169, f32[16,128]{1,0:T(8,128)S(1)} %bitcast.170, f32[8,128]{1,0:T(8,128)S(1)} %bitcast.178, f32[16,128]{1,0:T(8,128)S(1)} %bitcast.171, f32[8,128]{1,0:T(8,128)S(1)} %bitcast.175, ...), kind=kLoop, calls=%fused_computation.9.clone.1 | loop fusion | flops 37747712 | bytes 131072 | tf_op jit(solution)/shard_map/while/body/eval_jaxpr/reduce_sum | solution.py:31
  298.7 20.0 %multiply_reduce_fusion.2 = f32[8,128]{1,0:T(8,128)S(1)} fusion(f32[8,16,128]{2,1,0:T(8,128)S(1)} %broadcast_multiply_fusion.2, f32[16,128]{1,0:T(8,128)S(1)} %bitcast.169, f32[16,128]{1,0:T(8,128)S(1)} %bitcast.170, f32[8,128]{1,0:T(8,128)S(1)} %bitcast.178, f32[16,128]{1,0:T(8,128)S(1)} %bitcast.171, f32[8,128]{1,0:T(8,128)S(1)} %bitcast.175, ...), kind=kLoop, calls=%fused_computation.9.clone.1 | loop fusion | flops 37747712 | bytes 131072 | tf_op jit(solution)/shard_map/while/body/eval_jaxpr/reduce_sum | solution.py:31
  321.0 20.0 %multiply_reduce_fusion.2 = f32[8,128]{1,0:T(8,128)S(1)} fusion(f32[8,16,128]{2,1,0:T(8,128)S(1)} %broadcast_multiply_fusion.2, f32[16,128]{1,0:T(8,128)S(1)} %bitcast.169, f32[16,128]{1,0:T(8,128)S(1)} %bitcast.170, f32[8,128]{1,0:T(8,128)S(1)} %bitcast.178, f32[16,128]{1,0:T(8,128)S(1)} %bitcast.171, f32[8,128]{1,0:T(8,128)S(1)} %bitcast.175, ...), kind=kLoop, calls=%fused_computation.9.clone.1 | loop fusion | flops 37747712 | bytes 131072 | tf_op jit(solution)/shard_map/while/body/eval_jaxpr/reduce_sum | solution.py:31
  343.3 20.0 %multiply_reduce_fusion.2 = f32[8,128]{1,0:T(8,128)S(1)} fusion(f32[8,16,128]{2,1,0:T(8,128)S(1)} %broadcast_multiply_fusion.2, f32[16,128]{1,0:T(8,128)S(1)} %bitcast.169, f32[16,128]{1,0:T(8,128)S(1)} %bitcast.170, f32[8,128]{1,0:T(8,128)S(1)} %bitcast.178, f32[16,128]{1,0:T(8,128)S(1)} %bitcast.171, f32[8,128]{1,0:T(8,128)S(1)} %bitcast.175, ...), kind=kLoop, calls=%fused_computation.9.clone.1 | loop fusion | flops 37747712 | bytes 131072 | tf_op jit(solution)/shard_map/while/body/eval_jaxpr/reduce_sum | solution.py:31
  365.6 20.0 %multiply_reduce_fusion.2 = f32[8,128]{1,0:T(8,128)S(1)} fusion(f32[8,16,128]{2,1,0:T(8,128)S(1)} %broadcast_multiply_fusion.2, f32[16,128]{1,0:T(8,128)S(1)} %bitcast.169, f32[16,128]{1,0:T(8,128)S(1)} %bitcast.170, f32[8,128]{1,0:T(8,128)S(1)} %bitcast.178, f32[16,128]{1,0:T(8,128)S(1)} %bitcast.171, f32[8,128]{1,0:T(8,128)S(1)} %bitcast.175, ...), kind=kLoop, calls=%fused_computation.9.clone.1 | loop fusion | flops 37747712 | bytes 131072 | tf_op jit(solution)/shard_map/while/body/eval_jaxpr/reduce_sum | solution.py:31
  387.9 20.0 %multiply_reduce_fusion.2 = f32[8,128]{1,0:T(8,128)S(1)} fusion(f32[8,16,128]{2,1,0:T(8,128)S(1)} %broadcast_multiply_fusion.2, f32[16,128]{1,0:T(8,128)S(1)} %bitcast.169, f32[16,128]{1,0:T(8,128)S(1)} %bitcast.170, f32[8,128]{1,0:T(8,128)S(1)} %bitcast.178, f32[16,128]{1,0:T(8,128)S(1)} %bitcast.171, f32[8,128]{1,0:T(8,128)S(1)} %bitcast.175, ...), kind=kLoop, calls=%fused_computation.9.clone.1 | loop fusion | flops 37747712 | bytes 131072 | tf_op jit(solution)/shard_map/while/body/eval_jaxpr/reduce_sum | solution.py:31
  410.2 20.0 %multiply_reduce_fusion.2 = f32[8,128]{1,0:T(8,128)S(1)} fusion(f32[8,16,128]{2,1,0:T(8,128)S(1)} %broadcast_multiply_fusion.2, f32[16,128]{1,0:T(8,128)S(1)} %bitcast.169, f32[16,128]{1,0:T(8,128)S(1)} %bitcast.170, f32[8,128]{1,0:T(8,128)S(1)} %bitcast.178, f32[16,128]{1,0:T(8,128)S(1)} %bitcast.171, f32[8,128]{1,0:T(8,128)S(1)} %bitcast.175, ...), kind=kLoop, calls=%fused_computation.9.clone.1 | loop fusion | flops 37747712 | bytes 131072 | tf_op jit(solution)/shard_map/while/body/eval_jaxpr/reduce_sum | solution.py:31
  432.5 20.0 %multiply_reduce_fusion.2 = f32[8,128]{1,0:T(8,128)S(1)} fusion(f32[8,16,128]{2,1,0:T(8,128)S(1)} %broadcast_multiply_fusion.2, f32[16,128]{1,0:T(8,128)S(1)} %bitcast.169, f32[16,128]{1,0:T(8,128)S(1)} %bitcast.170, f32[8,128]{1,0:T(8,128)S(1)} %bitcast.178, f32[16,128]{1,0:T(8,128)S(1)} %bitcast.171, f32[8,128]{1,0:T(8,128)S(1)} %bitcast.175, ...), kind=kLoop, calls=%fused_computation.9.clone.1 | loop fusion | flops 37747712 | bytes 131072 | tf_op jit(solution)/shard_map/while/body/eval_jaxpr/reduce_sum | solution.py:31
  454.8 20.0 %multiply_reduce_fusion.2 = f32[8,128]{1,0:T(8,128)S(1)} fusion(f32[8,16,128]{2,1,0:T(8,128)S(1)} %broadcast_multiply_fusion.2, f32[16,128]{1,0:T(8,128)S(1)} %bitcast.169, f32[16,128]{1,0:T(8,128)S(1)} %bitcast.170, f32[8,128]{1,0:T(8,128)S(1)} %bitcast.178, f32[16,128]{1,0:T(8,128)S(1)} %bitcast.171, f32[8,128]{1,0:T(8,128)S(1)} %bitcast.175, ...), kind=kLoop, calls=%fused_computation.9.clone.1 | loop fusion | flops 37747712 | bytes 131072 | tf_op jit(solution)/shard_map/while/body/eval_jaxpr/reduce_sum | solution.py:31
  477.1 20.0 %multiply_reduce_fusion.2 = f32[8,128]{1,0:T(8,128)S(1)} fusion(f32[8,16,128]{2,1,0:T(8,128)S(1)} %broadcast_multiply_fusion.2, f32[16,128]{1,0:T(8,128)S(1)} %bitcast.169, f32[16,128]{1,0:T(8,128)S(1)} %bitcast.170, f32[8,128]{1,0:T(8,128)S(1)} %bitcast.178, f32[16,128]{1,0:T(8,128)S(1)} %bitcast.171, f32[8,128]{1,0:T(8,128)S(1)} %bitcast.175, ...), kind=kLoop, calls=%fused_computation.9.clone.1 | loop fusion | flops 37747712 | bytes 131072 | tf_op jit(solution)/shard_map/while/body/eval_jaxpr/reduce_sum | solution.py:31
  499.4 20.0 %multiply_reduce_fusion.2 = f32[8,128]{1,0:T(8,128)S(1)} fusion(f32[8,16,128]{2,1,0:T(8,128)S(1)} %broadcast_multiply_fusion.2, f32[16,128]{1,0:T(8,128)S(1)} %bitcast.169, f32[16,128]{1,0:T(8,128)S(1)} %bitcast.170, f32[8,128]{1,0:T(8,128)S(1)} %bitcast.178, f32[16,128]{1,0:T(8,128)S(1)} %bitcast.171, f32[8,128]{1,0:T(8,128)S(1)} %bitcast.175, ...), kind=kLoop, calls=%fused_computation.9.clone.1 | loop fusion | flops 37747712 | bytes 131072 | tf_op jit(solution)/shard_map/while/body/eval_jaxpr/reduce_sum | solution.py:31
  521.7 20.0 %multiply_reduce_fusion.2 = f32[8,128]{1,0:T(8,128)S(1)} fusion(f32[8,16,128]{2,1,0:T(8,128)S(1)} %broadcast_multiply_fusion.2, f32[16,128]{1,0:T(8,128)S(1)} %bitcast.169, f32[16,128]{1,0:T(8,128)S(1)} %bitcast.170, f32[8,128]{1,0:T(8,128)S(1)} %bitcast.178, f32[16,128]{1,0:T(8,128)S(1)} %bitcast.171, f32[8,128]{1,0:T(8,128)S(1)} %bitcast.175, ...), kind=kLoop, calls=%fused_computation.9.clone.1 | loop fusion | flops 37747712 | bytes 131072 | tf_op jit(solution)/shard_map/while/body/eval_jaxpr/reduce_sum | solution.py:31
  543.9 20.0 %multiply_reduce_fusion.2 = f32[8,128]{1,0:T(8,128)S(1)} fusion(f32[8,16,128]{2,1,0:T(8,128)S(1)} %broadcast_multiply_fusion.2, f32[16,128]{1,0:T(8,128)S(1)} %bitcast.169, f32[16,128]{1,0:T(8,128)S(1)} %bitcast.170, f32[8,128]{1,0:T(8,128)S(1)} %bitcast.178, f32[16,128]{1,0:T(8,128)S(1)} %bitcast.171, f32[8,128]{1,0:T(8,128)S(1)} %bitcast.175, ...), kind=kLoop, calls=%fused_computation.9.clone.1 | loop fusion | flops 37747712 | bytes 131072 | tf_op jit(solution)/shard_map/while/body/eval_jaxpr/reduce_sum | solution.py:31
  566.0 94.2 %all-reduce.3.cloned.1.call-done = f32[16384]{0:T(1024)} async-done(((f32[16384]{0:T(1024)}), f32[16384]{0:T(1024)}) %all-reduce.3.cloned.1.call-update) | async-done | bytes 65552
  683.7 19.3 %scatter_fusion = bf16[256,128,128]{2,1,0:T(8,128)(2,1)} fusion(bf16[256,128,128]{2,1,0:T(8,128)(2,1)} %broadcast.325, s32[128]{0:T(128)S(1)} %fusion.28, bf16[128,128,128]{2,1,0:T(8,128)(2,1)} %bitcast.160), kind=kCustom, calls=%fused_computation.8 | custom fusion | bytes 12583424 | tf_op jit(solution)/shard_map/scatter | solution.py:137
  712.0 99.0 %all-to-all-done.2 = bf16[128,2,128,128]{3,2,1,0:T(8,128)(2,1)} async-done(((bf16[128,2,128,128]{3,2,1,0:T(8,128)(2,1)}), bf16[128,2,128,128]{3,2,1,0:T(8,128)(2,1)}, u32[]{:S(2)}, u32[]{:S(2)}) %all-to-all-start.2) | async-done | bytes 8388640 | tf_op jit(solution)/shard_map/all_to_all | solution.py:140
  811.0 23.2 %copy.107 = bf16[32,8,128,128]{3,1,2,0:T(8,128)(2,1)} copy(bf16[32,8,128,128]{3,2,1,0:T(8,128)(2,1)} %bitcast.60) | data formatting | bytes 16777216
  (184 shorter events, 136.8 us)
Async XLA Ops:
  7.2 25.6 %copy-start = (bf16[64,128,128]{2,1,0:T(8,128)(2,1)S(1)}, bf16[64,128,128]{2,1,0:T(8,128)(2,1)}, u32[]{:S(2)}) copy-start(bf16[64,128,128]{2,1,0:T(8,128)(2,1)} %param.12) | copy-start | bytes 6291460
  48.6 6.2 copy-start.2
  48.6 6.8 copy-start.5
  48.6 106.8 %all-to-all-start.1 = ((bf16[128,2,128,128]{3,2,1,0:T(8,128)(2,1)}), bf16[128,2,128,128]{3,2,1,0:T(8,128)(2,1)}, u32[]{:S(2)}, u32[]{:S(2)}) async-start(bf16[128,2,128,128]{3,2,1,0:T(8,128)(2,1)} %select_select_fusion), calls=%async_computation.1 | async-start | bytes 16777216 | tf_op jit(solution)/shard_map/all_to_all | solution.py:90
  54.6 605.6 %all-reduce.3.cloned.1.call-start = ((), (), s32[]{:S(2)}) async-start(), calls=%async_computation.3 | async-start | bytes 131072
  161.8 7.8 copy-start.4
  161.8 7.8 copy-start.6
  161.8 7.8 copy-start.3
  161.8 402.9 %copy-start.7 = (u32[128]{0:T(128)S(1)}, u32[128]{0:T(128)}, u32[]{:S(2)}) copy-start(u32[128]{0:T(128)} %constant.203) | copy-start | bytes 1540
  703.0 108.0 %all-to-all-start.2 = ((bf16[128,2,128,128]{3,2,1,0:T(8,128)(2,1)}), bf16[128,2,128,128]{3,2,1,0:T(8,128)(2,1)}, u32[]{:S(2)}, u32[]{:S(2)}) async-start(bf16[128,2,128,128]{3,2,1,0:T(8,128)(2,1)} %bitcast.152), calls=%async_computation.2 | async-start | bytes 16777216 | tf_op jit(solution)/shard_map/all_to_all | solution.py:140
  846.1 10.6 %copy-start.1 = (bf16[64,128,128]{2,1,0:T(8,128)(2,1)S(1)}, bf16[64,128,128]{2,1,0:T(8,128)(2,1)}, u32[]{:S(2)}) copy-start(bf16[64,128,128]{2,1,0:T(8,128)(2,1)} %param.12) | copy-start | bytes 6291460
Sparse Core Ops, SparseCore 0:
  564.8 95.2 all-reduce.2
where the time goes:
time: 875 us; the launch traced here: 864 us
  other arithmetic  332 us (38%)
  waiting for transfers between devices  278 us (32%)
  local copies, waits for them, and re-layouts  125 us (14%)
  blocking collectives  58.4 us (7%)
  loops' own time  21.5 us (2%)
  matrix products  20.5 us (2%)
  between operations  15.4 us (2%)
  starting transfers between devices  13.5 us (2%)
    reduce_sum x16, other arithmetic, pair_block(): return jnp.sum(shaped * weight, axis=(2, 3)).reshape(-1)  320 us
    all_to_all x1, waiting for transfers between devices, body(): lax.all_to_all(returning, ('row', 'col'), split_axis=0, concat_axis=0, ti...  99 us
    unnamed x2, waiting for transfers between devices  94.2 us
    all_to_all x1, waiting for transfers between devices, body(): lax.all_to_all(outgoing, ('row', 'col'), split_axis=0, concat_axis=0, til...  85.3 us
    unnamed x23, local copies, waits for them, and re-layouts  29.6 us
    all_gather x1, blocking collectives, body(): targets = lax.all_gather(target_feat, 'col', axis=1, tiled=True)  28.7 us
    gather x7, local copies, waits for them, and re-layouts, gather_tiles(): values[:, chosen, :]  22.2 us
    another operation x1, loops' own time, target_sweep(): lax.map(one_group, jnp.arange(turns_count, dtype=jnp.int32)).reshape(-1)  21.5 us
  transfers between devices with their start and end apart: 3, of which 3 were waited for; matrix products, arithmetic and copies ran while one was open for 2% of the time, Pallas kernels for 0%

commit v1 on v0

v1 whole, which is shorter than its diff:
```python
import functools

import jax
import jax.numpy as jnp
from jax import lax
from jax.experimental import pallas as pl
from jax.experimental.pallas import tpu as pltpu
from jax.sharding import PartitionSpec as P

gradient_coef = 0.0093
kappa_coef = 6.3
density_floor = 0.1
AXES = ("row", "col")
VMEM_LIMIT = 56 * 2**20


def point_features(raw_density, grad_sq):
    density = jnp.maximum(raw_density, 0.0) + jnp.log1p(jnp.exp(-jnp.abs(raw_density))) + density_floor
    ratio = grad_sq / (density * density)
    omega_zero = jnp.sqrt(gradient_coef * ratio * ratio + 4.0 * jnp.pi / 3.0 * density)
    kappa_point = kappa_coef * 1.5 * jnp.pi * jnp.exp(jnp.log(density / (9.0 * jnp.pi)) * (1.0 / 6.0))
    return density, omega_zero, kappa_point


def params(**more):
    return pltpu.CompilerParams(vmem_limit_bytes=VMEM_LIMIT, **more)


def pick_kernel(asked, tiles, out):
    step = pl.program_id(0)
    width = out.shape[0]

    @pl.loop(0, width)
    def _(slot):
        wanted = asked[step * width + slot]

        @pl.when(wanted >= 0)
        def _():
            out[slot] = tiles[wanted]


def pick_tiles(asked, tiles):
    count = asked.shape[0]
    group = 32
    return pl.pallas_call(
        pick_kernel,
        grid=(count // group,),
        in_specs=[
            pl.BlockSpec(memory_space=pltpu.SMEM),
            pl.BlockSpec(memory_space=pltpu.VMEM),
        ],
        out_specs=pl.BlockSpec((group,) + tiles.shape[1:], lambda i: (i, 0, 0)),
        out_shape=jax.ShapeDtypeStruct((count,) + tiles.shape[1:], tiles.dtype),
        compiler_params=params(),
        name="pick_tiles",
    )(asked, tiles)


def density_kernel(slots, positions, basis, arrived, raw, dense, sems):
    blocks, pairs = positions.shape
    rows = basis.shape[0] // blocks
    orbs = basis.shape[1]
    tile = arrived.shape[1]
    kt = orbs // tile

    dense[...] = jnp.zeros_like(dense)

    def fetch(b, k):
        q = positions[b, k]
        left = pl.multiple_of((q // kt) * tile, tile)
        right = pl.multiple_of((q % kt) * tile, tile)
        return pltpu.make_async_copy(
            arrived.at[slots[b * pairs + k]],
            dense.at[b, pl.ds(left, tile), pl.ds(right, tile)],
            sems.at[b * pairs + k],
        )

    for b in range(blocks):

        @pl.loop(0, pairs)
        def _(k):
            fetch(b, k).start()

    for b in range(blocks):

        @pl.loop(0, pairs)
        def _(k):
            fetch(b, k).wait()

        chi = basis[b * rows : (b + 1) * rows, :]
        mixed = jnp.dot(chi, dense[b], preferred_element_type=jnp.float32)
        both = mixed * chi.astype(jnp.float32)
        part = both[:, :tile]
        for m in range(1, kt):
            part = part + both[:, m * tile : (m + 1) * tile]
        raw[b : b + 1, :] = jnp.sum(part.T, axis=0, keepdims=True)


def block_density(slots, positions, basis, arrived):
    blocks = positions.shape[0]
    rows = basis.shape[0] // blocks
    orbs = basis.shape[1]
    return pl.pallas_call(
        density_kernel,
        in_specs=[
            pl.BlockSpec(memory_space=pltpu.SMEM),
            pl.BlockSpec(memory_space=pltpu.SMEM),
            pl.BlockSpec(memory_space=pltpu.VMEM),
            pl.BlockSpec(memory_space=pl.ANY),
        ],
        out_specs=pl.BlockSpec(memory_space=pltpu.VMEM),
        out_shape=jax.ShapeDtypeStruct((blocks, rows), jnp.float32),
        scratch_shapes=[
            pltpu.VMEM((blocks, orbs, orbs), basis.dtype),
            pltpu.SemaphoreType.DMA((positions.size,)),
        ],
        compiler_params=params(),
        name="block_density",
    )(slots, positions, basis, arrived)


def field_kernel(
    kept, counts, slots, positions, first, raw, source, basis, field, tiles_out, feats, column, scaled, staged, sems
):
    blocks, pairs = positions.shape
    rows = raw.shape[1]
    tile = tiles_out.shape[1]
    kt = basis.shape[1] // tile
    weights = source[:, 0]
    density, omega, kappa = point_features(raw[...], source[:, 1])
    feats[0] = weights * density
    feats[1] = omega
    feats[2] = kappa
    for axis in range(3):
        feats[3 + axis] = source[:, 2 + axis]

    def send(b, k):
        return pltpu.make_async_copy(
            staged.at[b * pairs + k], tiles_out.at[slots[b * pairs + k]], sems.at[b * pairs + k]
        )

    for b in range(blocks):
        at = first[0] + b
        for f in range(5):
            row = feats[1 + f, pl.ds(at, 1), :]
            column[f] = jnp.broadcast_to(row, (rows, rows)).T

        def one_source(j, total):
            s = kept[b, j]
            r2 = None
            for axis in range(3):
                gap = column[2 + axis] - feats[3 + axis, pl.ds(s, 1), :]
                r2 = gap * gap if r2 is None else r2 + gap * gap
            g = column[0] * r2 + column[1]
            h = feats[1, pl.ds(s, 1), :] * r2 + feats[2, pl.ds(s, 1), :]
            phi = -1.5 / (g * h * (g + h))
            return total + phi * feats[0, pl.ds(s, 1), :]

        total = lax.fori_loop(0, counts[b], one_source, jnp.zeros((rows, rows), jnp.float32))
        potential = jnp.sum(total, axis=1, keepdims=True)
        wide = jnp.broadcast_to(potential, (rows, rows))
        field[b : b + 1, :] = wide.T[0:1, :]
        weight = jnp.broadcast_to(source[pl.ds(at, 1), 0], (rows, rows)).T
        factor = weight * wide
        for m in range(kt):
            chi = basis[b * rows : (b + 1) * rows, m * tile : (m + 1) * tile]
            scaled[m] = (chi.astype(jnp.float32) * factor).astype(jnp.bfloat16).T
            scaled[kt + m] = chi

        @pl.loop(0, pairs)
        def _(k):
            q = positions[b, k]
            product = jnp.dot(
                scaled[q // kt], scaled[kt + q % kt], preferred_element_type=jnp.float32
            )
            staged[b * pairs + k] = product.astype(jnp.bfloat16)
            send(b, k).start()

    for b in range(blocks):

        @pl.loop(0, pairs)
        def _(k):
            send(b, k).wait()


def field_and_tiles(kept, counts, slots, positions, first, raw, source, basis, slot_count):
    blocks, pairs = positions.shape
    total, rows = raw.shape
    tile = 128
    kt = basis.shape[1] // tile
    smem = pl.BlockSpec(memory_space=pltpu.SMEM)
    vmem = pl.BlockSpec(memory_space=pltpu.VMEM)
    return pl.pallas_call(
        field_kernel,
        in_specs=[smem] * 5 + [vmem] * 3,
        out_specs=[vmem, pl.BlockSpec(memory_space=pl.ANY)],
        out_shape=[
            jax.ShapeDtypeStruct((blocks, rows), jnp.float32),
            jax.ShapeDtypeStruct((slot_count, tile, tile), jnp.bfloat16),
        ],
        scratch_shapes=[
            pltpu.VMEM((6, total, rows), jnp.float32),
            pltpu.VMEM((5, rows, rows), jnp.float32),
            pltpu.VMEM((2 * kt, tile, rows), jnp.bfloat16),
            pltpu.VMEM((blocks * pairs, tile, tile), jnp.bfloat16),
            pltpu.SemaphoreType.DMA((blocks * pairs,)),
        ],
        compiler_params=params(),
        name="field_and_tiles",
    )(kept, counts, slots, positions, first, raw, source, basis)


def collect_kernel(order, starts, landed, out):
    step = pl.program_id(0)
    width = out.shape[0]

    @pl.loop(0, width)
    def _(t):
        g = step * width + t

        def add(j, total):
            return total + landed[order[j]].astype(jnp.float32)

        out[t] = lax.fori_loop(
            starts[g], starts[g + 1], add, jnp.zeros(out.shape[1:], jnp.float32)
        )


def collect_tiles(order, starts, landed, store_count):
    tile = landed.shape[1]
    group = 8
    smem = pl.BlockSpec(memory_space=pltpu.SMEM)
    return pl.pallas_call(
        collect_kernel,
        grid=(store_count // group,),
        in_specs=[smem, smem, pl.BlockSpec(memory_space=pltpu.VMEM)],
        out_specs=pl.BlockSpec((group, tile, tile), lambda i: (i, 0, 0)),
        out_shape=jax.ShapeDtypeStruct((store_count, tile, tile), jnp.float32),
        compiler_params=params(),
        name="collect_tiles",
    )(order, starts, landed)


def kept_list(keep):
    width = keep.shape[1]
    places = jnp.arange(width, dtype=jnp.int32)
    rank = jnp.cumsum(keep, axis=1) - keep
    hit = (rank[:, :, None] == places[None, None, :]) & (keep[:, :, None] > 0)
    return (
        jnp.sum(jnp.where(hit, places[None, :, None], 0), axis=1),
        jnp.sum(keep, axis=1),
    )


def slot_order(asked, store_count):
    count = asked.shape[0]
    places = jnp.arange(count, dtype=jnp.int32)
    key = jnp.where(asked >= 0, asked, store_count) * count + places
    rank = jnp.sum((key[None, :] < key[:, None]).astype(jnp.int32), axis=1)
    order = jnp.sum(jnp.where(rank[:, None] == places[None, :], places[:, None], 0), axis=0)
    stores = jnp.arange(store_count + 1, dtype=jnp.int32)
    starts = jnp.sum(
        ((asked[None, :] >= 0) & (asked[None, :] < stores[:, None])).astype(jnp.int32), axis=1
    )
    return order, starts


def body(basis, dmat, tile_home, pair_tiles, pair_pos, coords, weights, grad_sq, pair_keep):
    peer_count = lax.axis_size(AXES)
    me = lax.axis_index(AXES)
    blocks, pairs = pair_tiles.shape
    store_count, tile = dmat.shape[0], dmat.shape[1]
    rows = basis.shape[0] // blocks
    capacity = 2
    slot_count = peer_count * capacity
    wanted = tile_home[pair_tiles.reshape(-1)]
    owner = wanted // store_count
    within = wanted % store_count
    same = owner[:, None] == owner[None, :]
    places = jnp.arange(blocks * pairs, dtype=jnp.int32)
    earlier = jnp.sum((same & (places[None, :] < places[:, None])).astype(jnp.int32), axis=1)
    slots = owner * capacity + earlier
    slot_places = jnp.arange(slot_count, dtype=jnp.int32)
    asking = (
        jnp.sum(jnp.where(slots[:, None] == slot_places[None, :], within[:, None] + 1, 0), axis=0) - 1
    )
    asked = lax.all_to_all(
        asking.reshape(peer_count, capacity), AXES, split_axis=0, concat_axis=0, tiled=True
    ).reshape(-1)

    arrived = lax.all_to_all(
        pick_tiles(asked, dmat).reshape(peer_count, capacity, tile, tile),
        AXES,
        split_axis=0,
        concat_axis=0,
        tiled=True,
    ).reshape(slot_count, tile, tile)

    mine = jnp.concatenate([weights[None], grad_sq[None], coords], axis=0)
    mine = mine.reshape(5, blocks, rows).transpose(1, 0, 2)
    source = lax.all_gather(mine, AXES, axis=0, tiled=True)
    keep = lax.dynamic_slice_in_dim(pair_keep, me * blocks, blocks, 0)
    kept, counts = kept_list(keep)
    order, starts = slot_order(asked, store_count)

    raw = block_density(slots, pair_pos, basis, arrived)
    raw = lax.all_gather(raw, AXES, axis=0, tiled=True)
    first = (me * blocks).astype(jnp.int32).reshape(1)
    field, returning = field_and_tiles(
        kept, counts, slots, pair_pos, first, raw, source, basis, slot_count
    )
    landed = lax.all_to_all(
        returning.reshape(peer_count, capacity, tile, tile),
        AXES,
        split_axis=0,
        concat_axis=0,
        tiled=True,
    ).reshape(slot_count, tile, tile)
    return collect_tiles(order, starts, landed, store_count), field.reshape(-1)


def solution(mesh):
    in_specs = (
        P(AXES, None),
        P(AXES, None, None),
        P(),
        P(AXES, None),
        P(AXES, None),
        P(None, AXES),
        P(AXES),
        P(AXES),
        P(),
    )
    out_specs = (P(AXES, None, None), P(AXES))
    return jax.shard_map(body, mesh=mesh, in_specs=in_specs, out_specs=out_specs, check_vma=False)
```

time: 875 us -> 349 us (0.40); the launches traced: 864 us -> 347 us
  other arithmetic: 332 us -> 7.86 us
  local copies, waits for them, and re-layouts: 125 us -> 3.56 us
  waiting for transfers between devices: 278 us -> 195 us
  Pallas kernels: 0 us -> 50.8 us
  loops' own time: 21.5 us -> 0 us
  matrix products: 20.5 us -> 0 us
    reduce_sum x17 -> x7, other arithmetic: 320 us -> 4.91 us  [the longest x1 1.67 us: kept_list(): jnp.sum(jnp.where(hit, places[None, :, None], 0), axis=1)]
    unnamed x2 -> x1, waiting for transfers between devices: 94.2 us -> 0.03 us
    pallas_call x0 -> x4, Pallas kernels: none -> 50.8 us  [the longest x1 26 us: field_and_tiles(): pl.pallas_call(field_kernel, in_specs=[smem] * 5 + [vmem] * 3, out_specs=...]
    gather x11 -> x1, local copies, waits for them, and re-layouts: 39.4 us -> 1.15 us  [body(): wanted = tile_home[pair_tiles.reshape(-1)]]
    unnamed x23 -> x12, local copies, waits for them, and re-layouts: 29.6 us -> 0.03 us
    another operation x1 -> x0, loops' own time: 21.5 us -> none  [target_sweep(): lax.map(one_group, jnp.arange(turns_count, dtype=jnp.int32)).reshape(-1)]
    dot_general x3 -> x0, matrix products: 20.5 us -> none  [the longest x1 7.72 us: body(): jnp.einsum('bpna,bnac->bpnc', left_orb, fetched, preferred_element_type=j...]
    scatter x2 -> x0, local copies, waits for them, and re-layouts: 20.3 us -> none  [the longest x1 19.3 us: body(): returning = jnp.zeros((peer_count * capacity, tile_width, tile_width), jn...]
  transfers between devices with their start and end apart: 3 -> 3, of which waited for: 3 -> 2; matrix products, arithmetic and copies ran while one was open for 2% -> 2% of each run, Pallas kernels for 0% -> 2%
where the time goes in v1:
time: 349 us; the launch traced here: 347 us
  waiting for transfers between devices  195 us (56%)
  blocking collectives  63.2 us (18%)
  Pallas kernels  50.8 us (15%)
  between operations  14.2 us (4%)
  starting transfers between devices  12.2 us (3%)
  other arithmetic  7.86 us (2%)
  local copies, waits for them, and re-layouts  3.56 us (1%)
    all_to_all x1, waiting for transfers between devices, body(): lax.all_to_all(returning.reshape(peer_count, capacity, tile, tile), AXES,...  99.1 us
    all_to_all x1, waiting for transfers between devices, body(): lax.all_to_all(pick_tiles(asked, dmat).reshape(peer_count, capacity, tile...  95.9 us
    all_gather x1, blocking collectives, body(): raw = lax.all_gather(raw, AXES, axis=0, tiled=True)  42.5 us
    pallas_call x1, Pallas kernels, field_and_tiles(): pl.pallas_call(field_kernel, in_specs=[smem] * 5 + [vmem] * 3, out_specs=...  26 us
    all_to_all x1, blocking collectives, body(): lax.all_to_all(asking.reshape(peer_count, capacity), AXES, split_axis=0,...  20.7 us
    pallas_call x1, Pallas kernels, block_density(): pl.pallas_call(density_kernel, in_specs=[pl.BlockSpec(memory_space=pltpu....  8.41 us
    pallas_call x1, Pallas kernels, pick_tiles(): pl.pallas_call(pick_kernel, grid=(count // group,), in_specs=[pl.BlockSpe...  8.18 us
    pallas_call x1, Pallas kernels, collect_tiles(): pl.pallas_call(collect_kernel, grid=(store_count // group,), in_specs=[sm...  8.16 us
  transfers between devices with their start and end apart: 3, of which 2 were waited for; matrix products, arithmetic and copies ran while one was open for 2% of the time, Pallas kernels for 2%

profile of v1, /device:TPU:1, one launch (start us, length us, event | category | flops | bytes accessed | tf_op | source)
XLA Modules:
  0.0 346.9 jit_solution(8323878456717803642)
XLA Ops:
  7.2 0.8 reshape.186
  8.0 1.1 gather_fusion
  9.6 20.7 %all_to_all.16 = s32[128,1,2]{2,1,0:T(1,128)S(1)} all-to-all(s32[128,1,2]{2,1,0:T(1,128)S(1)} %bitcast.24), channel_id=1, replica_groups=mesh['row'=4,'col'=32] {'row','col'}, dimensions={0} | all-to-all | bytes 2048 | tf_op jit(solution)/shard_map/all_to_all | solution.py:287
  30.3 0.5 broadcast.185
  30.8 0.8 reduce.5
  31.6 0.7 reshape.187.asked
  32.4 8.2 %pick_tiles.1 = bf16[256,128,128]{2,1,0:T(8,128)(2,1)} custom-call(s32[256]{0:T(256)} %reshape.187.asked, bf16[64,128,128]{2,1,0:T(8,128)(2,1)} %tiles.1), custom_call_target="tpu_custom_call" | custom-call | tf_op jit(solution)/shard_map/pick_tiles/pallas_call | solution.py:45
  40.6 6.0 %all-to-all-start.1 = ((bf16[128,2,128,128]{3,2,1,0:T(8,128)(2,1)}), bf16[128,2,128,128]{3,2,1,0:T(8,128)(2,1)}, u32[]{:S(2)}, u32[]{:S(2)}) async-start(bf16[128,2,128,128]{3,2,1,0:T(8,128)(2,1)} %bitcast.21), calls=%async_computation.1 | async-start | bytes 16777216 | tf_op jit(solution)/shard_map/all_to_all | solution.py:291
  46.6 0.6 maximum_bitcast_fusion
  47.3 1.4 fusion.5
  48.7 1.2 reduce-window.6
  49.9 0.2 slice_reduce_fusion
  50.1 0.2 reduce-window.9
  50.4 1.7 select_reduce_fusion.kept
  52.1 95.9 %all-to-all-done.1 = bf16[128,2,128,128]{3,2,1,0:T(8,128)(2,1)} async-done(((bf16[128,2,128,128]{3,2,1,0:T(8,128)(2,1)}), bf16[128,2,128,128]{3,2,1,0:T(8,128)(2,1)}, u32[]{:S(2)}, u32[]{:S(2)}) %all-to-all-start.1) | async-done | bytes 8388640 | tf_op jit(solution)/shard_map/all_to_all | solution.py:291
  148.0 8.4 %block_density.1 = f32[4,128]{1,0:T(4,128)} custom-call(s32[128]{0:T(128)} %copy-done.3, s32[4,32]{1,0:T(4,128)} %positions.3, bf16[512,1024]{1,0:T(8,128)(2,1)} %basis.3, bf16[256,128,128]{2,1,0:T(8,128)(2,1)} %bitcast.4.arrived), custom_call_target="tpu_custom_call" | custom-call | tf_op jit(solution)/shard_map/block_density/pallas_call | solution.py:103
  156.4 42.5 %all-gather = f32[128,4,128]{2,1,0:T(4,128)} all-gather(f32[1,4,128]{2,1,0:T(4,128)} %bitcast.25), channel_id=1, replica_groups=mesh['row'=4,'col'=32] {'row','col'}, dimensions={0}, use_global_device_ids=true | all-gather | bytes 264192 | tf_op jit(solution)/shard_map/all_gather | solution.py:307
  198.9 26.0 %field_and_tiles.1 = (f32[4,128]{1,0:T(4,128)}, bf16[256,128,128]{2,1,0:T(8,128)(2,1)}) custom-call(s32[4,512]{1,0:T(4,128)} %select_reduce_fusion.kept, s32[4]{0:T(128)} %get-tuple-element.6.counts, s32[128]{0:T(128)} %copy-done.3, s32[4,32]{1,0:T(4,128)} %positions.3, s32[1]{0:T(128)} %bitcast.2.first, f32[512,128]{1,0:T(8,128)} %bitcast.23, ...), custom_call_target="tpu_custom_call" | custom-call | tf_op jit(solution)/shard_map/field_and_tiles/pallas_call | solution.py:193
  225.0 6.2 %all-to-all-start.2 = ((bf16[128,2,128,128]{3,2,1,0:T(8,128)(2,1)}), bf16[128,2,128,128]{3,2,1,0:T(8,128)(2,1)}, u32[]{:S(2)}, u32[]{:S(2)}) async-start(bf16[128,2,128,128]{3,2,1,0:T(8,128)(2,1)} %bitcast.22), calls=%async_computation.2 | async-start | bytes 16777216 | tf_op jit(solution)/shard_map/all_to_all | solution.py:312
  231.2 0.7 convert_reduce_fusion.1.starts
  231.9 0.2 convert_reduce_fusion
  232.1 0.7 select_reduce_fusion.1.order
  232.8 99.1 %all-to-all-done.2 = bf16[128,2,128,128]{3,2,1,0:T(8,128)(2,1)} async-done(((bf16[128,2,128,128]{3,2,1,0:T(8,128)(2,1)}), bf16[128,2,128,128]{3,2,1,0:T(8,128)(2,1)}, u32[]{:S(2)}, u32[]{:S(2)}) %all-to-all-start.2) | async-done | bytes 8388640 | tf_op jit(solution)/shard_map/all_to_all | solution.py:312
  331.9 8.2 %collect_tiles.1 = f32[64,128,128]{2,1,0:T(8,128)} custom-call(s32[256]{0:T(256)} %select_reduce_fusion.1.order, s32[65]{0:T(128)} %convert_reduce_fusion.1.starts, bf16[256,128,128]{2,1,0:T(8,128)(2,1)} %bitcast.12.landed), custom_call_target="tpu_custom_call" | custom-call | tf_op jit(solution)/shard_map/collect_tiles/pallas_call | solution.py:233
  (29 shorter events, 0.7 us)
Async XLA Ops:
  7.2 0.8 copy-start
  9.3 31.2 %copy-start.3 = (s32[128]{0:T(128)}, s32[128]{0:T(128)S(1)}, u32[]{:S(2)}) copy-start(s32[128]{0:T(128)S(1)} %multiply_add_fusion.slots) | copy-start | bytes 1540
  40.6 6.0 %copy-start.2 = (f32[3,512]{1,0:T(4,128)S(1)}, f32[3,512]{1,0:T(4,128)}, u32[]{:S(2)}) copy-start(f32[3,512]{1,0:T(4,128)} %param.14) | copy-start | bytes 18436
  40.6 6.1 %copy-start.4 = (f32[512]{0:T(512)S(1)}, f32[512]{0:T(512)}, u32[]{:S(2)}) copy-start(f32[512]{0:T(512)} %param.16) | copy-start | bytes 6148
  40.6 6.1 %copy-start.5 = (f32[512]{0:T(512)S(1)}, f32[512]{0:T(512)}, u32[]{:S(2)}) copy-start(f32[512]{0:T(512)} %param.15) | copy-start | bytes 6148
  40.6 107.4 %all-to-all-start.1 = ((bf16[128,2,128,128]{3,2,1,0:T(8,128)(2,1)}), bf16[128,2,128,128]{3,2,1,0:T(8,128)(2,1)}, u32[]{:S(2)}, u32[]{:S(2)}) async-start(bf16[128,2,128,128]{3,2,1,0:T(8,128)(2,1)} %bitcast.21), calls=%async_computation.1 | async-start | bytes 16777216 | tf_op jit(solution)/shard_map/all_to_all | solution.py:291
  46.6 152.4 %all-gather.3.cloned.1.call-start = ((), (), s32[]{:S(2)}) async-start(), calls=%async_computation.3 | async-start | bytes 2113536 | tf_op jit(solution)/shard_map/all_gather | solution.py:301
  225.0 6.2 %copy-start.1 = (s32[256]{0:T(256)S(1)}, s32[256]{0:T(256)}, u32[]{:S(2)}) copy-start(s32[256]{0:T(256)} %reshape.187.asked) | copy-start | bytes 3076
  225.0 106.9 %all-to-all-start.2 = ((bf16[128,2,128,128]{3,2,1,0:T(8,128)(2,1)}), bf16[128,2,128,128]{3,2,1,0:T(8,128)(2,1)}, u32[]{:S(2)}, u32[]{:S(2)}) async-start(bf16[128,2,128,128]{3,2,1,0:T(8,128)(2,1)} %bitcast.22), calls=%async_computation.2 | async-start | bytes 16777216 | tf_op jit(solution)/shard_map/all_to_all | solution.py:312
Sparse Core Ops, SparseCore 0:
  51.1 137.0 all-gather.2

commit v2 on v1

--- a/solution.py
+++ b/solution.py
@@ -12,6 +12,8 @@
 density_floor = 0.1
 AXES = ("row", "col")
 VMEM_LIMIT = 56 * 2**20
+MESH = pl.DeviceIdType.MESH
+STRIDE = 37
 
 
 def point_features(raw_density, grad_sq):
@@ -26,97 +28,169 @@
     return pltpu.CompilerParams(vmem_limit_bytes=VMEM_LIMIT, **more)
 
 
-def pick_kernel(asked, tiles, out):
-    step = pl.program_id(0)
-    width = out.shape[0]
-
-    @pl.loop(0, width)
-    def _(slot):
-        wanted = asked[step * width + slot]
-
-        @pl.when(wanted >= 0)
-        def _():
-            out[slot] = tiles[wanted]
-
-
-def pick_tiles(asked, tiles):
-    count = asked.shape[0]
-    group = 32
-    return pl.pallas_call(
-        pick_kernel,
-        grid=(count // group,),
-        in_specs=[
-            pl.BlockSpec(memory_space=pltpu.SMEM),
-            pl.BlockSpec(memory_space=pltpu.VMEM),
-        ],
-        out_specs=pl.BlockSpec((group,) + tiles.shape[1:], lambda i: (i, 0, 0)),
-        out_shape=jax.ShapeDtypeStruct((count,) + tiles.shape[1:], tiles.dtype),
-        compiler_params=params(),
-        name="pick_tiles",
-    )(asked, tiles)
-
-
-def density_kernel(slots, positions, basis, arrived, raw, dense, sems):
-    blocks, pairs = positions.shape
+def neighbour(step):
+    row, col = lax.axis_index("row"), lax.axis_index("col")
+    x, z, core = col // 8, lax.rem(col // 2, 4), lax.rem(col, 2)
+    y = lax.rem(row + step // 32, 4)
+    x = lax.rem(x + lax.rem(step // 8, 4), 4)
+    z = lax.rem(z + lax.rem(step // 2, 4), 4)
+    core = lax.rem(core + lax.rem(step, 2), 2)
+    return y, x * 8 + z * 2 + core
+
+
+def device_number(place):
+    return place[0] * 32 + place[1]
+
+
+def greet_all(peers):
+    barrier = pltpu.get_barrier_semaphore()
+    for step in range(1, peers):
+        pl.semaphore_signal(barrier, inc=1, device_id=neighbour(step), device_id_type=MESH)
+    pl.semaphore_wait(barrier, peers - 1)
+
+
+def fetch_kernel(
+    asking,
+    table,
+    tiles,
+    basis,
+    asked,
+    raw_all,
+    wanted,
+    stage,
+    arrived,
+    dense,
+    raw,
+    smem_sem,
+    ask_send,
+    ask_recv,
+    tile_send,
+    tile_recv,
+    raw_send,
+    raw_recv,
+):
+    peers = asking.shape[0]
+    blocks, places = table.shape
+    orbs = basis.shape[1]
     rows = basis.shape[0] // blocks
-    orbs = basis.shape[1]
-    tile = arrived.shape[1]
+    tile = tiles.shape[1]
     kt = orbs // tile
-
-    dense[...] = jnp.zeros_like(dense)
-
-    def fetch(b, k):
-        q = positions[b, k]
-        left = pl.multiple_of((q // kt) * tile, tile)
-        right = pl.multiple_of((q % kt) * tile, tile)
-        return pltpu.make_async_copy(
-            arrived.at[slots[b * pairs + k]],
-            dense.at[b, pl.ds(left, tile), pl.ds(right, tile)],
-            sems.at[b * pairs + k],
+    me = device_number((lax.axis_index("row"), lax.axis_index("col")))
+
+    def remote(source, target, send, recv, step, place):
+        return pltpu.make_async_remote_copy(
+            src_ref=source,
+            dst_ref=target,
+            send_sem=send.at[step],
+            recv_sem=recv.at[step],
+            device_id=place,
+            device_id_type=MESH,
         )
 
+    def ask(step):
+        place = neighbour(step)
+        return remote(
+            asking.at[device_number(place)], asked.at[me], ask_send, ask_recv, step, place
+        )
+
+    def give(step):
+        place = neighbour(step)
+        return remote(
+            stage.at[device_number(place)], arrived.at[me], tile_send, tile_recv, step, place
+        )
+
+    def tell(step):
+        return remote(raw, raw_all.at[me], raw_send, raw_recv, step, neighbour(step))
+
+    greet_all(peers)
+
+    @pl.loop(1, peers)
+    def _(step):
+        ask(step).start()
+
+    asked[me] = asking[me]
+    arrived[peers] = jnp.zeros(arrived.shape[1:], arrived.dtype)
+
+    @pl.loop(1, peers)
+    def _(step):
+        ask(step).wait()
+
+    to_smem = pltpu.make_async_copy(asked, wanted, smem_sem)
+    to_smem.start()
+    to_smem.wait()
+
+    @pl.loop(1, peers)
+    def _(turn):
+        step = lax.rem(turn * STRIDE, peers)
+        to = device_number(neighbour(step))
+        for slot in range(2):
+            stage[to, slot] = tiles[jnp.maximum(wanted[to, 0, slot] - 1, 0)]
+        give(step).start()
+
+    for slot in range(2):
+        arrived[me, slot] = tiles[jnp.maximum(wanted[me, 0, slot] - 1, 0)]
+
+    @pl.loop(1, peers)
+    def _(step):
+        give(step).wait()
+
     for b in range(blocks):
 
-        @pl.loop(0, pairs)
-        def _(k):
-            fetch(b, k).start()
-
-    for b in range(blocks):
-
-        @pl.loop(0, pairs)
-        def _(k):
-            fetch(b, k).wait()
+        @pl.loop(0, kt)
+        def _(left):
+            for right in range(kt):
+                slot = table[b, left * kt + right]
+                dense[pl.ds(pl.multiple_of(left * tile, tile), tile), right * tile : (right + 1) * tile] = (
+                    arrived[slot // 2, lax.rem(slot, 2)]
+                )
 
         chi = basis[b * rows : (b + 1) * rows, :]
-        mixed = jnp.dot(chi, dense[b], preferred_element_type=jnp.float32)
+        mixed = jnp.dot(chi, dense[...], preferred_element_type=jnp.float32)
         both = mixed * chi.astype(jnp.float32)
         part = both[:, :tile]
         for m in range(1, kt):
             part = part + both[:, m * tile : (m + 1) * tile]
         raw[b : b + 1, :] = jnp.sum(part.T, axis=0, keepdims=True)
 
-
-def block_density(slots, positions, basis, arrived):
-    blocks = positions.shape[0]
+    @pl.loop(1, peers)
+    def _(step):
+        tell(step).start()
+
+    raw_all[me] = raw[...]
+
+    @pl.loop(1, peers)
+    def _(step):
+        tell(step).wait()
+
+
+def fetch_and_density(asking, table, tiles, basis):
+    peers = asking.shape[0]
+    blocks = table.shape[0]
+    tile = tiles.shape[1]
     rows = basis.shape[0] // blocks
     orbs = basis.shape[1]
+    smem = pl.BlockSpec(memory_space=pltpu.SMEM)
+    vmem = pl.BlockSpec(memory_space=pltpu.VMEM)
     return pl.pallas_call(
-        density_kernel,
-        in_specs=[
-            pl.BlockSpec(memory_space=pltpu.SMEM),
-            pl.BlockSpec(memory_space=pltpu.SMEM),
-            pl.BlockSpec(memory_space=pltpu.VMEM),
-            pl.BlockSpec(memory_space=pl.ANY),
+        fetch_kernel,
+        in_specs=[vmem, smem, vmem, vmem],
+        out_specs=[vmem, vmem],
+        out_shape=[
+            jax.ShapeDtypeStruct(asking.shape, asking.dtype),
+            jax.ShapeDtypeStruct((peers, blocks, rows), jnp.float32),
         ],
-        out_specs=pl.BlockSpec(memory_space=pltpu.VMEM),
-        out_shape=jax.ShapeDtypeStruct((blocks, rows), jnp.float32),
         scratch_shapes=[
-            pltpu.VMEM((blocks, orbs, orbs), basis.dtype),
-            pltpu.SemaphoreType.DMA((positions.size,)),
-        ],
-        compiler_params=params(),
-        name="block_density",
-    )(slots, positions, basis, arrived)
+            pltpu.SMEM(asking.shape, asking.dtype),
+            pltpu.VMEM((peers, 2, tile, tile), tiles.dtype),
+            pltpu.VMEM((peers + 1, 2, tile, tile), tiles.dtype),
+            pltpu.VMEM((orbs, orbs), basis.dtype),
+            pltpu.VMEM((blocks, rows), jnp.float32),
+            pltpu.SemaphoreType.DMA,
+        ]
+        + [pltpu.SemaphoreType.DMA((peers,))] * 6,
+        compiler_params=params(collective_id=0, has_side_effects=True),
+        name="fetch_and_density",
+    )(asking, table, tiles, basis)
 
 
 def field_kernel(
@@ -281,30 +355,28 @@
     earlier = jnp.sum((same & (places[None, :] < places[:, None])).astype(jnp.int32), axis=1)
     slots = owner * capacity + earlier
     slot_places = jnp.arange(slot_count, dtype=jnp.int32)
-    asking = (
-        jnp.sum(jnp.where(slots[:, None] == slot_places[None, :], within[:, None] + 1, 0), axis=0) - 1
+    lanes = jnp.arange(tile, dtype=jnp.int32)
+    entry = jnp.where(
+        (owner[:, None] == jnp.arange(peer_count, dtype=jnp.int32)[None, :])[:, :, None]
+        & (earlier[:, None] == lanes[None, :])[:, None, :],
+        within[:, None, None] + 1,
+        0,
     )
-    asked = lax.all_to_all(
-        asking.reshape(peer_count, capacity), AXES, split_axis=0, concat_axis=0, tiled=True
-    ).reshape(-1)
-
-    arrived = lax.all_to_all(
-        pick_tiles(asked, dmat).reshape(peer_count, capacity, tile, tile),
-        AXES,
-        split_axis=0,
-        concat_axis=0,
-        tiled=True,
-    ).reshape(slot_count, tile, tile)
-
+    asking = jnp.sum(entry, axis=0).reshape(peer_count, 1, tile)
+    kt = basis.shape[1] // tile
+    spot = pair_pos[:, :, None] == jnp.arange(kt * kt, dtype=jnp.int32)[None, None, :]
+    table = jnp.sum(
+        jnp.where(spot, slots.reshape(blocks, pairs)[:, :, None] - slot_count, 0), axis=1
+    ) + slot_count
     mine = jnp.concatenate([weights[None], grad_sq[None], coords], axis=0)
     mine = mine.reshape(5, blocks, rows).transpose(1, 0, 2)
     source = lax.all_gather(mine, AXES, axis=0, tiled=True)
     keep = lax.dynamic_slice_in_dim(pair_keep, me * blocks, blocks, 0)
     kept, counts = kept_list(keep)
-    order, starts = slot_order(asked, store_count)
-
-    raw = block_density(slots, pair_pos, basis, arrived)
-    raw = lax.all_gather(raw, AXES, axis=0, tiled=True)
+
+    asked, raw = fetch_and_density(asking, table, dmat, basis)
+    raw = raw.reshape(peer_count * blocks, rows)
+    order, starts = slot_order(asked[:, 0, :capacity].reshape(-1) - 1, store_count)
     first = (me * blocks).astype(jnp.int32).reshape(1)
     field, returning = field_and_tiles(
         kept, counts, slots, pair_pos, first, raw, source, basis, slot_count

time: 349 us -> 318 us (0.911)
  Pallas kernels: 50.8 us -> 182 us
  waiting for transfers between devices: 195 us -> 98.8 us
  blocking collectives: 63.2 us -> 0 us
  starting transfers between devices: 12.2 us -> 6.18 us
  other arithmetic: 7.86 us -> 13.5 us
    pallas_call x2 -> x1, Pallas kernels: 16.6 us -> 147 us  [fetch_and_density(): pl.pallas_call(fetch_kernel, in_specs=[vmem, smem, vmem, vmem], out_specs...]
    all_to_all x1 -> x0, waiting for transfers between devices: 95.9 us -> none  [body(): lax.all_to_all(pick_tiles(asked, dmat).reshape(peer_count, capacity, tile...]
    all_gather x1 -> x0, blocking collectives: 42.5 us -> none  [body(): raw = lax.all_gather(raw, AXES, axis=0, tiled=True)]
    all_to_all x1 -> x0, blocking collectives: 20.7 us -> none  [body(): lax.all_to_all(asking.reshape(peer_count, capacity), AXES, split_axis=0,...]
    all_to_all x1 -> x0, starting transfers between devices: 5.97 us -> none  [body(): lax.all_to_all(pick_tiles(asked, dmat).reshape(peer_count, capacity, tile...]
    reduce_sum x1 -> x2, other arithmetic: 0.11 us -> 4.35 us  [the longest x1 3.56 us: body(): asking = jnp.sum(entry, axis=0).reshape(peer_count, 1, tile)]
  transfers between devices with their start and end apart: 3 -> 2, of which waited for: 2 -> 1; matrix products, arithmetic and copies ran while one was open for 2% -> 5% of each run, Pallas kernels for 2% -> 47%
where the time goes in v2:
time: 318 us; the launch traced here: 317 us
  Pallas kernels  182 us (57%)
  waiting for transfers between devices  98.8 us (31%)
  between operations  14.1 us (4%)
  other arithmetic  13.5 us (4%)
  starting transfers between devices  6.18 us (2%)
    pallas_call x1, Pallas kernels, fetch_and_density(): pl.pallas_call(fetch_kernel, in_specs=[vmem, smem, vmem, vmem], out_specs...  147 us
    all_to_all x1, waiting for transfers between devices, body(): lax.all_to_all(returning.reshape(peer_count, capacity, tile, tile), AXES,...  98.7 us
    pallas_call x1, Pallas kernels, field_and_tiles(): pl.pallas_call(field_kernel, in_specs=[smem] * 5 + [vmem] * 3, out_specs=...  26.3 us
    pallas_call x1, Pallas kernels, collect_tiles(): pl.pallas_call(collect_kernel, grid=(store_count // group,), in_specs=[sm...  8.05 us
  transfers between devices with their start and end apart: 2, of which 1 were waited for; matrix products, arithmetic and copies ran while one was open for 5% of the time, Pallas kernels for 47%

profile of v2, /device:TPU:1, one launch (start us, length us, event | category | flops | bytes accessed | tf_op | source)
XLA Modules:
  0.0 316.7 jit_solution(5314089145398180351)
XLA Ops:
  7.2 1.3 maximum_bitcast_fusion
  8.6 0.8 reshape.232
  9.4 1.1 gather_fusion
  10.6 0.2 convert_reduce_fusion.2
  10.9 1.4 fusion.10
  12.3 1.2 reduce-window.6
  13.5 0.2 slice_reduce_fusion
  13.7 0.2 reduce-window.9
  13.9 0.8 select_reduce_fusion.3
  14.7 0.6 broadcast_add_fusion.table
  15.3 0.1 iota_compare_fusion.4
  15.4 3.6 %select_reduce_fusion = s32[128,128]{1,0:T(8,128)} fusion(s32[128]{0:T(128)S(1)} %get-tuple-element.13, pred[128,128]{1,0:T(8,128)(4,1)S(1)} %get-tuple-element.14, pred[128,128]{1,0:T(8,128)(4,1)S(1)} %get-tuple-element.15), kind=kLoop, calls=%fused_computation.1 | loop fusion | flops 6275072 | bytes 98816 | tf_op jit(solution)/shard_map/reduce_sum | solution.py:365
  19.0 147.4 %fetch_and_density.1 = (s32[128,1,128]{2,1,0:T(1,128)}, f32[128,4,128]{2,1,0:T(4,128)}) custom-call(s32[128,1,128]{2,1,0:T(1,128)} %bitcast.20, s32[4,64]{1,0:T(4,128)} %broadcast_add_fusion.table, bf16[64,128,128]{2,1,0:T(8,128)(2,1)} %tiles.1, bf16[512,1024]{1,0:T(8,128)(2,1)} %basis.3), custom_call_target="tpu_custom_call" | custom-call | tf_op jit(solution)/shard_map/fetch_and_density/pallas_call | solution.py:174
  166.3 0.6 multiply_add_fusion.slots
  167.0 1.7 select_reduce_fusion.1.kept
  168.7 26.3 %field_and_tiles.1 = (f32[4,128]{1,0:T(4,128)}, bf16[256,128,128]{2,1,0:T(8,128)(2,1)}) custom-call(s32[4,512]{1,0:T(4,128)} %select_reduce_fusion.1.kept, s32[4]{0:T(128)} %get-tuple-element.10.counts, s32[128]{0:T(128)} %multiply_add_fusion.slots, s32[4,32]{1,0:T(4,128)} %positions.1, s32[1]{0:T(128)} %bitcast.2.first, f32[512,128]{1,0:T(8,128)} %bitcast.19, ...), custom_call_target="tpu_custom_call" | custom-call | tf_op jit(solution)/shard_map/field_and_tiles/pallas_call | solution.py:267
  195.0 6.1 %all-to-all-start = ((bf16[128,2,128,128]{3,2,1,0:T(8,128)(2,1)}), bf16[128,2,128,128]{3,2,1,0:T(8,128)(2,1)}, u32[]{:S(2)}, u32[]{:S(2)}) async-start(bf16[128,2,128,128]{3,2,1,0:T(8,128)(2,1)} %bitcast.18), calls=%async_computation | async-start | bytes 16777216 | tf_op jit(solution)/shard_map/all_to_all | solution.py:384
  201.1 0.2 add_reduce_fusion
  201.3 0.1 sub.25
  201.5 0.7 convert_reduce_fusion.1.starts
  202.2 0.2 convert_reduce_fusion
  202.4 0.7 select_reduce_fusion.2.order
  203.1 98.7 %all-to-all-done = bf16[128,2,128,128]{3,2,1,0:T(8,128)(2,1)} async-done(((bf16[128,2,128,128]{3,2,1,0:T(8,128)(2,1)}), bf16[128,2,128,128]{3,2,1,0:T(8,128)(2,1)}, u32[]{:S(2)}, u32[]{:S(2)}) %all-to-all-start) | async-done | bytes 8388640 | tf_op jit(solution)/shard_map/all_to_all | solution.py:384
  301.8 8.0 %collect_tiles.1 = f32[64,128,128]{2,1,0:T(8,128)} custom-call(s32[256]{0:T(256)} %select_reduce_fusion.2.order, s32[65]{0:T(128)} %convert_reduce_fusion.1.starts, bf16[256,128,128]{2,1,0:T(8,128)(2,1)} %bitcast.9.landed), custom_call_target="tpu_custom_call" | custom-call | tf_op jit(solution)/shard_map/collect_tiles/pallas_call | solution.py:307
  (19 shorter events, 0.4 us)
Async XLA Ops:
  7.2 2.2 copy-start
  7.2 161.5 %all-gather.2.cloned.1.call-start = ((), (), s32[]{:S(2)}) async-start(), calls=%async_computation.1 | async-start | bytes 2113536 | tf_op jit(solution)/shard_map/all_gather | solution.py:373
  195.0 6.2 %copy-start.1 = (s32[128,1,128]{2,1,0:T(1,128)S(1)}, s32[128,1,128]{2,1,0:T(1,128)}, u32[]{:S(2)}) copy-start(s32[128,1,128]{2,1,0:T(1,128)} %get-tuple-element.6) | copy-start | bytes 196612
  195.0 106.8 %all-to-all-start = ((bf16[128,2,128,128]{3,2,1,0:T(8,128)(2,1)}), bf16[128,2,128,128]{3,2,1,0:T(8,128)(2,1)}, u32[]{:S(2)}, u32[]{:S(2)}) async-start(bf16[128,2,128,128]{3,2,1,0:T(8,128)(2,1)} %bitcast.18), calls=%async_computation | async-start | bytes 16777216 | tf_op jit(solution)/shard_map/all_to_all | solution.py:384
Sparse Core Ops, SparseCore 0:
  11.2 136.9 all-gather.1

commit v3 on v1

--- a/solution.py
+++ b/solution.py
@@ -12,6 +12,32 @@
 density_floor = 0.1
 AXES = ("row", "col")
 VMEM_LIMIT = 56 * 2**20
+MESH = pl.DeviceIdType.MESH
+STRIDE = 7
+STEPS = (
+    (0, 0, 0, 1),
+    (0, 1, 0, 0),
+    (1, 0, 0, 0),
+    (0, 0, 1, 0),
+    (0, 3, 0, 0),
+    (3, 0, 0, 0),
+    (0, 0, 3, 0),
+    (0, 1, 1, 1),
+    (1, 0, 1, 1),
+    (1, 1, 0, 1),
+    (0, 3, 3, 1),
+    (3, 0, 3, 1),
+    (3, 3, 0, 1),
+    (0, 1, 3, 1),
+    (1, 0, 3, 1),
+    (1, 3, 0, 1),
+)
+ROOM = (56, 8, 8, 8, 4, 4, 4) + (1,) * 9
+BASE = tuple(sum(ROOM[:k]) for k in range(len(ROOM)))
+LINKS = len(ROOM)
+RELAYED = sum(ROOM)
+PLAN_ROWS = 2 * LINKS + 8
+AT_LOC, AT_SRC, AT_CODE, AT_BACK, AT_LEFT = range(2 * LINKS, 2 * LINKS + 5)
 
 
 def point_features(raw_density, grad_sq):
@@ -24,6 +50,542 @@
 
 def params(**more):
     return pltpu.CompilerParams(vmem_limit_bytes=VMEM_LIMIT, **more)
+
+
+def moved(device, move):
+    dy, dx, dz, dc = move
+    y = (device // 32 + dy) % 4
+    x = (device // 8 + dx) % 4
+    z = (device // 2 + dz) % 4
+    return y * 32 + x * 8 + z * 2 + (device + dc) % 2
+
+
+def back(move):
+    return tuple((4 - m) % 4 for m in move[:3]) + (move[3],)
+
+
+def parity(device):
+    return (device + device // 2 + device // 8 + device // 32) % 2
+
+
+def this_device():
+    return lax.axis_index("row") * 32 + lax.axis_index("col")
+
+
+def inside(value, count):
+    return jnp.minimum(jnp.maximum(value, 0), count - 1)
+
+
+def place_of(device):
+    return device // 32, lax.rem(device, 32)
+
+
+def neighbour(step):
+    move = (step // 32, lax.rem(step // 8, 4), lax.rem(step // 2, 4), lax.rem(step, 2))
+    return moved(this_device(), move)
+
+
+def narrow_step(turn):
+    up = lax.rem(turn * STRIDE, 64)
+    return 2 * up + lax.rem(up + up // 4 + up // 16 + 1, 2)
+
+
+def wide_step(turn):
+    up = lax.rem(turn * STRIDE, 64)
+    return 2 * up + lax.rem(up + up // 4 + up // 16, 2)
+
+
+def greet_all(peers):
+    barrier = pltpu.get_barrier_semaphore()
+    for step in range(1, peers):
+        pl.semaphore_signal(
+            barrier, inc=1, device_id=place_of(neighbour(step)), device_id_type=MESH
+        )
+
+
+def wait_all(peers):
+    pl.semaphore_wait(pltpu.get_barrier_semaphore(), peers - 1)
+
+
+def remote(source, target, send, recv, at, device):
+    return pltpu.make_async_remote_copy(
+        src_ref=source,
+        dst_ref=target,
+        send_sem=send.at[at],
+        recv_sem=recv.at[at],
+        device_id=place_of(device),
+        device_id_type=MESH,
+    )
+
+
+def make_plan(counts, plan):
+    peers = counts.shape[0]
+    me = this_device()
+    asker = lax.broadcasted_iota(jnp.int32, (peers, peers), 0)
+    owner = lax.broadcasted_iota(jnp.int32, (peers, peers), 1)
+    wide = parity(asker) == parity(owner)
+    zero = jnp.zeros((peers, peers), jnp.float32)
+    left = jnp.where(wide | (counts < 2), 0.0, 1.0)
+    free = jnp.where(wide & (counts < 2), 1.0, 0.0)
+    earlier = jnp.where(owner < asker, 1.0, 0.0).astype(jnp.bfloat16)
+    loc, src, code, again = zero, zero, zero, zero
+
+    def dot(a, b):
+        return jnp.dot(
+            a.astype(jnp.bfloat16), b.astype(jnp.bfloat16), preferred_element_type=jnp.float32
+        )
+
+    def mine(values):
+        return jnp.sum(jnp.where(owner == me, values, 0.0), axis=1, keepdims=True)
+
+    def by_slot(column):
+        hit = column == (owner + 1).astype(jnp.float32)
+        return jnp.sum(jnp.where(hit, asker, 0), axis=0, keepdims=True)
+
+    for k in range(LINKS):
+        move, home = STEPS[k], back(STEPS[k])
+        there = moved(owner, move)
+        onto = jnp.where(asker == there, 1.0, 0.0)
+        off = jnp.where(owner == moved(asker, move), 1.0, 0.0)
+        want = left * dot(free, onto)
+        rank = dot(earlier, want)
+        numbered = jnp.where((want > 0.0) & (rank < ROOM[k]), rank + 1.0, 0.0)
+        relay = dot(numbered, off)
+        left = jnp.where(numbered > 0.0, 0.0, left)
+        free = jnp.where(relay > 0.0, 0.0, free)
+        loc = loc + jnp.where(numbered > 0.0, (2 * there + 1).astype(jnp.float32), 0.0)
+        src = src + jnp.where(relay > 0.0, (moved(owner, home) + 1).astype(jnp.float32), 0.0)
+        code = code + jnp.where(relay > 0.0, relay + BASE[k], 0.0)
+        again = again + jnp.where(numbered > 0.0, numbered + (BASE[k] - 1.0), 0.0)
+        plan[k : k + 1, :] = by_slot(mine(numbered))
+        plan[LINKS + k : LINKS + k + 1, :] = by_slot(mine(relay))
+
+    def row_of(values):
+        return jnp.sum(jnp.where(asker == me, values, 0.0), axis=0, keepdims=True)
+
+    def turned(values):
+        return jnp.sum(jnp.where(asker == owner, mine(values), 0.0), axis=0, keepdims=True)
+
+    plan[AT_LOC : AT_LOC + 1, :] = row_of(loc).astype(jnp.int32)
+    plan[AT_SRC : AT_SRC + 1, :] = row_of(src).astype(jnp.int32)
+    plan[AT_CODE : AT_CODE + 1, :] = turned(code).astype(jnp.int32)
+    plan[AT_BACK : AT_BACK + 1, :] = turned(again).astype(jnp.int32)
+    plan[AT_LEFT : AT_LEFT + 1, :] = jnp.sum(left, axis=0, keepdims=True).astype(jnp.int32)
+    plan[AT_LEFT + 1 :, :] = jnp.zeros((PLAN_ROWS - AT_LEFT - 1, peers), jnp.int32)
+
+
+def fetch_kernel(
+    asking,
+    table,
+    tiles,
+    basis,
+    asked,
+    plan,
+    raw_all,
+    wanted,
+    route,
+    stage,
+    arrived,
+    link_out,
+    link_in,
+    dense,
+    raw,
+    smem_sems,
+    ask_send,
+    ask_recv,
+    first_send,
+    first_recv,
+    second_send,
+    second_recv,
+    link_send,
+    link_recv,
+    raw_send,
+    raw_recv,
+):
+    peers = asking.shape[0]
+    blocks = table.shape[0]
+    orbs = basis.shape[1]
+    rows = basis.shape[0] // blocks
+    tile = tiles.shape[1]
+    kt = orbs // tile
+    me = this_device()
+
+    def ask(step):
+        to = neighbour(step)
+        return remote(asking.at[to], asked.at[me], ask_send, ask_recv, step, to)
+
+    def first(step):
+        to = neighbour(step)
+        return remote(stage.at[to, 0], arrived.at[me, 0], first_send, first_recv, step, to)
+
+    def second(step):
+        to = neighbour(step)
+        return remote(stage.at[to, 1], arrived.at[me, 1], second_send, second_recv, step, to)
+
+    def link(k):
+        part = pl.ds(BASE[k], ROOM[k])
+        return remote(
+            link_out.at[part], link_in.at[part], link_send, link_recv, k, moved(me, STEPS[k])
+        )
+
+    def tell(step):
+        return remote(raw, raw_all.at[me], raw_send, raw_recv, step, neighbour(step))
+
+    def tile_for(device, slot):
+        return tiles[inside(wanted[inside(device, peers), 0, slot] - 1, tiles.shape[0])]
+
+    def second_for(device):
+        at = route[AT_CODE, device]
+        return jnp.where(at > 0, link_in[inside(at - 1, RELAYED)], tile_for(device, 1))
+
+    greet_all(peers)
+    wait_all(peers)
+
+    @pl.loop(1, peers)
+    def _(step):
+        ask(step).start()
+
+    asked[me] = asking[me]
+    arrived[peers] = jnp.zeros(arrived.shape[1:], arrived.dtype)
+
+    @pl.loop(1, peers)
+    def _(step):
+        ask(step).wait()
+
+    to_smem = pltpu.make_async_copy(asked, wanted, smem_sems.at[0])
+    to_smem.start()
+    to_smem.wait()
+
+    @pl.loop(0, 64)
+    def _(turn):
+        step = narrow_step(turn)
+        to = neighbour(step)
+        stage[to, 0] = tile_for(to, 0)
+        first(step).start()
+
+    make_plan(asked[:, 1, :], plan)
+    to_smem = pltpu.make_async_copy(plan, route, smem_sems.at[1])
+    to_smem.start()
+    to_smem.wait()
+
+    for k in range(LINKS):
+
+        @pl.loop(0, ROOM[k])
+        def _(s):
+            link_out[BASE[k] + s] = tile_for(route[k, s], 1)
+
+        link(k).start()
+
+    @pl.loop(1, 64)
+    def _(turn):
+        step = wide_step(turn)
+        to = neighbour(step)
+        stage[to, 0] = tile_for(to, 0)
+        first(step).start()
+
+    arrived[me, 0] = tile_for(me, 0)
+
+    for k in range(LINKS):
+        link(k).wait()
+
+    @pl.loop(1, 64)
+    def _(turn):
+        step = wide_step(turn)
+        to = neighbour(step)
+        stage[to, 1] = second_for(to)
+        second(step).start()
+
+    arrived[me, 1] = second_for(me)
+
+    @pl.loop(1, peers)
+    def _(step):
+        first(step).wait()
+
+    @pl.loop(1, 64)
+    def _(turn):
+        second(wide_step(turn)).wait()
+
+    for b in range(blocks):
+
+        @pl.loop(0, kt)
+        def _(row):
+            for column in range(kt):
+                slot = table[b, row * kt + column]
+                slot = jnp.where(
+                    slot >= 4 * peers, route[AT_LOC, inside(slot - 4 * peers, peers)], slot
+                )
+                slot = inside(slot, 2 * peers + 1)
+                dense[
+                    pl.ds(pl.multiple_of(row * tile, tile), tile),
+                    column * tile : (column + 1) * tile,
+                ] = arrived[slot // 2, lax.rem(slot, 2)]
+
+        chi = basis[b * rows : (b + 1) * rows, :]
+        mixed = jnp.dot(chi, dense[...], preferred_element_type=jnp.float32)
+        both = mixed * chi.astype(jnp.float32)
+        part = both[:, :tile]
+        for m in range(1, kt):
+            part = part + both[:, m * tile : (m + 1) * tile]
+        raw[b : b + 1, :] = jnp.sum(part.T, axis=0, keepdims=True)
+
+    @pl.loop(1, peers)
+    def _(step):
+        tell(step).start()
+
+    raw_all[me] = raw[...]
+
+    @pl.loop(1, peers)
+    def _(step):
+        tell(step).wait()
+
+
+def fetch_and_density(asking, table, tiles, basis):
+    peers = asking.shape[0]
+    blocks = table.shape[0]
+    tile = tiles.shape[1]
+    rows = basis.shape[0] // blocks
+    orbs = basis.shape[1]
+    smem = pl.BlockSpec(memory_space=pltpu.SMEM)
+    vmem = pl.BlockSpec(memory_space=pltpu.VMEM)
+    pair = pltpu.SemaphoreType.DMA((peers,))
+    return pl.pallas_call(
+        fetch_kernel,
+        in_specs=[vmem, smem, vmem, vmem],
+        out_specs=[vmem, vmem, vmem],
+        out_shape=[
+            jax.ShapeDtypeStruct(asking.shape, asking.dtype),
+            jax.ShapeDtypeStruct((PLAN_ROWS, peers), jnp.int32),
+            jax.ShapeDtypeStruct((peers, blocks, rows), jnp.float32),
+        ],
+        scratch_shapes=[
+            pltpu.SMEM(asking.shape, asking.dtype),
+            pltpu.SMEM((PLAN_ROWS, peers), jnp.int32),
+            pltpu.VMEM((peers, 2, tile, tile), tiles.dtype),
+            pltpu.VMEM((peers + 1, 2, tile, tile), tiles.dtype),
+            pltpu.VMEM((RELAYED, tile, tile), tiles.dtype),
+            pltpu.VMEM((RELAYED, tile, tile), tiles.dtype),
+            pltpu.VMEM((orbs, orbs), basis.dtype),
+            pltpu.VMEM((blocks, rows), jnp.float32),
+            pltpu.SemaphoreType.DMA((2,)),
+            pair,
+            pair,
+            pair,
+            pair,
+            pair,
+            pair,
+            pltpu.SemaphoreType.DMA((LINKS,)),
+            pltpu.SemaphoreType.DMA((LINKS,)),
+            pair,
+            pair,
+        ],
+        compiler_params=params(collective_id=0, has_side_effects=True),
+        name="fetch_and_density",
+    )(asking, table, tiles, basis)
+
+
+def field_only_kernel(kept, counts, first, raw, source, field, factor, feats, column):
+    blocks, rows = field.shape
+    weights = source[:, 0]
+    density, omega, kappa = point_features(raw[...], source[:, 1])
+    feats[0] = weights * density
+    feats[1] = omega
+    feats[2] = kappa
+    for axis in range(3):
+        feats[3 + axis] = source[:, 2 + axis]
+
+    for b in range(blocks):
+        at = first[0] + b
+        for f in range(5):
+            row = feats[1 + f, pl.ds(at, 1), :]
+            column[f] = jnp.broadcast_to(row, (rows, rows)).T
+
+        def one_source(j, total):
+            s = kept[b, j]
+            r2 = None
+            for axis in range(3):
+                gap = column[2 + axis] - feats[3 + axis, pl.ds(s, 1), :]
+                r2 = gap * gap if r2 is None else r2 + gap * gap
+            g = column[0] * r2 + column[1]
+            h = feats[1, pl.ds(s, 1), :] * r2 + feats[2, pl.ds(s, 1), :]
+            phi = -1.5 / (g * h * (g + h))
+            return total + phi * feats[0, pl.ds(s, 1), :]
+
+        total = lax.fori_loop(0, counts[b], one_source, jnp.zeros((rows, rows), jnp.float32))
+        wide = jnp.broadcast_to(jnp.sum(total, axis=1, keepdims=True), (rows, rows))
+        field[b : b + 1, :] = wide.T[0:1, :]
+        weight = jnp.broadcast_to(source[pl.ds(at, 1), 0], (rows, rows)).T
+        factor[b * rows : (b + 1) * rows, :] = weight * wide
+
+
+def field_only(kept, counts, first, raw, source, blocks):
+    total, rows = raw.shape
+    smem = pl.BlockSpec(memory_space=pltpu.SMEM)
+    vmem = pl.BlockSpec(memory_space=pltpu.VMEM)
+    return pl.pallas_call(
+        field_only_kernel,
+        in_specs=[smem] * 3 + [vmem] * 2,
+        out_specs=[vmem, vmem],
+        out_shape=[
+            jax.ShapeDtypeStruct((blocks, rows), jnp.float32),
+            jax.ShapeDtypeStruct((blocks * rows, rows), jnp.float32),
+        ],
+        scratch_shapes=[
+            pltpu.VMEM((6, total, rows), jnp.float32),
+            pltpu.VMEM((5, rows, rows), jnp.float32),
+        ],
+        compiler_params=params(),
+        name="field_only",
+    )(kept, counts, first, raw, source)
+
+
+def return_kernel(
+    route,
+    mine,
+    factor,
+    basis,
+    land,
+    seconds,
+    products,
+    stage,
+    link_out,
+    scaled,
+    own_sems,
+    first_send,
+    first_recv,
+    second_send,
+    second_recv,
+    link_send,
+    link_recv,
+):
+    peers = mine.shape[0] // 2
+    tile = land.shape[1]
+    kt = basis.shape[1] // tile
+    rows = tile
+    blocks = basis.shape[0] // rows
+    me = this_device()
+
+    def first(step):
+        to = neighbour(step)
+        return remote(stage.at[to, 0], land.at[me], first_send, first_recv, step, to)
+
+    def second(step):
+        to = neighbour(step)
+        return remote(stage.at[to, 1], seconds.at[me], second_send, second_recv, step, to)
+
+    def link(k):
+        return remote(
+            link_out.at[pl.ds(BASE[k], ROOM[k])],
+            land.at[pl.ds(2 * peers + BASE[k], ROOM[k])],
+            link_send,
+            link_recv,
+            k,
+            moved(me, back(STEPS[k])),
+        )
+
+    def product_for(at):
+        return products[inside(mine[at], 2 * peers)]
+
+    def second_for(device):
+        via = route[AT_SRC, device]
+        holder = inside(jnp.where(via > 0, via - 1, device), peers)
+        return product_for(2 * holder + 1)
+
+    greet_all(peers)
+
+    @pl.loop(0, blocks)
+    def _(b):
+        chi = basis[pl.ds(pl.multiple_of(b * rows, rows), rows), :]
+        by = factor[pl.ds(pl.multiple_of(b * rows, rows), rows), :]
+        for m in range(kt):
+            part = chi[:, m * tile : (m + 1) * tile].astype(jnp.float32) * by
+            scaled[...] = part.astype(jnp.bfloat16).T
+            product = jnp.dot(scaled[...], chi, preferred_element_type=jnp.float32)
+            for n in range(kt):
+                products[b * kt * kt + m * kt + n] = product[
+                    :, n * tile : (n + 1) * tile
+                ].astype(jnp.bfloat16)
+
+    wait_all(peers)
+
+    @pl.loop(1, 64)
+    def _(turn):
+        step = wide_step(turn)
+        to = neighbour(step)
+        stage[to, 1] = second_for(to)
+        second(step).start()
+
+    seconds[me] = second_for(me)
+    stage[me, 0] = product_for(2 * me)
+    own = pltpu.make_async_copy(stage.at[me, 0], land.at[me], own_sems.at[0])
+    own.start()
+
+    @pl.loop(0, 64)
+    def _(turn):
+        step = narrow_step(turn)
+        to = neighbour(step)
+        stage[to, 0] = product_for(2 * to)
+        first(step).start()
+
+    @pl.loop(1, 64)
+    def _(turn):
+        second(wide_step(turn)).wait()
+
+    for k in range(LINKS):
+
+        @pl.loop(0, ROOM[k])
+        def _(s):
+            link_out[BASE[k] + s] = seconds[inside(route[LINKS + k, s], peers)]
+
+        link(k).start()
+
+    keep = pltpu.make_async_copy(seconds, land.at[pl.ds(peers, peers)], own_sems.at[1])
+    keep.start()
+
+    @pl.loop(1, 64)
+    def _(turn):
+        step = wide_step(turn)
+        to = neighbour(step)
+        stage[to, 0] = product_for(2 * to)
+        first(step).start()
+
+    for k in range(LINKS):
+        link(k).wait()
+
+    @pl.loop(1, peers)
+    def _(step):
+        first(step).wait()
+
+    own.wait()
+    keep.wait()
+
+
+def return_tiles(plan, mine, factor, basis, peers):
+    tile = 128
+    smem = pl.BlockSpec(memory_space=pltpu.SMEM)
+    vmem = pl.BlockSpec(memory_space=pltpu.VMEM)
+    pair = pltpu.SemaphoreType.DMA((peers,))
+    return pl.pallas_call(
+        return_kernel,
+        in_specs=[smem, smem, vmem, vmem],
+        out_specs=pl.BlockSpec(memory_space=pl.ANY),
+        out_shape=jax.ShapeDtypeStruct((2 * peers + RELAYED, tile, tile), jnp.bfloat16),
+        scratch_shapes=[
+            pltpu.VMEM((peers, tile, tile), jnp.bfloat16),
+            pltpu.VMEM((mine.shape[0], tile, tile), jnp.bfloat16),
+            pltpu.VMEM((peers, 2, tile, tile), jnp.bfloat16),
+            pltpu.VMEM((RELAYED, tile, tile), jnp.bfloat16),
+            pltpu.VMEM((tile, tile), jnp.bfloat16),
+            pltpu.SemaphoreType.DMA((2,)),
+            pair,
+            pair,
+            pair,
+            pair,
+            pltpu.SemaphoreType.DMA((LINKS,)),
+            pltpu.SemaphoreType.DMA((LINKS,)),
+        ],
+        compiler_params=params(collective_id=1, has_side_effects=True),
+        name="return_tiles",
+    )(plan, mine, factor, basis)
 
 
 def pick_kernel(asked, tiles, out):
@@ -252,12 +814,12 @@
     )
 
 
-def slot_order(asked, store_count):
+def slot_order(asked, positions, store_count):
     count = asked.shape[0]
     places = jnp.arange(count, dtype=jnp.int32)
     key = jnp.where(asked >= 0, asked, store_count) * count + places
     rank = jnp.sum((key[None, :] < key[:, None]).astype(jnp.int32), axis=1)
-    order = jnp.sum(jnp.where(rank[:, None] == places[None, :], places[:, None], 0), axis=0)
+    order = jnp.sum(jnp.where(rank[:, None] == places[None, :], positions[:, None], 0), axis=0)
     stores = jnp.arange(store_count + 1, dtype=jnp.int32)
     starts = jnp.sum(
         ((asked[None, :] >= 0) & (asked[None, :] < stores[:, None])).astype(jnp.int32), axis=1
@@ -266,13 +828,14 @@
 
 
 def body(basis, dmat, tile_home, pair_tiles, pair_pos, coords, weights, grad_sq, pair_keep):
-    peer_count = lax.axis_size(AXES)
+    peers = lax.axis_size(AXES)
     me = lax.axis_index(AXES)
     blocks, pairs = pair_tiles.shape
     store_count, tile = dmat.shape[0], dmat.shape[1]
     rows = basis.shape[0] // blocks
+    kt = basis.shape[1] // tile
     capacity = 2
-    slot_count = peer_count * capacity
+    slot_count = peers * capacity
     wanted = tile_home[pair_tiles.reshape(-1)]
     owner = wanted // store_count
     within = wanted % store_count
@@ -280,43 +843,76 @@
     places = jnp.arange(blocks * pairs, dtype=jnp.int32)
     earlier = jnp.sum((same & (places[None, :] < places[:, None])).astype(jnp.int32), axis=1)
     slots = owner * capacity + earlier
-    slot_places = jnp.arange(slot_count, dtype=jnp.int32)
-    asking = (
-        jnp.sum(jnp.where(slots[:, None] == slot_places[None, :], within[:, None] + 1, 0), axis=0) - 1
+    devices = jnp.arange(peers, dtype=jnp.int32)
+    lanes = jnp.arange(tile, dtype=jnp.int32)
+    held = owner[:, None] == devices[None, :]
+    entry = jnp.where(
+        held[:, :, None] & (earlier[:, None] == lanes[None, :])[:, None, :],
+        within[:, None, None] + 1,
+        0,
     )
-    asked = lax.all_to_all(
-        asking.reshape(peer_count, capacity), AXES, split_axis=0, concat_axis=0, tiled=True
-    ).reshape(-1)
-
-    arrived = lax.all_to_all(
-        pick_tiles(asked, dmat).reshape(peer_count, capacity, tile, tile),
-        AXES,
-        split_axis=0,
-        concat_axis=0,
-        tiled=True,
-    ).reshape(slot_count, tile, tile)
-
-    mine = jnp.concatenate([weights[None], grad_sq[None], coords], axis=0)
-    mine = mine.reshape(5, blocks, rows).transpose(1, 0, 2)
-    source = lax.all_gather(mine, AXES, axis=0, tiled=True)
+    named = jnp.sum(held.astype(jnp.int32), axis=0)
+    asking = jnp.stack(
+        [jnp.sum(entry, axis=0), jnp.broadcast_to(named[None, :], (peers, tile))], axis=1
+    )
+    even_me = parity(me.astype(jnp.int32))
+    relayed = (earlier == 1) & (parity(owner) != even_me)
+    spot = pair_pos[:, :, None] == jnp.arange(kt * kt, dtype=jnp.int32)[None, None, :]
+    found = jnp.where(relayed, 2 * slot_count + owner, slots).reshape(blocks, pairs)
+    table = (
+        jnp.sum(jnp.where(spot, found[:, :, None] - slot_count, 0), axis=1) + slot_count
+    )
+    product_at = pair_pos + kt * kt * jnp.arange(blocks, dtype=jnp.int32)[:, None]
+    mine = jnp.sum(
+        jnp.where(
+            slots[:, None] == jnp.arange(slot_count, dtype=jnp.int32)[None, :],
+            product_at.reshape(-1)[:, None],
+            0,
+        ),
+        axis=0,
+    )
+
+    local = jnp.concatenate([weights[None], grad_sq[None], coords], axis=0)
+    local = local.reshape(5, blocks, rows).transpose(1, 0, 2)
+    source = lax.all_gather(local, AXES, axis=0, tiled=True)
     keep = lax.dynamic_slice_in_dim(pair_keep, me * blocks, blocks, 0)
     kept, counts = kept_list(keep)
-    order, starts = slot_order(asked, store_count)
-
-    raw = block_density(slots, pair_pos, basis, arrived)
-    raw = lax.all_gather(raw, AXES, axis=0, tiled=True)
     first = (me * blocks).astype(jnp.int32).reshape(1)
-    field, returning = field_and_tiles(
-        kept, counts, slots, pair_pos, first, raw, source, basis, slot_count
-    )
-    landed = lax.all_to_all(
-        returning.reshape(peer_count, capacity, tile, tile),
-        AXES,
-        split_axis=0,
-        concat_axis=0,
-        tiled=True,
-    ).reshape(slot_count, tile, tile)
-    return collect_tiles(order, starts, landed, store_count), field.reshape(-1)
+
+    asked, plan, raw = fetch_and_density(asking, table, dmat, basis)
+    raw = raw.reshape(peers * blocks, rows)
+    asked = asked[:, 0, :capacity].reshape(-1) - 1
+
+    def two_slots():
+        shape = (peers, capacity, tile, tile)
+
+        def exchange(values):
+            return lax.all_to_all(
+                values.reshape(shape), AXES, split_axis=0, concat_axis=0, tiled=True
+            ).reshape(slot_count, tile, tile)
+
+        arrived = exchange(pick_tiles(asked, dmat))
+        again = block_density(slots, pair_pos, basis, arrived)
+        again = lax.all_gather(again, AXES, axis=0, tiled=True)
+        field, returning = field_and_tiles(
+            kept, counts, slots, pair_pos, first, again, source, basis, slot_count
+        )
+        order, starts = slot_order(
+            asked, jnp.arange(slot_count, dtype=jnp.int32), store_count
+        )
+        return collect_tiles(order, starts, exchange(returning), store_count), field
+
+    def relays():
+        field, factor = field_only(kept, counts, first, raw, source, blocks)
+        wide = parity(devices) == even_me
+        seconds = jnp.where(wide, peers + devices, 2 * peers + plan[AT_BACK])
+        places = jnp.stack([devices, seconds], axis=1).reshape(-1)
+        order, starts = slot_order(asked, places, store_count)
+        land = return_tiles(plan, mine, factor, basis, peers)
+        return collect_tiles(order, starts, land, store_count), field
+
+    pieces, field = lax.cond(jnp.sum(plan[AT_LEFT]) > 0, two_slots, relays)
+    return pieces, field.reshape(-1)
 
 
 def solution(mesh):

time: 349 us -> 278 us (0.80)
  waiting for transfers between devices: 195 us -> 0.04 us
  Pallas kernels: 50.8 us -> 243 us
  blocking collectives: 63.2 us -> 0 us
  starting transfers between devices: 12.2 us -> 0.04 us
  other arithmetic: 7.86 us -> 14.4 us
    all_to_all x2 -> x0, waiting for transfers between devices: 195 us -> none  [the longest x1 99.1 us: body(): lax.all_to_all(returning.reshape(peer_count, capacity, tile, tile), AXES,...]
    pallas_call x3, Pallas kernels: 42.6 us -> 236 us  [the longest x1 138 us: fetch_and_density(): pl.pallas_call(fetch_kernel, in_specs=[vmem, smem, vmem, vmem], out_specs...]
    all_gather x1 -> x0, blocking collectives: 42.5 us -> none  [body(): raw = lax.all_gather(raw, AXES, axis=0, tiled=True)]
    all_to_all x1 -> x0, blocking collectives: 20.7 us -> none  [body(): lax.all_to_all(asking.reshape(peer_count, capacity), AXES, split_axis=0,...]
    all_to_all x2 -> x0, starting transfers between devices: 12.1 us -> none  [the longest x1 6.15 us: body(): lax.all_to_all(returning.reshape(peer_count, capacity, tile, tile), AXES,...]
    reduce_sum x2 -> x5, other arithmetic: 0.82 us -> 5.75 us  [the longest x1 2.92 us: body(): jnp.sum(entry, axis=0)]
  transfers between devices with their start and end apart: 3 -> 1, of which waited for: 2 -> 0; matrix products, arithmetic and copies ran while one was open for 2% -> 5% of each run, Pallas kernels for 2% -> 50%
where the time goes in v3:
time: 278 us
  Pallas kernels  243 us (87%)
  between operations  14.9 us (5%)
  other arithmetic  14.4 us (5%)
  local copies, waits for them, and re-layouts  4.88 us (2%)
    pallas_call x1, Pallas kernels, fetch_and_density(): pl.pallas_call(fetch_kernel, in_specs=[vmem, smem, vmem, vmem], out_specs...  138 us
    pallas_call x1, Pallas kernels, return_tiles(): pl.pallas_call(return_kernel, in_specs=[smem, smem, vmem, vmem], out_spec...  92.2 us
    pallas_call x1, Pallas kernels, collect_tiles(): pl.pallas_call(collect_kernel, grid=(store_count // group,), in_specs=[sm...  6.82 us
    pallas_call x1, Pallas kernels, field_only(): pl.pallas_call(field_only_kernel, in_specs=[smem] * 3 + [vmem] * 2, out_s...  5.84 us
  transfers between devices with their start and end apart: 1, of which 0 were waited for; matrix products, arithmetic and copies ran while one was open for 5% of the time, Pallas kernels for 50%

profile of v3, /device:TPU:1, one launch (start us, length us, event | category | flops | bytes accessed | tf_op | source)
XLA Modules:
  0.0 277.7 jit_solution(5716014460251201709)
XLA Ops:
  7.3 1.5 maximum_bitcast_fusion
  8.8 0.8 reshape.300
  9.6 1.1 gather_fusion
  11.2 0.8 select_reduce_fusion.5
  12.1 2.9 %select_reduce_fusion.3 = s32[128,128]{1,0:T(8,128)S(1)} fusion(s32[128]{0:T(128)S(1)} %get-tuple-element.195, pred[128,128]{1,0:T(8,128)(4,1)S(1)} %get-tuple-element.198, pred[128,128]{1,0:T(8,128)(4,1)S(1)} %get-tuple-element.199), kind=kLoop, calls=%fused_computation.47 | loop fusion | flops 6275072 | bytes 98816 | tf_op jit(solution)/shard_map/reduce_sum | solution.py:856
  15.0 0.8 pad_add_fusion.1.asking
  15.8 0.6 broadcast_add_fusion.1.table
  16.4 138.1 %fetch_and_density.1 = (s32[128,2,128]{2,1,0:T(2,128)}, s32[40,128]{1,0:T(8,128)S(1)}, f32[128,4,128]{2,1,0:T(4,128)}) custom-call(s32[128,2,128]{2,1,0:T(2,128)} %pad_add_fusion.1.asking, s32[4,64]{1,0:T(4,128)} %broadcast_add_fusion.1.table, bf16[64,128,128]{2,1,0:T(8,128)(2,1)} %tiles.1, bf16[512,1024]{1,0:T(8,128)(2,1)} %basis.1), custom_call_target="tpu_custom_call" | custom-call | tf_op jit(solution)/shard_map/fetch_and_density/pallas_call | solution.py:351
  154.5 1.1 add_reduce_fusion
  155.7 0.8 fusion.21
  156.6 1.2 reduce-window.6
  157.8 0.2 slice_reduce_fusion
  158.0 0.2 reduce-window.9
  158.2 0.6 slice_reduce_fusion.1
  159.6 1.1 select_reduce_fusion.4
  160.8 108.0 %conditional.1 = (f32[64,128,128]{2,1,0:T(8,128)S(1)}, f32[4,128]{1,0:T(4,128)}) conditional(s32[]{:T(128)} %convert_element_type.23, (s32[256]{0:T(256)S(1)}, s32[128]{0:T(128)S(1)}, s32[128]{0:T(128)S(1)}, s32[]{:T(128)}, s32[128]{0:T(128)S(1)}, /*index=5*/s32[40,128]{1,0:T(8,128)S(1)}, s32[128,1]{0,1:T(1,128)S(1)}, s32[128,1]{0,1:T(1,128)S(1)}, ...), branch_computations={%region_9.14_spmd, %region_14.18_spmd} | conditional | flops 567875 | bytes 55850992 | solution.py:914
  161.0 0.7 convert_reduce_fusion.1.starts
  161.7 0.2 convert_reduce_fusion
  162.2 0.7 select_reduce_fusion.order
  162.9 5.8 %field_only.1 = (f32[4,128]{1,0:T(4,128)}, f32[512,128]{1,0:T(8,128)}) custom-call(s32[4,512]{1,0:T(4,128)S(1)} %get-tuple-element.145.kept, s32[4]{0:T(128)S(1)} %get-tuple-element.146.counts, s32[1]{0:T(128)} %get-tuple-element.147.first, f32[512,128]{1,0:T(8,128)} %bitcast.41, f32[512,5,128]{2,1,0:T(8,128)} %get-tuple-element.149.source), custom_call_target="tpu_custom_call" | custom-call | tf_op jit(solution)/shard_map/cond/branch_0_fun/field_only/pallas_call | solution.py:424
  168.9 0.7 select_reduce_fusion.1.mine
  169.6 92.2 %return_tiles.1.landed = bf16[357,128,128]{2,1,0:T(8,128)(2,1)} custom-call(s32[40,128]{1,0:T(8,128)S(1)} %get-tuple-element.136.route, s32[256]{0:T(256)} %select_reduce_fusion.1.mine, f32[512,128]{1,0:T(8,128)} %get-tuple-element.150.factor, bf16[512,1024]{1,0:T(8,128)(2,1)S(1)} %get-tuple-element.151.basis), custom_call_target="tpu_custom_call" | custom-call | tf_op jit(solution)/shard_map/cond/branch_0_fun/return_tiles/pallas_call | solution.py:567
  261.8 6.8 %collect_tiles.2 = f32[64,128,128]{2,1,0:T(8,128)S(1)} custom-call(s32[256]{0:T(256)} %select_reduce_fusion.order, s32[65]{0:T(128)} %convert_reduce_fusion.1.starts, bf16[357,128,128]{2,1,0:T(8,128)(2,1)} %return_tiles.1.landed), custom_call_target="tpu_custom_call" | custom-call | tf_op jit(solution)/shard_map/cond/branch_0_fun/collect_tiles/pallas_call | solution.py:795
  268.8 2.0 copy-done.4
  (41 shorter events, 1.4 us)
Async XLA Ops:
  7.2 2.4 copy-start
  7.2 153.6 %copy-start.5 = (s32[4,32]{1,0:T(4,128)S(1)}, s32[4,32]{1,0:T(4,128)}, u32[]{:S(2)}) copy-start(s32[4,32]{1,0:T(4,128)} %param.15) | copy-start | bytes 1540
  7.2 153.6 %copy-start.1 = (bf16[512,1024]{1,0:T(8,128)(2,1)S(1)}, bf16[512,1024]{1,0:T(8,128)(2,1)}, u32[]{:S(2)}) copy-start(bf16[512,1024]{1,0:T(8,128)(2,1)} %basis.1) | copy-start | bytes 3145732
  7.2 153.6 %copy-start.3 = (bf16[64,128,128]{2,1,0:T(8,128)(2,1)S(1)}, bf16[64,128,128]{2,1,0:T(8,128)(2,1)}, u32[]{:S(2)}) copy-start(bf16[64,128,128]{2,1,0:T(8,128)(2,1)} %tiles.1) | copy-start | bytes 6291460
  7.2 153.5 %all-gather.3.cloned.1.call-start = ((), (), s32[]{:S(2)}) async-start(), calls=%async_computation.2 | async-start | bytes 2113536 | tf_op jit(solution)/shard_map/all_gather | solution.py:877
  268.8 2.0 copy-start.4
Sparse Core Ops, SparseCore 0:
  11.2 115.7 all-gather.2

commit v4 on v3

--- a/solution.py
+++ b/solution.py
@@ -36,8 +36,11 @@
 BASE = tuple(sum(ROOM[:k]) for k in range(len(ROOM)))
 LINKS = len(ROOM)
 RELAYED = sum(ROOM)
-PLAN_ROWS = 2 * LINKS + 8
-AT_LOC, AT_SRC, AT_CODE, AT_BACK, AT_LEFT = range(2 * LINKS, 2 * LINKS + 5)
+AT_LOC, AT_SRC, AT_CODE, AT_LEFT, AT_STARTS = range(2 * LINKS, 2 * LINKS + 5)
+AT_TABLE, AT_MINE, AT_ORDER = 2 * LINKS + 5, 2 * LINKS + 7, 2 * LINKS + 9
+AT_KEPT = 2 * LINKS + 11
+AT_COUNTS = AT_KEPT + 16
+PLAN_ROWS = AT_COUNTS + 5
 
 
 def point_features(raw_density, grad_sq):
@@ -93,6 +96,124 @@
 def wide_step(turn):
     up = lax.rem(turn * STRIDE, 64)
     return 2 * up + lax.rem(up + up // 4 + up // 16, 2)
+
+
+def iotas(peers):
+    return (
+        lax.broadcasted_iota(jnp.int32, (peers, peers), 0).astype(jnp.float32),
+        lax.broadcasted_iota(jnp.int32, (peers, peers), 1).astype(jnp.float32),
+    )
+
+
+def down(row, peers):
+    sub, lane = iotas(peers)
+    return jnp.sum(jnp.where(sub == lane, row, 0.0), axis=1, keepdims=True)
+
+
+def across(hit, column):
+    return jnp.sum(jnp.where(hit, column, 0.0), axis=0, keepdims=True)
+
+
+def make_requests(want, asking):
+    peers = want.shape[1]
+    sub, lane = iotas(peers)
+    owner_int = want[...] // 64
+    owner = owner_int.astype(jnp.float32)
+    within = (want[...] - owner_int * 64).astype(jnp.float32)
+    owner_down = down(owner, peers)
+    same = owner_down == owner
+    rank = across(same & (sub < lane), jnp.ones_like(owner_down))
+    columns = [
+        jnp.sum(
+            jnp.where((owner == sub) & (rank == slot), within + 1.0, 0.0), axis=1, keepdims=True
+        )
+        for slot in range(2)
+    ]
+    entries = jnp.where(lane == 0.0, columns[0], jnp.where(lane == 1.0, columns[1], 0.0))
+    named = across(owner_down == lane, jnp.ones_like(owner_down))
+    asking[:, 0, :] = entries.astype(jnp.int32)
+    asking[:, 1, :] = jnp.broadcast_to(named, (peers, peers)).astype(jnp.int32)
+
+
+def make_tables(want, spots, plan):
+    peers = want.shape[1]
+    sub, lane = iotas(peers)
+    me = this_device()
+    owner_int = want[...] // 64
+    owner = owner_int.astype(jnp.float32)
+    owner_down = down(owner, peers)
+    rank = across((owner_down == owner) & (sub < lane), jnp.ones_like(owner_down))
+    odd = parity(owner_int) != parity(me)
+    found = jnp.where((rank == 1.0) & odd, 4.0 * peers + owner, 2.0 * owner + rank)
+    pair = lax.broadcasted_iota(jnp.int32, (1, peers), 1)
+    spot = (spots[...] + 64 * (pair // 32)).astype(jnp.float32)
+    rank_down, found_down, spot_down = down(rank, peers), down(found, peers), down(spot, peers)
+    for half in range(2):
+        row = across(spot_down == lane + half * peers, found_down - 2.0 * peers) + 2.0 * peers
+        plan[AT_TABLE + half : AT_TABLE + half + 1, :] = row.astype(jnp.int32)
+        row = across((owner_down == lane) & (rank_down == half), spot_down)
+        plan[AT_MINE + half : AT_MINE + half + 1, :] = row.astype(jnp.int32)
+
+
+def make_order(entries, again, plan):
+    peers = entries.shape[0]
+    sub, lane = iotas(peers)
+    me = this_device()
+    asker = lax.broadcasted_iota(jnp.int32, (peers, 1), 0)
+    wide = parity(asker) == parity(me)
+    number = asker.astype(jnp.float32)
+    asked = [
+        jnp.sum(jnp.where(lane == slot, entries, 0.0), axis=1, keepdims=True) for slot in range(2)
+    ]
+    places = [number, jnp.where(wide, number + peers, again + 2.0 * peers)]
+    keys = [
+        jnp.where(asked[slot] > 0.0, asked[slot] - 1.0, 64.0) * (2.0 * peers) + 2.0 * number + slot
+        for slot in range(2)
+    ]
+    rows = [across(sub == lane, key) for key in keys]
+    ranks = [
+        sum(
+            jnp.sum(jnp.where(row < key, 1.0, 0.0), axis=1, keepdims=True) for row in rows
+        )
+        for key in keys
+    ]
+    for half in range(2):
+        row = sum(
+            across(ranks[slot] == lane + half * peers, places[slot]) for slot in range(2)
+        )
+        plan[AT_ORDER + half : AT_ORDER + half + 1, :] = row.astype(jnp.int32)
+    row = sum(
+        across((asked[slot] > 0.0) & (asked[slot] - 1.0 < lane), jnp.ones_like(number))
+        for slot in range(2)
+    )
+    plan[AT_STARTS : AT_STARTS + 1, :] = row.astype(jnp.int32)
+
+
+def make_kept(keep, plan):
+    blocks = keep.shape[0]
+    peers = 128
+    sub, lane = iotas(peers)
+    parts = keep.shape[1] // peers
+    for b in range(blocks):
+        before = jnp.zeros((1, 1), jnp.float32)
+        ranks = []
+        for g in range(parts):
+            row = keep[b : b + 1, g * peers : (g + 1) * peers]
+            rank = jnp.sum(jnp.where(lane < sub, row, 0.0), axis=1, keepdims=True) + before
+            ranks.append(jnp.where(down(row, peers) > 0.0, rank, -1.0))
+            before = before + jnp.sum(row, axis=1, keepdims=True)
+        for h in range(parts):
+            total = jnp.zeros((1, peers), jnp.float32)
+            for g in range(parts):
+                block = lax.broadcasted_iota(jnp.int32, (peers, 1), 0) + g * peers
+                device = block // 4
+                place = ((device % 2) * 64 + device // 2) * 4 + block % 4
+                total = total + across(ranks[g] == lane + h * peers, place.astype(jnp.float32))
+            at = AT_KEPT + parts * b + h
+            plan[at : at + 1, :] = total.astype(jnp.int32)
+        plan[AT_COUNTS + b : AT_COUNTS + b + 1, :] = jnp.broadcast_to(before, (1, peers)).astype(
+            jnp.int32
+        )
 
 
 def greet_all(peers):
@@ -169,28 +290,39 @@
     plan[AT_LOC : AT_LOC + 1, :] = row_of(loc).astype(jnp.int32)
     plan[AT_SRC : AT_SRC + 1, :] = row_of(src).astype(jnp.int32)
     plan[AT_CODE : AT_CODE + 1, :] = turned(code).astype(jnp.int32)
-    plan[AT_BACK : AT_BACK + 1, :] = turned(again).astype(jnp.int32)
-    plan[AT_LEFT : AT_LEFT + 1, :] = jnp.sum(left, axis=0, keepdims=True).astype(jnp.int32)
-    plan[AT_LEFT + 1 :, :] = jnp.zeros((PLAN_ROWS - AT_LEFT - 1, peers), jnp.int32)
+    unplaced = jnp.sum(jnp.sum(left, axis=1, keepdims=True), axis=0, keepdims=True)
+    plan[AT_LEFT : AT_LEFT + 1, :] = jnp.broadcast_to(unplaced, (1, peers)).astype(jnp.int32)
+    plan[AT_COUNTS + 4 :, :] = jnp.zeros((PLAN_ROWS - AT_COUNTS - 4, peers), jnp.int32)
+    return mine(again)
 
 
 def fetch_kernel(
-    asking,
-    table,
+    home,
+    pair_tiles,
+    spots,
+    pair_keep,
+    weights,
+    grad_sq,
+    coords,
     tiles,
     basis,
     asked,
     plan,
     raw_all,
+    source_all,
     wanted,
     route,
+    want_smem,
+    want,
+    asking,
+    keep,
+    local,
     stage,
     arrived,
     link_out,
     link_in,
     dense,
-    raw,
-    smem_sems,
+    own_sems,
     ask_send,
     ask_recv,
     first_send,
@@ -199,16 +331,21 @@
     second_recv,
     link_send,
     link_recv,
+    share_send,
+    share_recv,
     raw_send,
     raw_recv,
 ):
-    peers = asking.shape[0]
-    blocks = table.shape[0]
+    peers = asked.shape[0]
+    chips = peers // 2
+    blocks, pairs = pair_tiles.shape
     orbs = basis.shape[1]
     rows = basis.shape[0] // blocks
     tile = tiles.shape[1]
     kt = orbs // tile
     me = this_device()
+    chip, core = me // 2, lax.rem(me, 2)
+    partner = 2 * chip + 1 - core
 
     def ask(step):
         to = neighbour(step)
@@ -228,8 +365,21 @@
             link_out.at[part], link_in.at[part], link_send, link_recv, k, moved(me, STEPS[k])
         )
 
-    def tell(step):
-        return remote(raw, raw_all.at[me], raw_send, raw_recv, step, neighbour(step))
+    def share(up):
+        to = neighbour(2 * up)
+        return remote(local, source_all.at[:, core, chip], share_send, share_recv, up, to)
+
+    def share_on():
+        part = source_all.at[:, core]
+        return remote(part, part, share_send, share_recv, 0, partner)
+
+    def tell_partner():
+        part = raw_all.at[core, chip]
+        return remote(part, part, raw_send, raw_recv, 0, partner)
+
+    def tell(up):
+        part = raw_all.at[:, chip]
+        return remote(part, part, raw_send, raw_recv, up, neighbour(2 * up))
 
     def tile_for(device, slot):
         return tiles[inside(wanted[inside(device, peers), 0, slot] - 1, tiles.shape[0])]
@@ -238,23 +388,47 @@
         at = route[AT_CODE, device]
         return jnp.where(at > 0, link_in[inside(at - 1, RELAYED)], tile_for(device, 1))
 
+    def move(source, target, at):
+        copy = pltpu.make_async_copy(source, target, own_sems.at[at])
+        copy.start()
+        return copy
+
     greet_all(peers)
+    pair = lax.div(me, 2)
+    keep_copy = move(pair_keep.at[pl.ds(pl.multiple_of(8 * pair, 8), 8)], keep, 0)
+
+    for b in range(blocks):
+
+        @pl.loop(0, pairs)
+        def _(j):
+            want_smem[0, b * pairs + j] = home[inside(pair_tiles[b, j], home.shape[0])]
+
+    move(want_smem, want, 1).wait()
+    make_requests(want, asking)
+    local[0] = weights[...]
+    local[1] = grad_sq[...]
+    for axis in range(3):
+        for b in range(blocks):
+            local[2 + axis, b : b + 1, :] = coords[axis : axis + 1, b * rows : (b + 1) * rows]
     wait_all(peers)
 
     @pl.loop(1, peers)
     def _(step):
         ask(step).start()
 
+    @pl.loop(1, chips)
+    def _(up):
+        share(up).start()
+
     asked[me] = asking[me]
+    source_all[:, core, chip] = local[...]
     arrived[peers] = jnp.zeros(arrived.shape[1:], arrived.dtype)
 
     @pl.loop(1, peers)
     def _(step):
         ask(step).wait()
 
-    to_smem = pltpu.make_async_copy(asked, wanted, smem_sems.at[0])
-    to_smem.start()
-    to_smem.wait()
+    move(asked, wanted, 2).wait()
 
     @pl.loop(0, 64)
     def _(turn):
@@ -263,10 +437,8 @@
         stage[to, 0] = tile_for(to, 0)
         first(step).start()
 
-    make_plan(asked[:, 1, :], plan)
-    to_smem = pltpu.make_async_copy(plan, route, smem_sems.at[1])
-    to_smem.start()
-    to_smem.wait()
+    again = make_plan(asked[:, 1, :], plan)
+    move(plan, route, 3).wait()
 
     for k in range(LINKS):
 
@@ -297,6 +469,18 @@
 
     arrived[me, 1] = second_for(me)
 
+    @pl.loop(1, chips)
+    def _(up):
+        share(up).wait()
+
+    share_on().start()
+    make_tables(want, spots, plan)
+    make_order(asked[:, 0, :].astype(jnp.float32), again, plan)
+    keep_copy.wait()
+    kept = jnp.where(core == 0, keep[0:4, :], keep[4:8, :]).astype(jnp.float32)
+    make_kept(kept, plan)
+    move(plan, route, 4).wait()
+
     @pl.loop(1, peers)
     def _(step):
         first(step).wait()
@@ -310,63 +494,73 @@
         @pl.loop(0, kt)
         def _(row):
             for column in range(kt):
-                slot = table[b, row * kt + column]
+                q = b * kt * kt + row * kt + column
+                slot = route[AT_TABLE + q // peers, lax.rem(q, peers)]
                 slot = jnp.where(
                     slot >= 4 * peers, route[AT_LOC, inside(slot - 4 * peers, peers)], slot
                 )
                 slot = inside(slot, 2 * peers + 1)
                 dense[
+                    b % 2,
                     pl.ds(pl.multiple_of(row * tile, tile), tile),
                     column * tile : (column + 1) * tile,
                 ] = arrived[slot // 2, lax.rem(slot, 2)]
 
         chi = basis[b * rows : (b + 1) * rows, :]
-        mixed = jnp.dot(chi, dense[...], preferred_element_type=jnp.float32)
+        mixed = jnp.dot(chi, dense[b % 2], preferred_element_type=jnp.float32)
         both = mixed * chi.astype(jnp.float32)
         part = both[:, :tile]
         for m in range(1, kt):
             part = part + both[:, m * tile : (m + 1) * tile]
-        raw[b : b + 1, :] = jnp.sum(part.T, axis=0, keepdims=True)
-
-    @pl.loop(1, peers)
-    def _(step):
-        tell(step).start()
-
-    raw_all[me] = raw[...]
-
-    @pl.loop(1, peers)
-    def _(step):
-        tell(step).wait()
-
-
-def fetch_and_density(asking, table, tiles, basis):
-    peers = asking.shape[0]
-    blocks = table.shape[0]
+        raw_all[core, chip, b : b + 1, :] = jnp.sum(part.T, axis=0, keepdims=True)
+
+    tell_partner().start()
+    share_on().wait()
+    tell_partner().wait()
+
+    @pl.loop(1, chips)
+    def _(up):
+        tell(up).start()
+
+    @pl.loop(1, chips)
+    def _(up):
+        tell(up).wait()
+
+
+def fetch_and_density(home, pair_tiles, spots, pair_keep, weights, grad_sq, coords, tiles, basis):
+    blocks, pairs = pair_tiles.shape
     tile = tiles.shape[1]
+    peers = blocks * pairs
     rows = basis.shape[0] // blocks
     orbs = basis.shape[1]
     smem = pl.BlockSpec(memory_space=pltpu.SMEM)
     vmem = pl.BlockSpec(memory_space=pltpu.VMEM)
     pair = pltpu.SemaphoreType.DMA((peers,))
+    half = pltpu.SemaphoreType.DMA((peers // 2,))
     return pl.pallas_call(
         fetch_kernel,
-        in_specs=[vmem, smem, vmem, vmem],
-        out_specs=[vmem, vmem, vmem],
+        in_specs=[smem, smem, vmem, pl.BlockSpec(memory_space=pl.ANY)] + [vmem] * 5,
+        out_specs=[vmem, vmem, vmem, vmem],
         out_shape=[
-            jax.ShapeDtypeStruct(asking.shape, asking.dtype),
+            jax.ShapeDtypeStruct((peers, 2, peers), jnp.int32),
             jax.ShapeDtypeStruct((PLAN_ROWS, peers), jnp.int32),
-            jax.ShapeDtypeStruct((peers, blocks, rows), jnp.float32),
+            jax.ShapeDtypeStruct((2, peers // 2, blocks, rows), jnp.float32),
+            jax.ShapeDtypeStruct((5, 2, peers // 2, blocks, rows), jnp.float32),
         ],
         scratch_shapes=[
-            pltpu.SMEM(asking.shape, asking.dtype),
+            pltpu.SMEM((peers, 2, peers), jnp.int32),
             pltpu.SMEM((PLAN_ROWS, peers), jnp.int32),
+            pltpu.SMEM((1, peers), jnp.int32),
+            pltpu.VMEM((1, peers), jnp.int32),
+            pltpu.VMEM((peers, 2, peers), jnp.int32),
+            pltpu.VMEM((8, pair_keep.shape[1]), jnp.int32),
+            pltpu.VMEM((5, blocks, rows), jnp.float32),
             pltpu.VMEM((peers, 2, tile, tile), tiles.dtype),
             pltpu.VMEM((peers + 1, 2, tile, tile), tiles.dtype),
             pltpu.VMEM((RELAYED, tile, tile), tiles.dtype),
             pltpu.VMEM((RELAYED, tile, tile), tiles.dtype),
-            pltpu.VMEM((orbs, orbs), basis.dtype),
-            pltpu.VMEM((blocks, rows), jnp.float32),
-            pltpu.SemaphoreType.DMA((2,)),
+            pltpu.VMEM((2, orbs, orbs), basis.dtype),
+            pltpu.SemaphoreType.DMA((5,)),
             pair,
             pair,
             pair,
@@ -375,32 +569,36 @@
             pair,
             pltpu.SemaphoreType.DMA((LINKS,)),
             pltpu.SemaphoreType.DMA((LINKS,)),
-            pair,
-            pair,
+            half,
+            half,
+            half,
+            half,
         ],
         compiler_params=params(collective_id=0, has_side_effects=True),
         name="fetch_and_density",
-    )(asking, table, tiles, basis)
-
-
-def field_only_kernel(kept, counts, first, raw, source, field, factor, feats, column):
+    )(home, pair_tiles, spots, pair_keep, weights, grad_sq, coords, tiles, basis)
+
+
+def field_only_kernel(plan, raw, source, field, factor, feats, column):
     blocks, rows = field.shape
-    weights = source[:, 0]
-    density, omega, kappa = point_features(raw[...], source[:, 1])
+    me = this_device()
+    start = (lax.rem(me, 2) * 64 + me // 2) * blocks
+    weights = source[0]
+    density, omega, kappa = point_features(raw[...], source[1])
     feats[0] = weights * density
     feats[1] = omega
     feats[2] = kappa
     for axis in range(3):
-        feats[3 + axis] = source[:, 2 + axis]
+        feats[3 + axis] = source[2 + axis]
 
     for b in range(blocks):
-        at = first[0] + b
+        at = start + b
         for f in range(5):
             row = feats[1 + f, pl.ds(at, 1), :]
             column[f] = jnp.broadcast_to(row, (rows, rows)).T
 
         def one_source(j, total):
-            s = kept[b, j]
+            s = plan[AT_KEPT + 4 * b + j // rows, lax.rem(j, rows)]
             r2 = None
             for axis in range(3):
                 gap = column[2 + axis] - feats[3 + axis, pl.ds(s, 1), :]
@@ -410,20 +608,20 @@
             phi = -1.5 / (g * h * (g + h))
             return total + phi * feats[0, pl.ds(s, 1), :]
 
-        total = lax.fori_loop(0, counts[b], one_source, jnp.zeros((rows, rows), jnp.float32))
+        total = lax.fori_loop(0, plan[AT_COUNTS + b, 0], one_source, jnp.zeros((rows, rows), jnp.float32))
         wide = jnp.broadcast_to(jnp.sum(total, axis=1, keepdims=True), (rows, rows))
         field[b : b + 1, :] = wide.T[0:1, :]
-        weight = jnp.broadcast_to(source[pl.ds(at, 1), 0], (rows, rows)).T
+        weight = jnp.broadcast_to(source[0, pl.ds(at, 1), :], (rows, rows)).T
         factor[b * rows : (b + 1) * rows, :] = weight * wide
 
 
-def field_only(kept, counts, first, raw, source, blocks):
+def field_only(plan, raw, source, blocks):
     total, rows = raw.shape
     smem = pl.BlockSpec(memory_space=pltpu.SMEM)
     vmem = pl.BlockSpec(memory_space=pltpu.VMEM)
     return pl.pallas_call(
         field_only_kernel,
-        in_specs=[smem] * 3 + [vmem] * 2,
+        in_specs=[smem, vmem, vmem],
         out_specs=[vmem, vmem],
         out_shape=[
             jax.ShapeDtypeStruct((blocks, rows), jnp.float32),
@@ -435,12 +633,11 @@
         ],
         compiler_params=params(),
         name="field_only",
-    )(kept, counts, first, raw, source)
+    )(plan, raw, source)
 
 
 def return_kernel(
     route,
-    mine,
     factor,
     basis,
     land,
@@ -457,7 +654,7 @@
     link_send,
     link_recv,
 ):
-    peers = mine.shape[0] // 2
+    peers = route.shape[1]
     tile = land.shape[1]
     kt = basis.shape[1] // tile
     rows = tile
@@ -482,13 +679,13 @@
             moved(me, back(STEPS[k])),
         )
 
-    def product_for(at):
-        return products[inside(mine[at], 2 * peers)]
+    def product_for(device, slot):
+        return products[inside(route[AT_MINE + slot, device], 2 * peers)]
 
     def second_for(device):
         via = route[AT_SRC, device]
         holder = inside(jnp.where(via > 0, via - 1, device), peers)
-        return product_for(2 * holder + 1)
+        return product_for(holder, 1)
 
     greet_all(peers)
 
@@ -515,7 +712,7 @@
         second(step).start()
 
     seconds[me] = second_for(me)
-    stage[me, 0] = product_for(2 * me)
+    stage[me, 0] = product_for(me, 0)
     own = pltpu.make_async_copy(stage.at[me, 0], land.at[me], own_sems.at[0])
     own.start()
 
@@ -523,7 +720,7 @@
     def _(turn):
         step = narrow_step(turn)
         to = neighbour(step)
-        stage[to, 0] = product_for(2 * to)
+        stage[to, 0] = product_for(to, 0)
         first(step).start()
 
     @pl.loop(1, 64)
@@ -545,7 +742,7 @@
     def _(turn):
         step = wide_step(turn)
         to = neighbour(step)
-        stage[to, 0] = product_for(2 * to)
+        stage[to, 0] = product_for(to, 0)
         first(step).start()
 
     for k in range(LINKS):
@@ -559,19 +756,20 @@
     keep.wait()
 
 
-def return_tiles(plan, mine, factor, basis, peers):
+def return_tiles(plan, factor, basis):
+    peers = plan.shape[1]
     tile = 128
     smem = pl.BlockSpec(memory_space=pltpu.SMEM)
     vmem = pl.BlockSpec(memory_space=pltpu.VMEM)
     pair = pltpu.SemaphoreType.DMA((peers,))
     return pl.pallas_call(
         return_kernel,
-        in_specs=[smem, smem, vmem, vmem],
+        in_specs=[smem, vmem, vmem],
         out_specs=pl.BlockSpec(memory_space=pl.ANY),
         out_shape=jax.ShapeDtypeStruct((2 * peers + RELAYED, tile, tile), jnp.bfloat16),
         scratch_shapes=[
             pltpu.VMEM((peers, tile, tile), jnp.bfloat16),
-            pltpu.VMEM((mine.shape[0], tile, tile), jnp.bfloat16),
+            pltpu.VMEM((2 * peers, tile, tile), jnp.bfloat16),
             pltpu.VMEM((peers, 2, tile, tile), jnp.bfloat16),
             pltpu.VMEM((RELAYED, tile, tile), jnp.bfloat16),
             pltpu.VMEM((tile, tile), jnp.bfloat16),
@@ -585,7 +783,7 @@
         ],
         compiler_params=params(collective_id=1, has_side_effects=True),
         name="return_tiles",
-    )(plan, mine, factor, basis)
+    )(plan, factor, basis)
 
 
 def pick_kernel(asked, tiles, out):
@@ -803,6 +1001,44 @@
     )(order, starts, landed)
 
 
+def collect_planned_kernel(plan, landed, out):
+    step = pl.program_id(0)
+    width = out.shape[0]
+    peers = plan.shape[1]
+
+    @pl.loop(0, width)
+    def _(t):
+        g = step * width + t
+
+        def add(j, total):
+            place = plan[AT_ORDER + j // peers, lax.rem(j, peers)]
+            return total + landed[place].astype(jnp.float32)
+
+        out[t] = lax.fori_loop(
+            plan[AT_STARTS, g],
+            plan[AT_STARTS, g + 1],
+            add,
+            jnp.zeros(out.shape[1:], jnp.float32),
+        )
+
+
+def collect_planned(plan, landed, store_count):
+    tile = landed.shape[1]
+    group = 8
+    return pl.pallas_call(
+        collect_planned_kernel,
+        grid=(store_count // group,),
+        in_specs=[
+            pl.BlockSpec(memory_space=pltpu.SMEM),
+            pl.BlockSpec(memory_space=pltpu.VMEM),
+        ],
+        out_specs=pl.BlockSpec((group, tile, tile), lambda i: (i, 0, 0)),
+        out_shape=jax.ShapeDtypeStruct((store_count, tile, tile), jnp.float32),
+        compiler_params=params(),
+        name="collect_planned",
+    )(plan, landed)
+
+
 def kept_list(keep):
     width = keep.shape[1]
     places = jnp.arange(width, dtype=jnp.int32)
@@ -814,12 +1050,12 @@
     )
 
 
-def slot_order(asked, positions, store_count):
+def slot_order(asked, store_count):
     count = asked.shape[0]
     places = jnp.arange(count, dtype=jnp.int32)
     key = jnp.where(asked >= 0, asked, store_count) * count + places
     rank = jnp.sum((key[None, :] < key[:, None]).astype(jnp.int32), axis=1)
-    order = jnp.sum(jnp.where(rank[:, None] == places[None, :], positions[:, None], 0), axis=0)
+    order = jnp.sum(jnp.where(rank[:, None] == places[None, :], places[:, None], 0), axis=0)
     stores = jnp.arange(store_count + 1, dtype=jnp.int32)
     starts = jnp.sum(
         ((asked[None, :] >= 0) & (asked[None, :] < stores[:, None])).astype(jnp.int32), axis=1
@@ -833,57 +1069,28 @@
     blocks, pairs = pair_tiles.shape
     store_count, tile = dmat.shape[0], dmat.shape[1]
     rows = basis.shape[0] // blocks
-    kt = basis.shape[1] // tile
     capacity = 2
     slot_count = peers * capacity
-    wanted = tile_home[pair_tiles.reshape(-1)]
-    owner = wanted // store_count
-    within = wanted % store_count
-    same = owner[:, None] == owner[None, :]
-    places = jnp.arange(blocks * pairs, dtype=jnp.int32)
-    earlier = jnp.sum((same & (places[None, :] < places[:, None])).astype(jnp.int32), axis=1)
-    slots = owner * capacity + earlier
-    devices = jnp.arange(peers, dtype=jnp.int32)
-    lanes = jnp.arange(tile, dtype=jnp.int32)
-    held = owner[:, None] == devices[None, :]
-    entry = jnp.where(
-        held[:, :, None] & (earlier[:, None] == lanes[None, :])[:, None, :],
-        within[:, None, None] + 1,
-        0,
+    asked, plan, raw, source = fetch_and_density(
+        tile_home,
+        pair_tiles,
+        pair_pos.reshape(1, blocks * pairs),
+        pair_keep,
+        weights.reshape(blocks, rows),
+        grad_sq.reshape(blocks, rows),
+        coords,
+        dmat,
+        basis,
     )
-    named = jnp.sum(held.astype(jnp.int32), axis=0)
-    asking = jnp.stack(
-        [jnp.sum(entry, axis=0), jnp.broadcast_to(named[None, :], (peers, tile))], axis=1
-    )
-    even_me = parity(me.astype(jnp.int32))
-    relayed = (earlier == 1) & (parity(owner) != even_me)
-    spot = pair_pos[:, :, None] == jnp.arange(kt * kt, dtype=jnp.int32)[None, None, :]
-    found = jnp.where(relayed, 2 * slot_count + owner, slots).reshape(blocks, pairs)
-    table = (
-        jnp.sum(jnp.where(spot, found[:, :, None] - slot_count, 0), axis=1) + slot_count
-    )
-    product_at = pair_pos + kt * kt * jnp.arange(blocks, dtype=jnp.int32)[:, None]
-    mine = jnp.sum(
-        jnp.where(
-            slots[:, None] == jnp.arange(slot_count, dtype=jnp.int32)[None, :],
-            product_at.reshape(-1)[:, None],
-            0,
-        ),
-        axis=0,
-    )
-
-    local = jnp.concatenate([weights[None], grad_sq[None], coords], axis=0)
-    local = local.reshape(5, blocks, rows).transpose(1, 0, 2)
-    source = lax.all_gather(local, AXES, axis=0, tiled=True)
-    keep = lax.dynamic_slice_in_dim(pair_keep, me * blocks, blocks, 0)
-    kept, counts = kept_list(keep)
-    first = (me * blocks).astype(jnp.int32).reshape(1)
-
-    asked, plan, raw = fetch_and_density(asking, table, dmat, basis)
-    raw = raw.reshape(peers * blocks, rows)
-    asked = asked[:, 0, :capacity].reshape(-1) - 1
 
     def two_slots():
+        wanted = tile_home[pair_tiles.reshape(-1)]
+        owner = wanted // store_count
+        same = owner[:, None] == owner[None, :]
+        places = jnp.arange(blocks * pairs, dtype=jnp.int32)
+        earlier = jnp.sum((same & (places[None, :] < places[:, None])).astype(jnp.int32), axis=1)
+        slots = owner * capacity + earlier
+        requests = asked[:, 0, :capacity].reshape(-1) - 1
         shape = (peers, capacity, tile, tile)
 
         def exchange(values):
@@ -891,27 +1098,41 @@
                 values.reshape(shape), AXES, split_axis=0, concat_axis=0, tiled=True
             ).reshape(slot_count, tile, tile)
 
-        arrived = exchange(pick_tiles(asked, dmat))
-        again = block_density(slots, pair_pos, basis, arrived)
-        again = lax.all_gather(again, AXES, axis=0, tiled=True)
+        def spread(values):
+            wide = jnp.broadcast_to(values[None], (peers,) + values.shape)
+            return lax.all_to_all(wide, AXES, split_axis=0, concat_axis=0, tiled=True)
+
+        arrived = exchange(pick_tiles(requests, dmat))
+        again = spread(block_density(slots, pair_pos, basis, arrived))
+        features = source.transpose(2, 1, 3, 0, 4).reshape(peers * blocks, 5, rows)
+        keep = lax.dynamic_slice_in_dim(pair_keep, me * blocks, blocks, 0)
+        kept, counts = kept_list(keep)
+        first = (me * blocks).astype(jnp.int32).reshape(1)
         field, returning = field_and_tiles(
-            kept, counts, slots, pair_pos, first, again, source, basis, slot_count
-        )
-        order, starts = slot_order(
-            asked, jnp.arange(slot_count, dtype=jnp.int32), store_count
-        )
+            kept,
+            counts,
+            slots,
+            pair_pos,
+            first,
+            again.reshape(peers * blocks, rows),
+            features,
+            basis,
+            slot_count,
+        )
+        order, starts = slot_order(requests, store_count)
         return collect_tiles(order, starts, exchange(returning), store_count), field
 
     def relays():
-        field, factor = field_only(kept, counts, first, raw, source, blocks)
-        wide = parity(devices) == even_me
-        seconds = jnp.where(wide, peers + devices, 2 * peers + plan[AT_BACK])
-        places = jnp.stack([devices, seconds], axis=1).reshape(-1)
-        order, starts = slot_order(asked, places, store_count)
-        land = return_tiles(plan, mine, factor, basis, peers)
-        return collect_tiles(order, starts, land, store_count), field
-
-    pieces, field = lax.cond(jnp.sum(plan[AT_LEFT]) > 0, two_slots, relays)
+        field, factor = field_only(
+            plan,
+            raw.reshape(peers * blocks, rows),
+            source.reshape(5, peers * blocks, rows),
+            blocks,
+        )
+        land = return_tiles(plan, factor, basis)
+        return collect_planned(plan, land, store_count), field
+
+    pieces, field = lax.cond(plan[AT_LEFT, 0] > 0, two_slots, relays)
     return pieces, field.reshape(-1)
 
 

time: 278 us -> 253 us (0.910)
  other arithmetic: 14.4 us -> 0 us
  between operations: 14.9 us -> 1.4 us
  Pallas kernels: 243 us -> 247 us
    reduce_sum x10 -> x0, other arithmetic: 8.74 us -> none  [the longest x1 2.92 us: body(): jnp.sum(entry, axis=0)]
    pallas_call x4, Pallas kernels: 243 us -> 247 us  [the longest x1 141 us: fetch_and_density(): pl.pallas_call(fetch_kernel, in_specs=[smem, smem, vmem, pl.BlockSpec(mem...]
  transfers between devices with their start and end apart: 1 -> 0, of which waited for: 0 -> 0; matrix products, arithmetic and copies ran while one was open for 5% -> 0% of each run, Pallas kernels for 50% -> 0%
where the time goes in v4:
time: 253 us; the launch traced here: 252 us
  Pallas kernels  247 us (98%)
  local copies, waits for them, and re-layouts  3.97 us (2%)
    pallas_call x1, Pallas kernels, fetch_and_density(): pl.pallas_call(fetch_kernel, in_specs=[smem, smem, vmem, pl.BlockSpec(mem...  141 us
    pallas_call x1, Pallas kernels, return_tiles(): pl.pallas_call(return_kernel, in_specs=[smem, vmem, vmem], out_specs=pl.B...  93.4 us
    pallas_call x1, Pallas kernels, collect_planned(): pl.pallas_call(collect_planned_kernel, grid=(store_count // group,), in_s...  8.01 us

profile of v4, /device:TPU:1, one launch (start us, length us, event | category | flops | bytes accessed | tf_op | source)
XLA Modules:
  0.0 252.3 jit_solution(700947124497235329)
XLA Ops:
  0.6 0.0 copy-start.6
  0.6 0.0 copy-start
  0.7 0.0 copy-start.2
  0.7 0.0 copy-start.1
  0.7 0.0 copy-start.8
  0.7 1.4 reshape.160.spots
  2.1 140.6 %fetch_and_density.1 = (s32[128,2,128]{2,1,0:T(2,128)}, s32[64,128]{1,0:T(8,128)S(1)}, f32[2,64,4,128]{3,2,1,0:T(4,128)S(1)}, f32[5,2,64,4,128]{4,3,2,1,0:T(4,128)}) custom-call(s32[8192]{0:T(1024)} %home.1, s32[4,32]{1,0:T(4,128)} %pair_tiles.1, s32[1,128]{1,0:T(1,128)} %reshape.160.spots, s32[512,512]{1,0:T(8,128)} %pair_keep.1, f32[4,128]{1,0:T(4,128)} %bitcast.31, ...), custom_call_target="tpu_custom_call" | custom-call | tf_op jit(solution)/shard_map/fetch_and_density/pallas_call | solution.py:540
  142.7 0.5 slice.12
  143.9 0.0 copy-done.6
  143.9 0.0 copy-done
  143.9 0.0 copy-done.2
  143.9 0.0 copy-done.1
  143.9 0.0 copy-done.8
  143.9 106.4 %conditional.1 = (f32[64,128,128]{2,1,0:T(8,128)S(1)}, f32[4,128]{1,0:T(4,128)S(1)}) conditional(s32[]{:T(128)} %bitcast.14, (f32[2,64,4,128]{3,2,1,0:T(4,128)S(1)}, f32[5,2,64,4,128]{4,3,2,1,0:T(4,128)}, s32[64,128]{1,0:T(8,128)S(1)}, bf16[512,1024]{1,0:T(8,128)(2,1)S(1)}) %tuple.27, (s32[128,2,128]{2,1,0:T(2,128)}, s32[]{:T(128)}, ...), branch_computations={%region_0.0_spmd, %region_1.10_spmd} | conditional | flops 5008637 | bytes 60705656 | solution.py:1135
  144.1 4.6 %field_only.1 = (f32[4,128]{1,0:T(4,128)S(1)}, f32[512,128]{1,0:T(8,128)}) custom-call(s32[64,128]{1,0:T(8,128)S(1)} %get-tuple-element.26.plan.route, f32[512,128]{1,0:T(8,128)S(1)} %bitcast.29, f32[5,512,128]{2,1,0:T(8,128)} %bitcast.27), custom_call_target="tpu_custom_call" | custom-call | tf_op jit(solution)/shard_map/cond/branch_0_fun/field_only/pallas_call | solution.py:622
  148.7 93.4 %return_tiles.1.landed = bf16[357,128,128]{2,1,0:T(8,128)(2,1)} custom-call(s32[64,128]{1,0:T(8,128)S(1)} %get-tuple-element.26.plan.route, f32[512,128]{1,0:T(8,128)} %get-tuple-element.29.factor, bf16[512,1024]{1,0:T(8,128)(2,1)S(1)} %get-tuple-element.30.basis), custom_call_target="tpu_custom_call" | custom-call | tf_op jit(solution)/shard_map/cond/branch_0_fun/return_tiles/pallas_call | solution.py:765
  242.1 8.0 %collect_planned.1 = f32[64,128,128]{2,1,0:T(8,128)S(1)} custom-call(s32[64,128]{1,0:T(8,128)S(1)} %get-tuple-element.26.plan.route, bf16[357,128,128]{2,1,0:T(8,128)(2,1)} %return_tiles.1.landed), custom_call_target="tpu_custom_call" | custom-call | tf_op jit(solution)/shard_map/cond/branch_0_fun/collect_planned/pallas_call | solution.py:1028
  250.3 0.0 copy-start.4
  250.3 0.0 copy-start.9
  250.3 2.0 copy-done.4
  252.3 0.0 copy-done.9
Async XLA Ops:
  0.6 143.2 %copy-start.6 = (s32[4,32]{1,0:T(4,128)S(1)}, s32[4,32]{1,0:T(4,128)}, u32[]{:S(2)}) copy-start(s32[4,32]{1,0:T(4,128)} %param.15) | copy-start | bytes 1540
  0.6 143.2 %copy-start = (bf16[512,1024]{1,0:T(8,128)(2,1)S(1)}, bf16[512,1024]{1,0:T(8,128)(2,1)}, u32[]{:S(2)}) copy-start(bf16[512,1024]{1,0:T(8,128)(2,1)} %basis.1) | copy-start | bytes 3145732
  0.7 143.2 %copy-start.2 = (bf16[64,128,128]{2,1,0:T(8,128)(2,1)S(1)}, bf16[64,128,128]{2,1,0:T(8,128)(2,1)}, u32[]{:S(2)}) copy-start(bf16[64,128,128]{2,1,0:T(8,128)(2,1)} %tiles.1) | copy-start | bytes 6291460
  0.7 143.2 %copy-start.1 = (s32[8192]{0:T(1024)S(1)}, s32[8192]{0:T(1024)}, u32[]{:S(2)}) copy-start(s32[8192]{0:T(1024)} %home.1) | copy-start | bytes 98308
  0.7 143.2 %copy-start.8 = (s32[4,32]{1,0:T(4,128)S(1)}, s32[4,32]{1,0:T(4,128)}, u32[]{:S(2)}) copy-start(s32[4,32]{1,0:T(4,128)} %pair_tiles.1) | copy-start | bytes 1540
  250.3 2.0 copy-start.4
  250.3 2.0 copy-start.9

commit v5 on v4

--- a/solution.py
+++ b/solution.py
@@ -38,9 +38,9 @@
 RELAYED = sum(ROOM)
 AT_LOC, AT_SRC, AT_CODE, AT_LEFT, AT_STARTS = range(2 * LINKS, 2 * LINKS + 5)
 AT_TABLE, AT_MINE, AT_ORDER = 2 * LINKS + 5, 2 * LINKS + 7, 2 * LINKS + 9
-AT_KEPT = 2 * LINKS + 11
-AT_COUNTS = AT_KEPT + 16
-PLAN_ROWS = AT_COUNTS + 5
+AT_KEPT, AT_BLOCK, AT_FIRST, AT_LAST = range(2 * LINKS + 11, 2 * LINKS + 15)
+PLAN_ROWS = 2 * LINKS + 16
+ENTRIES = 44
 
 
 def point_features(raw_density, grad_sq):
@@ -117,9 +117,9 @@
 def make_requests(want, asking):
     peers = want.shape[1]
     sub, lane = iotas(peers)
-    owner_int = want[...] // 64
+    owner_int = want[0:1, :] // 64
     owner = owner_int.astype(jnp.float32)
-    within = (want[...] - owner_int * 64).astype(jnp.float32)
+    within = (want[0:1, :] - owner_int * 64).astype(jnp.float32)
     owner_down = down(owner, peers)
     same = owner_down == owner
     rank = across(same & (sub < lane), jnp.ones_like(owner_down))
@@ -135,18 +135,18 @@
     asking[:, 1, :] = jnp.broadcast_to(named, (peers, peers)).astype(jnp.int32)
 
 
-def make_tables(want, spots, plan):
+def make_tables(want, plan):
     peers = want.shape[1]
     sub, lane = iotas(peers)
     me = this_device()
-    owner_int = want[...] // 64
+    owner_int = want[0:1, :] // 64
     owner = owner_int.astype(jnp.float32)
     owner_down = down(owner, peers)
     rank = across((owner_down == owner) & (sub < lane), jnp.ones_like(owner_down))
     odd = parity(owner_int) != parity(me)
     found = jnp.where((rank == 1.0) & odd, 4.0 * peers + owner, 2.0 * owner + rank)
     pair = lax.broadcasted_iota(jnp.int32, (1, peers), 1)
-    spot = (spots[...] + 64 * (pair // 32)).astype(jnp.float32)
+    spot = (want[1:2, :] + 64 * (pair // 32)).astype(jnp.float32)
     rank_down, found_down, spot_down = down(rank, peers), down(found, peers), down(spot, peers)
     for half in range(2):
         row = across(spot_down == lane + half * peers, found_down - 2.0 * peers) + 2.0 * peers
@@ -193,27 +193,39 @@
     blocks = keep.shape[0]
     peers = 128
     sub, lane = iotas(peers)
+    lanes = lane[0:1, :]
     parts = keep.shape[1] // peers
+    before = jnp.zeros((1, 1), jnp.float32)
+    places, block_of, first, last = (jnp.zeros((1, peers), jnp.float32) for _ in range(4))
     for b in range(blocks):
-        before = jnp.zeros((1, 1), jnp.float32)
-        ranks = []
+        first = first + jnp.where(lanes == before, 1.0, 0.0)
+        if b:
+            block_of = block_of + jnp.where(lanes >= before, 1.0, 0.0)
         for g in range(parts):
             row = keep[b : b + 1, g * peers : (g + 1) * peers]
             rank = jnp.sum(jnp.where(lane < sub, row, 0.0), axis=1, keepdims=True) + before
-            ranks.append(jnp.where(down(row, peers) > 0.0, rank, -1.0))
+            rank = jnp.where(down(row, peers) > 0.0, rank, -1.0)
+            block = lax.broadcasted_iota(jnp.int32, (peers, 1), 0) + g * peers
+            device = block // 4
+            place = ((device % 2) * 64 + device // 2) * 4 + block % 4
+            places = places + across(rank == lane, place.astype(jnp.float32))
             before = before + jnp.sum(row, axis=1, keepdims=True)
-        for h in range(parts):
-            total = jnp.zeros((1, peers), jnp.float32)
-            for g in range(parts):
-                block = lax.broadcasted_iota(jnp.int32, (peers, 1), 0) + g * peers
-                device = block // 4
-                place = ((device % 2) * 64 + device // 2) * 4 + block % 4
-                total = total + across(ranks[g] == lane + h * peers, place.astype(jnp.float32))
-            at = AT_KEPT + parts * b + h
-            plan[at : at + 1, :] = total.astype(jnp.int32)
-        plan[AT_COUNTS + b : AT_COUNTS + b + 1, :] = jnp.broadcast_to(before, (1, peers)).astype(
-            jnp.int32
-        )
+        last = last + jnp.where(lanes == b, before - 1.0, 0.0)
+    for at, row in ((AT_KEPT, places), (AT_BLOCK, block_of), (AT_FIRST, first), (AT_LAST, last)):
+        plan[at : at + 1, :] = row.astype(jnp.int32)
+
+
+def most_kept(keep):
+    total = keep.shape[0]
+    peers = total // 4
+    row = lax.broadcasted_iota(jnp.int32, (peers, total), 1) // 4
+    group = jnp.where(row == lax.broadcasted_iota(jnp.int32, (peers, total), 0), 1.0, 0.0)
+    counts = jnp.dot(
+        group.astype(jnp.bfloat16),
+        keep[...].astype(jnp.float32).astype(jnp.bfloat16),
+        preferred_element_type=jnp.float32,
+    )
+    return jnp.max(jnp.sum(counts, axis=1, keepdims=True), axis=0, keepdims=True)
 
 
 def greet_all(peers):
@@ -291,15 +303,14 @@
     plan[AT_SRC : AT_SRC + 1, :] = row_of(src).astype(jnp.int32)
     plan[AT_CODE : AT_CODE + 1, :] = turned(code).astype(jnp.int32)
     unplaced = jnp.sum(jnp.sum(left, axis=1, keepdims=True), axis=0, keepdims=True)
-    plan[AT_LEFT : AT_LEFT + 1, :] = jnp.broadcast_to(unplaced, (1, peers)).astype(jnp.int32)
-    plan[AT_COUNTS + 4 :, :] = jnp.zeros((PLAN_ROWS - AT_COUNTS - 4, peers), jnp.int32)
-    return mine(again)
-
-
-def fetch_kernel(
+    plan[PLAN_ROWS - 1 :, :] = jnp.zeros((1, peers), jnp.int32)
+    return mine(again), unplaced
+
+
+def exchange_kernel(
     home,
     pair_tiles,
-    spots,
+    pair_pos,
     pair_keep,
     weights,
     grad_sq,
@@ -308,8 +319,8 @@
     basis,
     asked,
     plan,
-    raw_all,
-    source_all,
+    field,
+    land,
     wanted,
     route,
     want_smem,
@@ -317,6 +328,14 @@
     asking,
     keep,
     local,
+    raw_all,
+    source_all,
+    feats,
+    column,
+    partial,
+    scaled,
+    chis,
+    seconds,
     stage,
     arrived,
     link_out,
@@ -335,6 +354,12 @@
     share_recv,
     raw_send,
     raw_recv,
+    first_back_send,
+    first_back_recv,
+    second_back_send,
+    second_back_recv,
+    link_back_send,
+    link_back_recv,
 ):
     peers = asked.shape[0]
     chips = peers // 2
@@ -394,14 +419,14 @@
         return copy
 
     greet_all(peers)
-    pair = lax.div(me, 2)
-    keep_copy = move(pair_keep.at[pl.ds(pl.multiple_of(8 * pair, 8), 8)], keep, 0)
+    keep_copy = move(pair_keep, keep, 0)
 
     for b in range(blocks):
 
         @pl.loop(0, pairs)
         def _(j):
             want_smem[0, b * pairs + j] = home[inside(pair_tiles[b, j], home.shape[0])]
+            want_smem[1, b * pairs + j] = pair_pos[b, j]
 
     move(want_smem, want, 1).wait()
     make_requests(want, asking)
@@ -437,7 +462,7 @@
         stage[to, 0] = tile_for(to, 0)
         first(step).start()
 
-    again = make_plan(asked[:, 1, :], plan)
+    again, unplaced = make_plan(asked[:, 1, :], plan)
     move(plan, route, 3).wait()
 
     for k in range(LINKS):
@@ -474,11 +499,20 @@
         share(up).wait()
 
     share_on().start()
-    make_tables(want, spots, plan)
+    make_tables(want, plan)
     make_order(asked[:, 0, :].astype(jnp.float32), again, plan)
     keep_copy.wait()
-    kept = jnp.where(core == 0, keep[0:4, :], keep[4:8, :]).astype(jnp.float32)
-    make_kept(kept, plan)
+    mine = keep[pl.ds(pl.multiple_of(8 * chip, 8), 8), :]
+    make_kept(jnp.where(core == 0, mine[0:4, :], mine[4:8, :]).astype(jnp.float32), plan)
+    unplaced = unplaced + jnp.where(most_kept(keep) > ENTRIES, 1.0, 0.0)
+    plan[AT_LEFT : AT_LEFT + 1, :] = jnp.broadcast_to(unplaced, (1, peers)).astype(jnp.int32)
+    for b in range(blocks):
+        for m in range(kt):
+            chis[b * kt + m] = basis[b * rows : (b + 1) * rows, m * tile : (m + 1) * tile]
+        for axis in range(3):
+            row = local[2 + axis, b : b + 1, :]
+            column[b * 6 + 2 + axis] = jnp.broadcast_to(row, (rows, rows)).T
+        column[b * 6 + 5] = jnp.broadcast_to(local[0, b : b + 1, :], (rows, rows)).T
     move(plan, route, 4).wait()
 
     @pl.loop(1, peers)
@@ -526,264 +560,179 @@
     def _(up):
         tell(up).wait()
 
-
-def fetch_and_density(home, pair_tiles, spots, pair_keep, weights, grad_sq, coords, tiles, basis):
+    density, omega, kappa = point_features(raw_all[...], source_all[1])
+    feats[0] = (source_all[0] * density).reshape(blocks * peers, rows)
+    feats[1] = omega.reshape(blocks * peers, rows)
+    feats[2] = kappa.reshape(blocks * peers, rows)
+    for axis in range(3):
+        feats[3 + axis] = source_all[2 + axis].reshape(blocks * peers, rows)
+    start = pl.multiple_of((core * chips + chip) * blocks, blocks)
+    for b in range(blocks):
+        for f in range(2):
+            row = feats[1 + f, pl.ds(start + b, 1), :]
+            column[b * 6 + f] = jnp.broadcast_to(row, (rows, rows)).T
+
+    def one_pair(e, total):
+        s = inside(route[AT_KEPT, e], blocks * peers)
+        at = 6 * inside(route[AT_BLOCK, e], blocks)
+        r2 = None
+        for axis in range(3):
+            gap = column[at + 2 + axis] - feats[3 + axis, pl.ds(s, 1), :]
+            r2 = gap * gap if r2 is None else r2 + gap * gap
+        g = column[at] * r2 + column[at + 1]
+        h = feats[1, pl.ds(s, 1), :] * r2 + feats[2, pl.ds(s, 1), :]
+        phi = -1.5 / (g * h * (g + h))
+        total = jnp.where(route[AT_FIRST, e] > 0, 0.0, total) + phi * feats[0, pl.ds(s, 1), :]
+        partial[e] = total
+        return total
+
+    lax.fori_loop(0, ENTRIES, one_pair, jnp.zeros((rows, rows), jnp.float32))
+    for b in range(blocks):
+        total = partial[inside(route[AT_LAST, b], ENTRIES)]
+        wide = jnp.broadcast_to(jnp.sum(total, axis=1, keepdims=True), (rows, rows))
+        field[b : b + 1, :] = wide.T[0:1, :]
+        factor = column[b * 6 + 5] * wide
+        for m in range(kt):
+            part = chis[b * kt + m].astype(jnp.float32) * factor
+            scaled[b * kt + m] = part.astype(jnp.bfloat16).T
+
+    def first_back(step):
+        to = neighbour(step)
+        return remote(stage.at[to, 0], land.at[me], first_back_send, first_back_recv, step, to)
+
+    def second_back(step):
+        to = neighbour(step)
+        return remote(
+            stage.at[to, 1], seconds.at[me], second_back_send, second_back_recv, step, to
+        )
+
+    def link_back(k):
+        return remote(
+            link_out.at[pl.ds(BASE[k], ROOM[k])],
+            land.at[pl.ds(2 * peers + BASE[k], ROOM[k])],
+            link_back_send,
+            link_back_recv,
+            k,
+            moved(me, back(STEPS[k])),
+        )
+
+    def product_for(device, slot):
+        at = inside(route[AT_MINE + slot, device], 2 * peers)
+        b, q = at // (kt * kt), lax.rem(at, kt * kt)
+        return jnp.dot(
+            scaled[b * kt + q // kt],
+            chis[b * kt + lax.rem(q, kt)],
+            preferred_element_type=jnp.float32,
+        ).astype(jnp.bfloat16)
+
+    def second_product(device):
+        via = route[AT_SRC, device]
+        return product_for(inside(jnp.where(via > 0, via - 1, device), peers), 1)
+
+    @pl.loop(1, 64)
+    def _(turn):
+        step = wide_step(turn)
+        to = neighbour(step)
+        stage[to, 1] = second_product(to)
+        second_back(step).start()
+
+    seconds[me] = second_product(me)
+    stage[me, 0] = product_for(me, 0)
+    own = move(stage.at[me, 0], land.at[me], 5)
+
+    @pl.loop(0, 64)
+    def _(turn):
+        step = narrow_step(turn)
+        to = neighbour(step)
+        stage[to, 0] = product_for(to, 0)
+        first_back(step).start()
+
+    @pl.loop(1, 64)
+    def _(turn):
+        second_back(wide_step(turn)).wait()
+
+    for k in range(LINKS):
+
+        @pl.loop(0, ROOM[k])
+        def _(s):
+            link_out[BASE[k] + s] = seconds[inside(route[LINKS + k, s], peers)]
+
+        link_back(k).start()
+
+    rest = move(seconds, land.at[pl.ds(peers, peers)], 6)
+
+    @pl.loop(1, 64)
+    def _(turn):
+        step = wide_step(turn)
+        to = neighbour(step)
+        stage[to, 0] = product_for(to, 0)
+        first_back(step).start()
+
+    for k in range(LINKS):
+        link_back(k).wait()
+
+    @pl.loop(1, peers)
+    def _(step):
+        first_back(step).wait()
+
+    own.wait()
+    rest.wait()
+
+
+def exchange(home, pair_tiles, pair_pos, pair_keep, weights, grad_sq, coords, tiles, basis):
     blocks, pairs = pair_tiles.shape
     tile = tiles.shape[1]
     peers = blocks * pairs
     rows = basis.shape[0] // blocks
     orbs = basis.shape[1]
+    kt = orbs // tile
     smem = pl.BlockSpec(memory_space=pltpu.SMEM)
     vmem = pl.BlockSpec(memory_space=pltpu.VMEM)
+    hbm = pl.BlockSpec(memory_space=pl.ANY)
     pair = pltpu.SemaphoreType.DMA((peers,))
     half = pltpu.SemaphoreType.DMA((peers // 2,))
+    links = pltpu.SemaphoreType.DMA((LINKS,))
     return pl.pallas_call(
-        fetch_kernel,
-        in_specs=[smem, smem, vmem, pl.BlockSpec(memory_space=pl.ANY)] + [vmem] * 5,
-        out_specs=[vmem, vmem, vmem, vmem],
+        exchange_kernel,
+        in_specs=[smem, smem, smem, hbm] + [vmem] * 5,
+        out_specs=[vmem, vmem, vmem, hbm],
         out_shape=[
             jax.ShapeDtypeStruct((peers, 2, peers), jnp.int32),
             jax.ShapeDtypeStruct((PLAN_ROWS, peers), jnp.int32),
-            jax.ShapeDtypeStruct((2, peers // 2, blocks, rows), jnp.float32),
-            jax.ShapeDtypeStruct((5, 2, peers // 2, blocks, rows), jnp.float32),
+            jax.ShapeDtypeStruct((blocks, rows), jnp.float32),
+            jax.ShapeDtypeStruct((2 * peers + RELAYED, tile, tile), tiles.dtype),
         ],
         scratch_shapes=[
             pltpu.SMEM((peers, 2, peers), jnp.int32),
             pltpu.SMEM((PLAN_ROWS, peers), jnp.int32),
-            pltpu.SMEM((1, peers), jnp.int32),
-            pltpu.VMEM((1, peers), jnp.int32),
+            pltpu.SMEM((2, peers), jnp.int32),
+            pltpu.VMEM((2, peers), jnp.int32),
             pltpu.VMEM((peers, 2, peers), jnp.int32),
-            pltpu.VMEM((8, pair_keep.shape[1]), jnp.int32),
+            pltpu.VMEM(pair_keep.shape, jnp.int32),
             pltpu.VMEM((5, blocks, rows), jnp.float32),
+            pltpu.VMEM((2, peers // 2, blocks, rows), jnp.float32),
+            pltpu.VMEM((5, 2, peers // 2, blocks, rows), jnp.float32),
+            pltpu.VMEM((6, blocks * peers, rows), jnp.float32),
+            pltpu.VMEM((6 * blocks, rows, rows), jnp.float32),
+            pltpu.VMEM((ENTRIES, rows, rows), jnp.float32),
+            pltpu.VMEM((blocks * kt, tile, rows), basis.dtype),
+            pltpu.VMEM((blocks * kt, rows, tile), basis.dtype),
+            pltpu.VMEM((peers, tile, tile), basis.dtype),
             pltpu.VMEM((peers, 2, tile, tile), tiles.dtype),
             pltpu.VMEM((peers + 1, 2, tile, tile), tiles.dtype),
             pltpu.VMEM((RELAYED, tile, tile), tiles.dtype),
             pltpu.VMEM((RELAYED, tile, tile), tiles.dtype),
             pltpu.VMEM((2, orbs, orbs), basis.dtype),
-            pltpu.SemaphoreType.DMA((5,)),
-            pair,
-            pair,
-            pair,
-            pair,
-            pair,
-            pair,
-            pltpu.SemaphoreType.DMA((LINKS,)),
-            pltpu.SemaphoreType.DMA((LINKS,)),
-            half,
-            half,
-            half,
-            half,
-        ],
+            pltpu.SemaphoreType.DMA((7,)),
+        ]
+        + [pair] * 6
+        + [links] * 2
+        + [half] * 4
+        + [pair] * 4
+        + [links] * 2,
         compiler_params=params(collective_id=0, has_side_effects=True),
-        name="fetch_and_density",
-    )(home, pair_tiles, spots, pair_keep, weights, grad_sq, coords, tiles, basis)
-
-
-def field_only_kernel(plan, raw, source, field, factor, feats, column):
-    blocks, rows = field.shape
-    me = this_device()
-    start = (lax.rem(me, 2) * 64 + me // 2) * blocks
-    weights = source[0]
-    density, omega, kappa = point_features(raw[...], source[1])
-    feats[0] = weights * density
-    feats[1] = omega
-    feats[2] = kappa
-    for axis in range(3):
-        feats[3 + axis] = source[2 + axis]
-
-    for b in range(blocks):
-        at = start + b
-        for f in range(5):
-            row = feats[1 + f, pl.ds(at, 1), :]
-            column[f] = jnp.broadcast_to(row, (rows, rows)).T
-
-        def one_source(j, total):
-            s = plan[AT_KEPT + 4 * b + j // rows, lax.rem(j, rows)]
-            r2 = None
-            for axis in range(3):
-                gap = column[2 + axis] - feats[3 + axis, pl.ds(s, 1), :]
-                r2 = gap * gap if r2 is None else r2 + gap * gap
-            g = column[0] * r2 + column[1]
-            h = feats[1, pl.ds(s, 1), :] * r2 + feats[2, pl.ds(s, 1), :]
-            phi = -1.5 / (g * h * (g + h))
-            return total + phi * feats[0, pl.ds(s, 1), :]
-
-        total = lax.fori_loop(0, plan[AT_COUNTS + b, 0], one_source, jnp.zeros((rows, rows), jnp.float32))
-        wide = jnp.broadcast_to(jnp.sum(total, axis=1, keepdims=True), (rows, rows))
-        field[b : b + 1, :] = wide.T[0:1, :]
-        weight = jnp.broadcast_to(source[0, pl.ds(at, 1), :], (rows, rows)).T
-        factor[b * rows : (b + 1) * rows, :] = weight * wide
-
-
-def field_only(plan, raw, source, blocks):
-    total, rows = raw.shape
-    smem = pl.BlockSpec(memory_space=pltpu.SMEM)
-    vmem = pl.BlockSpec(memory_space=pltpu.VMEM)
-    return pl.pallas_call(
-        field_only_kernel,
-        in_specs=[smem, vmem, vmem],
-        out_specs=[vmem, vmem],
-        out_shape=[
-            jax.ShapeDtypeStruct((blocks, rows), jnp.float32),
-            jax.ShapeDtypeStruct((blocks * rows, rows), jnp.float32),
-        ],
-        scratch_shapes=[
-            pltpu.VMEM((6, total, rows), jnp.float32),
-            pltpu.VMEM((5, rows, rows), jnp.float32),
-        ],
-        compiler_params=params(),
-        name="field_only",
-    )(plan, raw, source)
-
-
-def return_kernel(
-    route,
-    factor,
-    basis,
-    land,
-    seconds,
-    products,
-    stage,
-    link_out,
-    scaled,
-    own_sems,
-    first_send,
-    first_recv,
-    second_send,
-    second_recv,
-    link_send,
-    link_recv,
-):
-    peers = route.shape[1]
-    tile = land.shape[1]
-    kt = basis.shape[1] // tile
-    rows = tile
-    blocks = basis.shape[0] // rows
-    me = this_device()
-
-    def first(step):
-        to = neighbour(step)
-        return remote(stage.at[to, 0], land.at[me], first_send, first_recv, step, to)
-
-    def second(step):
-        to = neighbour(step)
-        return remote(stage.at[to, 1], seconds.at[me], second_send, second_recv, step, to)
-
-    def link(k):
-        return remote(
-            link_out.at[pl.ds(BASE[k], ROOM[k])],
-            land.at[pl.ds(2 * peers + BASE[k], ROOM[k])],
-            link_send,
-            link_recv,
-            k,
-            moved(me, back(STEPS[k])),
-        )
-
-    def product_for(device, slot):
-        return products[inside(route[AT_MINE + slot, device], 2 * peers)]
-
-    def second_for(device):
-        via = route[AT_SRC, device]
-        holder = inside(jnp.where(via > 0, via - 1, device), peers)
-        return product_for(holder, 1)
-
-    greet_all(peers)
-
-    @pl.loop(0, blocks)
-    def _(b):
-        chi = basis[pl.ds(pl.multiple_of(b * rows, rows), rows), :]
-        by = factor[pl.ds(pl.multiple_of(b * rows, rows), rows), :]
-        for m in range(kt):
-            part = chi[:, m * tile : (m + 1) * tile].astype(jnp.float32) * by
-            scaled[...] = part.astype(jnp.bfloat16).T
-            product = jnp.dot(scaled[...], chi, preferred_element_type=jnp.float32)
-            for n in range(kt):
-                products[b * kt * kt + m * kt + n] = product[
-                    :, n * tile : (n + 1) * tile
-                ].astype(jnp.bfloat16)
-
-    wait_all(peers)
-
-    @pl.loop(1, 64)
-    def _(turn):
-        step = wide_step(turn)
-        to = neighbour(step)
-        stage[to, 1] = second_for(to)
-        second(step).start()
-
-    seconds[me] = second_for(me)
-    stage[me, 0] = product_for(me, 0)
-    own = pltpu.make_async_copy(stage.at[me, 0], land.at[me], own_sems.at[0])
-    own.start()
-
-    @pl.loop(0, 64)
-    def _(turn):
-        step = narrow_step(turn)
-        to = neighbour(step)
-        stage[to, 0] = product_for(to, 0)
-        first(step).start()
-
-    @pl.loop(1, 64)
-    def _(turn):
-        second(wide_step(turn)).wait()
-
-    for k in range(LINKS):
-
-        @pl.loop(0, ROOM[k])
-        def _(s):
-            link_out[BASE[k] + s] = seconds[inside(route[LINKS + k, s], peers)]
-
-        link(k).start()
-
-    keep = pltpu.make_async_copy(seconds, land.at[pl.ds(peers, peers)], own_sems.at[1])
-    keep.start()
-
-    @pl.loop(1, 64)
-    def _(turn):
-        step = wide_step(turn)
-        to = neighbour(step)
-        stage[to, 0] = product_for(to, 0)
-        first(step).start()
-
-    for k in range(LINKS):
-        link(k).wait()
-
-    @pl.loop(1, peers)
-    def _(step):
-        first(step).wait()
-
-    own.wait()
-    keep.wait()
-
-
-def return_tiles(plan, factor, basis):
-    peers = plan.shape[1]
-    tile = 128
-    smem = pl.BlockSpec(memory_space=pltpu.SMEM)
-    vmem = pl.BlockSpec(memory_space=pltpu.VMEM)
-    pair = pltpu.SemaphoreType.DMA((peers,))
-    return pl.pallas_call(
-        return_kernel,
-        in_specs=[smem, vmem, vmem],
-        out_specs=pl.BlockSpec(memory_space=pl.ANY),
-        out_shape=jax.ShapeDtypeStruct((2 * peers + RELAYED, tile, tile), jnp.bfloat16),
-        scratch_shapes=[
-            pltpu.VMEM((peers, tile, tile), jnp.bfloat16),
-            pltpu.VMEM((2 * peers, tile, tile), jnp.bfloat16),
-            pltpu.VMEM((peers, 2, tile, tile), jnp.bfloat16),
-            pltpu.VMEM((RELAYED, tile, tile), jnp.bfloat16),
-            pltpu.VMEM((tile, tile), jnp.bfloat16),
-            pltpu.SemaphoreType.DMA((2,)),
-            pair,
-            pair,
-            pair,
-            pair,
-            pltpu.SemaphoreType.DMA((LINKS,)),
-            pltpu.SemaphoreType.DMA((LINKS,)),
-        ],
-        compiler_params=params(collective_id=1, has_side_effects=True),
-        name="return_tiles",
-    )(plan, factor, basis)
+        name="exchange",
+    )(home, pair_tiles, pair_pos, pair_keep, weights, grad_sq, coords, tiles, basis)
 
 
 def pick_kernel(asked, tiles, out):
@@ -1071,10 +1020,10 @@
     rows = basis.shape[0] // blocks
     capacity = 2
     slot_count = peers * capacity
-    asked, plan, raw, source = fetch_and_density(
+    asked, plan, field, land = exchange(
         tile_home,
         pair_tiles,
-        pair_pos.reshape(1, blocks * pairs),
+        pair_pos,
         pair_keep,
         weights.reshape(blocks, rows),
         grad_sq.reshape(blocks, rows),
@@ -1093,7 +1042,7 @@
         requests = asked[:, 0, :capacity].reshape(-1) - 1
         shape = (peers, capacity, tile, tile)
 
-        def exchange(values):
+        def swap(values):
             return lax.all_to_all(
                 values.reshape(shape), AXES, split_axis=0, concat_axis=0, tiled=True
             ).reshape(slot_count, tile, tile)
@@ -1102,38 +1051,32 @@
             wide = jnp.broadcast_to(values[None], (peers,) + values.shape)
             return lax.all_to_all(wide, AXES, split_axis=0, concat_axis=0, tiled=True)
 
-        arrived = exchange(pick_tiles(requests, dmat))
+        arrived = swap(pick_tiles(requests, dmat))
         again = spread(block_density(slots, pair_pos, basis, arrived))
-        features = source.transpose(2, 1, 3, 0, 4).reshape(peers * blocks, 5, rows)
+        local = jnp.concatenate([weights[None], grad_sq[None], coords], axis=0)
+        features = spread(local.reshape(5, blocks, rows).transpose(1, 0, 2))
         keep = lax.dynamic_slice_in_dim(pair_keep, me * blocks, blocks, 0)
         kept, counts = kept_list(keep)
         first = (me * blocks).astype(jnp.int32).reshape(1)
-        field, returning = field_and_tiles(
+        again, returning = field_and_tiles(
             kept,
             counts,
             slots,
             pair_pos,
             first,
             again.reshape(peers * blocks, rows),
-            features,
+            features.reshape(peers * blocks, 5, rows),
             basis,
             slot_count,
         )
         order, starts = slot_order(requests, store_count)
-        return collect_tiles(order, starts, exchange(returning), store_count), field
+        return collect_tiles(order, starts, swap(returning), store_count), again
 
     def relays():
-        field, factor = field_only(
-            plan,
-            raw.reshape(peers * blocks, rows),
-            source.reshape(5, peers * blocks, rows),
-            blocks,
-        )
-        land = return_tiles(plan, factor, basis)
         return collect_planned(plan, land, store_count), field
 
-    pieces, field = lax.cond(plan[AT_LEFT, 0] > 0, two_slots, relays)
-    return pieces, field.reshape(-1)
+    pieces, potential = lax.cond(plan[AT_LEFT, 0] > 0, two_slots, relays)
+    return pieces, potential.reshape(-1)
 
 
 def solution(mesh):

time: 253 us -> 244 us (0.964)
  Pallas kernels: 247 us -> 238 us
    pallas_call x3 -> x1, Pallas kernels: 239 us -> 230 us  [exchange(): pl.pallas_call(exchange_kernel, in_specs=[smem, smem, smem, hbm] + [vmem]...]
where the time goes in v5:
time: 244 us; the launch traced here: 242 us
  Pallas kernels  238 us (98%)
  local copies, waits for them, and re-layouts  2.56 us (1%)
    pallas_call x1, Pallas kernels, exchange(): pl.pallas_call(exchange_kernel, in_specs=[smem, smem, smem, hbm] + [vmem]...  230 us
    pallas_call x1, Pallas kernels, collect_planned(): pl.pallas_call(collect_planned_kernel, grid=(store_count // group,), in_s...  8.02 us

profile of v5, /device:TPU:1, one launch (start us, length us, event | category | flops | bytes accessed | tf_op | source)
XLA Modules:
  0.0 242.3 jit_solution(2823881982221851535)
XLA Ops:
  0.6 0.0 copy-start.8
  0.6 0.0 copy-start.9
  0.7 0.0 copy-start.1
  0.7 0.0 copy-start.2
  0.7 0.0 copy-start
  0.7 0.0 copy-start.10
  0.7 0.0 copy-start.6
  0.7 0.0 copy-start.5
  0.7 230.2 %exchange.1 = (s32[128,2,128]{2,1,0:T(2,128)S(1)}, s32[48,128]{1,0:T(8,128)S(1)}, f32[4,128]{1,0:T(4,128)S(1)}, bf16[357,128,128]{2,1,0:T(8,128)(2,1)}) custom-call(s32[8192]{0:T(1024)} %home.1, s32[4,32]{1,0:T(4,128)} %pair_tiles.1, s32[4,32]{1,0:T(4,128)} %pair_pos.1, s32[512,512]{1,0:T(8,128)} %pair_keep.1, f32[4,128]{1,0:T(4,128)} %bitcast.28, ...), custom_call_target="tpu_custom_call" | custom-call | tf_op jit(solution)/shard_map/exchange/pallas_call | solution.py:695
  231.0 0.5 slice.12
  232.1 0.0 copy-done.8
  232.2 0.0 copy-done.9
  232.2 0.0 copy-done.1
  232.2 0.0 copy-done.2
  232.2 0.0 copy-done
  232.2 0.0 copy-done.10
  232.2 0.0 copy-done.6
  232.2 0.0 copy-done.5
  232.2 8.0 %conditional.1 = (f32[64,128,128]{2,1,0:T(8,128)S(1)}, f32[4,128]{1,0:T(4,128)S(1)}) conditional(s32[]{:T(128)} %bitcast.13, (s32[48,128]{1,0:T(8,128)S(1)}, bf16[357,128,128]{2,1,0:T(8,128)(2,1)}, f32[4,128]{1,0:T(4,128)S(1)}) %tuple.16, (s32[128,2,128]{2,1,0:T(2,128)S(1)}, s32[]{:T(128)}, s32[512,512]{1,0:T(8,128)}, s32[4,32]{1,0:T(4,128)S(1)}, ...), branch_computations={%region_0.0_spmd, %region_1.10_spmd} | conditional | flops 5013757 | bytes 60748672 | solution.py:1078
  232.2 8.0 %collect_planned.1 = f32[64,128,128]{2,1,0:T(8,128)S(1)} custom-call(s32[48,128]{1,0:T(8,128)S(1)} %get-tuple-element.28.plan, bf16[357,128,128]{2,1,0:T(8,128)(2,1)} %get-tuple-element.29.landed), custom_call_target="tpu_custom_call" | custom-call | tf_op jit(solution)/shard_map/cond/branch_0_fun/collect_planned/pallas_call | solution.py:977
  240.3 0.0 copy-start.3
  240.3 0.6 copy.27
  240.9 1.4 copy-done.3
Async XLA Ops:
  0.6 231.5 %copy-start.8 = (f32[512]{0:T(512)S(1)}, f32[512]{0:T(512)}, u32[]{:S(2)}) copy-start(f32[512]{0:T(512)} %param.17) | copy-start | bytes 6148
  0.6 231.5 %copy-start.9 = (f32[512]{0:T(512)S(1)}, f32[512]{0:T(512)}, u32[]{:S(2)}) copy-start(f32[512]{0:T(512)} %param.18) | copy-start | bytes 6148
  0.7 231.5 %copy-start.1 = (bf16[512,1024]{1,0:T(8,128)(2,1)S(1)}, bf16[512,1024]{1,0:T(8,128)(2,1)}, u32[]{:S(2)}) copy-start(bf16[512,1024]{1,0:T(8,128)(2,1)} %basis.1) | copy-start | bytes 3145732
  0.7 231.5 %copy-start.2 = (bf16[64,128,128]{2,1,0:T(8,128)(2,1)S(1)}, bf16[64,128,128]{2,1,0:T(8,128)(2,1)}, u32[]{:S(2)}) copy-start(bf16[64,128,128]{2,1,0:T(8,128)(2,1)} %tiles.1) | copy-start | bytes 6291460
  0.7 231.5 %copy-start = (s32[8192]{0:T(1024)S(1)}, s32[8192]{0:T(1024)}, u32[]{:S(2)}) copy-start(s32[8192]{0:T(1024)} %home.1) | copy-start | bytes 98308
  0.7 231.5 %copy-start.10 = (s32[4,32]{1,0:T(4,128)S(1)}, s32[4,32]{1,0:T(4,128)}, u32[]{:S(2)}) copy-start(s32[4,32]{1,0:T(4,128)} %pair_tiles.1) | copy-start | bytes 1540
  0.7 231.5 %copy-start.6 = (s32[4,32]{1,0:T(4,128)S(1)}, s32[4,32]{1,0:T(4,128)}, u32[]{:S(2)}) copy-start(s32[4,32]{1,0:T(4,128)} %pair_pos.1) | copy-start | bytes 1540
  0.7 231.5 %copy-start.5 = (f32[3,512]{1,0:T(4,128)S(1)}, f32[3,512]{1,0:T(4,128)}, u32[]{:S(2)}) copy-start(f32[3,512]{1,0:T(4,128)} %coords.1) | copy-start | bytes 18436
  240.3 2.0 copy-start.3

commit v6 on v5

--- a/solution.py
+++ b/solution.py
@@ -114,15 +114,40 @@
     return jnp.sum(jnp.where(hit, column, 0.0), axis=0, keepdims=True)
 
 
-def make_requests(want, asking):
-    peers = want.shape[1]
+def one_column(values):
+    blocks, pairs = values.shape
+    wide = jnp.concatenate(
+        [jnp.broadcast_to(values[b : b + 1, :], (pairs, pairs)) for b in range(blocks)], axis=0
+    ).astype(jnp.float32)
+    sub = lax.broadcasted_iota(jnp.int32, wide.shape, 0) % pairs
+    lane = lax.broadcasted_iota(jnp.int32, wide.shape, 1)
+    return jnp.sum(jnp.where(sub == lane, wide, 0.0), axis=1, keepdims=True)
+
+
+def find_owners(home, pair_tiles):
+    named = one_column(pair_tiles).astype(jnp.int32)
+    peers, groups = named.shape[0], home.shape[0]
     sub, lane = iotas(peers)
-    owner_int = want[0:1, :] // 64
-    owner = owner_int.astype(jnp.float32)
-    within = (want[0:1, :] - owner_int * 64).astype(jnp.float32)
-    owner_down = down(owner, peers)
-    same = owner_down == owner
-    rank = across(same & (sub < lane), jnp.ones_like(owner_down))
+    group = lax.broadcasted_iota(jnp.int32, (peers, groups), 1)
+    pick = jnp.where(group == named // peers, 1.0, 0.0).astype(jnp.bfloat16)
+    rest = (named % peers).astype(jnp.float32)
+
+    def look(table):
+        found = jnp.dot(
+            pick, table.astype(jnp.float32).astype(jnp.bfloat16), preferred_element_type=jnp.float32
+        )
+        return jnp.sum(jnp.where(lane == rest, found, 0.0), axis=1, keepdims=True)
+
+    device = home // 64
+    return look(device), look(home - device * 64)
+
+
+def make_requests(owner_down, within_down, asking):
+    peers = owner_down.shape[0]
+    sub, lane = iotas(peers)
+    owner = across(sub == lane, owner_down)
+    within = across(sub == lane, within_down)
+    rank = across((owner_down == owner) & (sub < lane), jnp.ones_like(owner_down))
     columns = [
         jnp.sum(
             jnp.where((owner == sub) & (rank == slot), within + 1.0, 0.0), axis=1, keepdims=True
@@ -135,19 +160,20 @@
     asking[:, 1, :] = jnp.broadcast_to(named, (peers, peers)).astype(jnp.int32)
 
 
-def make_tables(want, plan):
-    peers = want.shape[1]
+def make_tables(owner_down, spots_down, plan):
+    peers = owner_down.shape[0]
     sub, lane = iotas(peers)
     me = this_device()
-    owner_int = want[0:1, :] // 64
-    owner = owner_int.astype(jnp.float32)
-    owner_down = down(owner, peers)
-    rank = across((owner_down == owner) & (sub < lane), jnp.ones_like(owner_down))
-    odd = parity(owner_int) != parity(me)
-    found = jnp.where((rank == 1.0) & odd, 4.0 * peers + owner, 2.0 * owner + rank)
-    pair = lax.broadcasted_iota(jnp.int32, (1, peers), 1)
-    spot = (want[1:2, :] + 64 * (pair // 32)).astype(jnp.float32)
-    rank_down, found_down, spot_down = down(rank, peers), down(found, peers), down(spot, peers)
+    owner = across(sub == lane, owner_down)
+    rank_down = jnp.sum(
+        jnp.where((owner_down == owner) & (lane < sub), 1.0, 0.0), axis=1, keepdims=True
+    )
+    odd = parity(owner_down.astype(jnp.int32)) != parity(me)
+    found_down = jnp.where(
+        (rank_down == 1.0) & odd, 4.0 * peers + owner_down, 2.0 * owner_down + rank_down
+    )
+    pair = lax.broadcasted_iota(jnp.int32, (peers, 1), 0)
+    spot_down = spots_down + (64 * (pair // 32)).astype(jnp.float32)
     for half in range(2):
         row = across(spot_down == lane + half * peers, found_down - 2.0 * peers) + 2.0 * peers
         plan[AT_TABLE + half : AT_TABLE + half + 1, :] = row.astype(jnp.int32)
@@ -315,16 +341,17 @@
     weights,
     grad_sq,
     coords,
-    tiles,
-    basis,
+    tiles_far,
+    basis_far,
     asked,
     plan,
     field,
     land,
     wanted,
     route,
-    want_smem,
-    want,
+    tiles,
+    basis,
+    wanted_rows,
     asking,
     keep,
     local,
@@ -407,7 +434,7 @@
         return remote(part, part, raw_send, raw_recv, up, neighbour(2 * up))
 
     def tile_for(device, slot):
-        return tiles[inside(wanted[inside(device, peers), 0, slot] - 1, tiles.shape[0])]
+        return tiles[inside(wanted[slot, inside(device, peers)] - 1, tiles.shape[0])]
 
     def second_for(device):
         at = route[AT_CODE, device]
@@ -419,17 +446,11 @@
         return copy
 
     greet_all(peers)
+    tiles_copy = move(tiles_far, tiles, 1)
+    basis_copy = move(basis_far, basis, 2)
     keep_copy = move(pair_keep, keep, 0)
-
-    for b in range(blocks):
-
-        @pl.loop(0, pairs)
-        def _(j):
-            want_smem[0, b * pairs + j] = home[inside(pair_tiles[b, j], home.shape[0])]
-            want_smem[1, b * pairs + j] = pair_pos[b, j]
-
-    move(want_smem, want, 1).wait()
-    make_requests(want, asking)
+    owner_down, within_down = find_owners(home[...], pair_tiles[...])
+    make_requests(owner_down, within_down, asking)
     local[0] = weights[...]
     local[1] = grad_sq[...]
     for axis in range(3):
@@ -453,7 +474,13 @@
     def _(step):
         ask(step).wait()
 
-    move(asked, wanted, 2).wait()
+    entries = asked[:, 0, :].astype(jnp.float32)
+    sub, lane = iotas(peers)
+    for slot in range(2):
+        column_of = jnp.sum(jnp.where(lane == slot, entries, 0.0), axis=1, keepdims=True)
+        wanted_rows[slot : slot + 1, :] = across(sub == lane, column_of).astype(jnp.int32)
+    move(wanted_rows, wanted, 7).wait()
+    tiles_copy.wait()
 
     @pl.loop(0, 64)
     def _(turn):
@@ -499,9 +526,10 @@
         share(up).wait()
 
     share_on().start()
-    make_tables(want, plan)
+    make_tables(owner_down, one_column(pair_pos[...]), plan)
     make_order(asked[:, 0, :].astype(jnp.float32), again, plan)
     keep_copy.wait()
+    basis_copy.wait()
     mine = keep[pl.ds(pl.multiple_of(8 * chip, 8), 8), :]
     make_kept(jnp.where(core == 0, mine[0:4, :], mine[4:8, :]).astype(jnp.float32), plan)
     unplaced = unplaced + jnp.where(most_kept(keep) > ENTRIES, 1.0, 0.0)
@@ -694,7 +722,7 @@
     links = pltpu.SemaphoreType.DMA((LINKS,))
     return pl.pallas_call(
         exchange_kernel,
-        in_specs=[smem, smem, smem, hbm] + [vmem] * 5,
+        in_specs=[vmem, vmem, vmem, hbm, vmem, vmem, vmem, hbm, hbm],
         out_specs=[vmem, vmem, vmem, hbm],
         out_shape=[
             jax.ShapeDtypeStruct((peers, 2, peers), jnp.int32),
@@ -703,9 +731,10 @@
             jax.ShapeDtypeStruct((2 * peers + RELAYED, tile, tile), tiles.dtype),
         ],
         scratch_shapes=[
-            pltpu.SMEM((peers, 2, peers), jnp.int32),
+            pltpu.SMEM((2, peers), jnp.int32),
             pltpu.SMEM((PLAN_ROWS, peers), jnp.int32),
-            pltpu.SMEM((2, peers), jnp.int32),
+            pltpu.VMEM(tiles.shape, tiles.dtype),
+            pltpu.VMEM(basis.shape, basis.dtype),
             pltpu.VMEM((2, peers), jnp.int32),
             pltpu.VMEM((peers, 2, peers), jnp.int32),
             pltpu.VMEM(pair_keep.shape, jnp.int32),
@@ -723,7 +752,7 @@
             pltpu.VMEM((RELAYED, tile, tile), tiles.dtype),
             pltpu.VMEM((RELAYED, tile, tile), tiles.dtype),
             pltpu.VMEM((2, orbs, orbs), basis.dtype),
-            pltpu.SemaphoreType.DMA((7,)),
+            pltpu.SemaphoreType.DMA((8,)),
         ]
         + [pair] * 6
         + [links] * 2
@@ -1021,7 +1050,7 @@
     capacity = 2
     slot_count = peers * capacity
     asked, plan, field, land = exchange(
-        tile_home,
+        tile_home.reshape(-1, tile),
         pair_tiles,
         pair_pos,
         pair_keep,

time: 244 us -> 232 us (0.951)
  Pallas kernels: 238 us -> 228 us
    pallas_call x1, Pallas kernels: 230 us -> 220 us  [exchange(): pl.pallas_call(exchange_kernel, in_specs=[vmem, vmem, vmem, hbm, vmem, vm...]
where the time goes in v6:
time: 232 us
  Pallas kernels  228 us (98%)
  local copies, waits for them, and re-layouts  2.56 us (1%)
    pallas_call x1, Pallas kernels, exchange(): pl.pallas_call(exchange_kernel, in_specs=[vmem, vmem, vmem, hbm, vmem, vm...  220 us
    pallas_call x1, Pallas kernels, collect_planned(): pl.pallas_call(collect_planned_kernel, grid=(store_count // group,), in_s...  7.98 us

profile of v6, /device:TPU:1, one launch (start us, length us, event | category | flops | bytes accessed | tf_op | source)
XLA Modules:
  0.0 232.0 jit_solution(7225935394963637750)
XLA Ops:
  0.6 0.0 copy-start
  0.6 0.0 copy-start.8
  0.7 0.0 copy-start.9
  0.7 0.0 copy-start.1
  0.7 0.0 copy-start.2
  0.7 0.0 copy-start.10
  0.7 0.0 copy-start.6
  0.7 0.0 copy-start.5
  0.7 220.0 %exchange.1 = (s32[128,2,128]{2,1,0:T(2,128)S(1)}, s32[48,128]{1,0:T(8,128)S(1)}, f32[4,128]{1,0:T(4,128)S(1)}, bf16[357,128,128]{2,1,0:T(8,128)(2,1)}) custom-call(s32[64,128]{1,0:T(8,128)} %bitcast.26, s32[4,32]{1,0:T(4,128)} %pair_tiles.1, s32[4,32]{1,0:T(4,128)} %pair_pos.1, s32[512,512]{1,0:T(8,128)} %pair_keep.1, f32[4,128]{1,0:T(4,128)} %bitcast.30, ...), custom_call_target="tpu_custom_call" | custom-call | tf_op jit(solution)/shard_map/exchange/pallas_call | solution.py:723
  220.7 0.5 slice.12
  221.9 0.0 copy-done
  221.9 0.0 copy-done.8
  221.9 0.0 copy-done.9
  221.9 0.0 copy-done.1
  221.9 0.0 copy-done.2
  221.9 0.0 copy-done.10
  221.9 0.0 copy-done.6
  221.9 0.0 copy-done.5
  222.0 8.0 %conditional.1 = (f32[64,128,128]{2,1,0:T(8,128)S(1)}, f32[4,128]{1,0:T(4,128)S(1)}) conditional(s32[]{:T(128)} %bitcast.14, (s32[48,128]{1,0:T(8,128)S(1)}, bf16[357,128,128]{2,1,0:T(8,128)(2,1)}, f32[4,128]{1,0:T(4,128)S(1)}) %tuple.16, (s32[128,2,128]{2,1,0:T(2,128)S(1)}, s32[]{:T(128)}, s32[512,512]{1,0:T(8,128)}, s32[4,32]{1,0:T(4,128)S(1)}, ...), branch_computations={%region_0.0_spmd, %region_1.10_spmd} | conditional | flops 5013757 | bytes 60748672 | solution.py:1107
  222.0 8.0 %collect_planned.1 = f32[64,128,128]{2,1,0:T(8,128)S(1)} custom-call(s32[48,128]{1,0:T(8,128)S(1)} %get-tuple-element.28.plan, bf16[357,128,128]{2,1,0:T(8,128)(2,1)} %get-tuple-element.29.landed), custom_call_target="tpu_custom_call" | custom-call | tf_op jit(solution)/shard_map/cond/branch_0_fun/collect_planned/pallas_call | solution.py:1006
  230.0 0.0 copy-start.3
  230.0 0.6 copy.27
  230.6 1.4 copy-done.3
Async XLA Ops:
  0.6 221.2 %copy-start = (s32[8192]{0:T(1024)S(1)}, s32[8192]{0:T(1024)}, u32[]{:S(2)}) copy-start(s32[8192]{0:T(1024)} %param.13) | copy-start | bytes 98308
  0.6 221.2 %copy-start.8 = (f32[512]{0:T(512)S(1)}, f32[512]{0:T(512)}, u32[]{:S(2)}) copy-start(f32[512]{0:T(512)} %param.17) | copy-start | bytes 6148
  0.7 221.2 %copy-start.9 = (f32[512]{0:T(512)S(1)}, f32[512]{0:T(512)}, u32[]{:S(2)}) copy-start(f32[512]{0:T(512)} %param.18) | copy-start | bytes 6148
  0.7 221.2 %copy-start.1 = (bf16[512,1024]{1,0:T(8,128)(2,1)S(1)}, bf16[512,1024]{1,0:T(8,128)(2,1)}, u32[]{:S(2)}) copy-start(bf16[512,1024]{1,0:T(8,128)(2,1)} %basis_far.1) | copy-start | bytes 3145732
  0.7 221.2 %copy-start.2 = (bf16[64,128,128]{2,1,0:T(8,128)(2,1)S(1)}, bf16[64,128,128]{2,1,0:T(8,128)(2,1)}, u32[]{:S(2)}) copy-start(bf16[64,128,128]{2,1,0:T(8,128)(2,1)} %tiles_far.1) | copy-start | bytes 6291460
  0.7 221.2 %copy-start.10 = (s32[4,32]{1,0:T(4,128)S(1)}, s32[4,32]{1,0:T(4,128)}, u32[]{:S(2)}) copy-start(s32[4,32]{1,0:T(4,128)} %pair_tiles.1) | copy-start | bytes 1540
  0.7 221.2 %copy-start.6 = (s32[4,32]{1,0:T(4,128)S(1)}, s32[4,32]{1,0:T(4,128)}, u32[]{:S(2)}) copy-start(s32[4,32]{1,0:T(4,128)} %pair_pos.1) | copy-start | bytes 1540
  0.7 221.2 %copy-start.5 = (f32[3,512]{1,0:T(4,128)S(1)}, f32[3,512]{1,0:T(4,128)}, u32[]{:S(2)}) copy-start(f32[3,512]{1,0:T(4,128)} %coords.1) | copy-start | bytes 18436
  230.0 2.0 copy-start.3

commit v7 on v6

--- a/solution.py
+++ b/solution.py
@@ -32,7 +32,7 @@
     (1, 0, 3, 1),
     (1, 3, 0, 1),
 )
-ROOM = (56, 8, 8, 8, 4, 4, 4) + (1,) * 9
+ROOM = (48, 6, 6, 6, 4, 4, 4) + (1,) * 9
 BASE = tuple(sum(ROOM[:k]) for k in range(len(ROOM)))
 LINKS = len(ROOM)
 RELAYED = sum(ROOM)
@@ -51,8 +51,8 @@
     return density, omega_zero, kappa_point
 
 
-def params(**more):
-    return pltpu.CompilerParams(vmem_limit_bytes=VMEM_LIMIT, **more)
+def params(limit=VMEM_LIMIT, **more):
+    return pltpu.CompilerParams(vmem_limit_bytes=limit, **more)
 
 
 def moved(device, move):
@@ -974,45 +974,57 @@
         in_specs=[smem, smem, pl.BlockSpec(memory_space=pltpu.VMEM)],
         out_specs=pl.BlockSpec((group, tile, tile), lambda i: (i, 0, 0)),
         out_shape=jax.ShapeDtypeStruct((store_count, tile, tile), jnp.float32),
-        compiler_params=params(),
+        compiler_params=params(limit=61 * 2**20),
         name="collect_tiles",
     )(order, starts, landed)
 
 
-def collect_planned_kernel(plan, landed, out):
-    step = pl.program_id(0)
-    width = out.shape[0]
+def collect_planned_kernel(plan, landed, out, sums, sems):
+    count = sums.shape[0]
+    group = 8
     peers = plan.shape[1]
 
-    @pl.loop(0, width)
-    def _(t):
-        g = step * width + t
-
-        def add(j, total):
-            place = plan[AT_ORDER + j // peers, lax.rem(j, peers)]
-            return total + landed[place].astype(jnp.float32)
-
-        out[t] = lax.fori_loop(
-            plan[AT_STARTS, g],
-            plan[AT_STARTS, g + 1],
-            add,
-            jnp.zeros(out.shape[1:], jnp.float32),
-        )
+    def write(g):
+        part = pl.ds(pl.multiple_of(g * group, group), group)
+        return pltpu.make_async_copy(sums.at[part], out.at[part], sems.at[g])
+
+    @pl.loop(0, count // group)
+    def _(g):
+        for t in range(group):
+            at = g * group + t
+
+            def add(j, total):
+                place = plan[AT_ORDER + j // peers, lax.rem(j, peers)]
+                return total + landed[place].astype(jnp.float32)
+
+            sums[at] = lax.fori_loop(
+                plan[AT_STARTS, at],
+                plan[AT_STARTS, at + 1],
+                add,
+                jnp.zeros(sums.shape[1:], jnp.float32),
+            )
+        write(g).start()
+
+    @pl.loop(0, count // group)
+    def _(g):
+        write(g).wait()
 
 
 def collect_planned(plan, landed, store_count):
     tile = landed.shape[1]
-    group = 8
     return pl.pallas_call(
         collect_planned_kernel,
-        grid=(store_count // group,),
         in_specs=[
             pl.BlockSpec(memory_space=pltpu.SMEM),
             pl.BlockSpec(memory_space=pltpu.VMEM),
         ],
-        out_specs=pl.BlockSpec((group, tile, tile), lambda i: (i, 0, 0)),
+        out_specs=pl.BlockSpec(memory_space=pl.ANY),
         out_shape=jax.ShapeDtypeStruct((store_count, tile, tile), jnp.float32),
-        compiler_params=params(),
+        scratch_shapes=[
+            pltpu.VMEM((store_count, tile, tile), jnp.float32),
+            pltpu.SemaphoreType.DMA((store_count // 8,)),
+        ],
+        compiler_params=params(limit=61 * 2**20),
         name="collect_planned",
     )(plan, landed)
 

time: 232 us -> 228 us (0.983)
    pallas_call x1, Pallas kernels: 220 us -> 217 us  [exchange(): pl.pallas_call(exchange_kernel, in_specs=[vmem, vmem, vmem, hbm, vmem, vm...]
where the time goes in v7:
time: 228 us
  Pallas kernels  226 us (99%)
    pallas_call x1, Pallas kernels, exchange(): pl.pallas_call(exchange_kernel, in_specs=[vmem, vmem, vmem, hbm, vmem, vm...  217 us
    pallas_call x1, Pallas kernels, collect_planned(): pl.pallas_call(collect_planned_kernel, in_specs=[pl.BlockSpec(memory_spac...  8.51 us

profile of v7, /device:TPU:1, one launch (start us, length us, event | category | flops | bytes accessed | tf_op | source)
XLA Modules:
  0.0 228.2 jit_solution(7538295067963933328)
XLA Ops:
  0.6 0.0 copy-start
  0.6 0.0 copy-start.6
  0.7 0.0 copy-start.7
  0.7 0.0 copy-start.1
  0.7 0.0 copy-start.8
  0.7 0.0 copy-start.4
  0.7 0.0 copy-start.3
  0.7 217.1 %exchange.1 = (s32[128,2,128]{2,1,0:T(2,128)S(1)}, s32[48,128]{1,0:T(8,128)S(1)}, f32[4,128]{1,0:T(4,128)S(1)}, bf16[343,128,128]{2,1,0:T(8,128)(2,1)}) custom-call(s32[64,128]{1,0:T(8,128)} %bitcast.26, s32[4,32]{1,0:T(4,128)} %pair_tiles.1, s32[4,32]{1,0:T(4,128)} %pair_pos.1, s32[512,512]{1,0:T(8,128)} %pair_keep.1, f32[4,128]{1,0:T(4,128)} %bitcast.30, ...), custom_call_target="tpu_custom_call" | custom-call | tf_op jit(solution)/shard_map/exchange/pallas_call | solution.py:723
  217.8 0.5 slice.12
  219.0 0.0 copy-done
  219.0 0.0 copy-done.6
  219.0 0.0 copy-done.7
  219.0 0.0 copy-done.1
  219.0 0.0 copy-done.8
  219.0 0.0 copy-done.4
  219.0 0.0 copy-done.3
  219.1 8.5 %conditional.1 = (f32[64,128,128]{2,1,0:T(8,128)}, f32[4,128]{1,0:T(4,128)S(1)}) conditional(s32[]{:T(128)} %bitcast.14, (s32[48,128]{1,0:T(8,128)S(1)}, bf16[343,128,128]{2,1,0:T(8,128)(2,1)}, f32[4,128]{1,0:T(4,128)S(1)}) %tuple.16, (s32[128,2,128]{2,1,0:T(2,128)S(1)}, s32[]{:T(128)}, s32[512,512]{1,0:T(8,128)}, s32[4,32]{1,0:T(4,128)S(1)}, ...), branch_computations={%region_0.0_spmd, %region_1.10_spmd} | conditional | flops 5013757 | bytes 60748672 | solution.py:1119
  219.1 8.5 %collect_planned.1 = f32[64,128,128]{2,1,0:T(8,128)} custom-call(s32[48,128]{1,0:T(8,128)S(1)} %get-tuple-element.28.plan, bf16[343,128,128]{2,1,0:T(8,128)(2,1)} %get-tuple-element.29.landed), custom_call_target="tpu_custom_call" | custom-call | tf_op jit(solution)/shard_map/cond/branch_0_fun/collect_planned/pallas_call | solution.py:1015
  227.6 0.6 copy.27
Async XLA Ops:
  0.6 218.4 %copy-start = (s32[8192]{0:T(1024)S(1)}, s32[8192]{0:T(1024)}, u32[]{:S(2)}) copy-start(s32[8192]{0:T(1024)} %param.13) | copy-start | bytes 98308
  0.6 218.4 %copy-start.6 = (f32[512]{0:T(512)S(1)}, f32[512]{0:T(512)}, u32[]{:S(2)}) copy-start(f32[512]{0:T(512)} %param.17) | copy-start | bytes 6148
  0.7 218.4 %copy-start.7 = (f32[512]{0:T(512)S(1)}, f32[512]{0:T(512)}, u32[]{:S(2)}) copy-start(f32[512]{0:T(512)} %param.18) | copy-start | bytes 6148
  0.7 218.4 %copy-start.1 = (bf16[512,1024]{1,0:T(8,128)(2,1)S(1)}, bf16[512,1024]{1,0:T(8,128)(2,1)}, u32[]{:S(2)}) copy-start(bf16[512,1024]{1,0:T(8,128)(2,1)} %basis_far.1) | copy-start | bytes 3145732
  0.7 218.4 %copy-start.8 = (s32[4,32]{1,0:T(4,128)S(1)}, s32[4,32]{1,0:T(4,128)}, u32[]{:S(2)}) copy-start(s32[4,32]{1,0:T(4,128)} %pair_tiles.1) | copy-start | bytes 1540
  0.7 218.4 %copy-start.4 = (s32[4,32]{1,0:T(4,128)S(1)}, s32[4,32]{1,0:T(4,128)}, u32[]{:S(2)}) copy-start(s32[4,32]{1,0:T(4,128)} %pair_pos.1) | copy-start | bytes 1540
  0.7 218.4 %copy-start.3 = (f32[3,512]{1,0:T(4,128)S(1)}, f32[3,512]{1,0:T(4,128)}, u32[]{:S(2)}) copy-start(f32[3,512]{1,0:T(4,128)} %coords.1) | copy-start | bytes 18436
